TPU v7x, 128 devices: a whole 4x4x4 slice. The times are simulated.
128 devices in a mesh: seq: 64 (over y_lo, x, z, core), chan: 2 (over y_hi).
Axes of the slice: x: 4, y: 4 (y_hi: 2, y_lo: 2; y = y_hi * 2 + y_lo), z: 4, core: 2. Of those that a mesh axis runs over, the one named last changes fastest.
Arguments:
- tokens: bfloat16 [24576, 1024], P('seq'), may hold values from -6 to 6
- cotangent: bfloat16 [24576, 1024], P('seq'), may hold values from -16 to 16
- w_in: float32 [1024, 3, 1024], P('seq', None, 'chan'), may hold values from -0.1875 to 0.1875
- w_in_m: float32 [1024, 3, 1024], P('seq', None, 'chan'), may hold values from -1000 to 1000, as said below
- w_in_v: float32 [1024, 3, 1024], P('seq', None, 'chan'), may hold values from 1228.8 to 4915.2
- w_out: float32 [1024, 1024], P('seq', 'chan'), may hold values from -0.1875 to 0.1875
- w_out_m: float32 [1024, 1024], P('seq', 'chan'), may hold values from -1000 to 1000, as said below
- w_out_v: float32 [1024, 1024], P('seq', 'chan'), may hold values from 1228.8 to 4915.2
- w_gu: float32 [1024, 2, 4608], P('seq', None, 'chan'), may hold values from -0.1875 to 0.1875
- w_gu_m: float32 [1024, 2, 4608], P('seq', None, 'chan'), may hold values from -1000 to 1000, as said below
- w_gu_v: float32 [1024, 2, 4608], P('seq', None, 'chan'), may hold values from 122.88 to 491.52
- w_down: float32 [1024, 4608], P('seq', 'chan'), may hold values from -0.09375 to 0.09375
- w_down_m: float32 [1024, 4608], P('seq', 'chan'), may hold values from -1000 to 1000, as said below
- w_down_v: float32 [1024, 4608], P('seq', 'chan'), may hold values from 491.52 to 1966.08
- vectors: float32 [5, 1024], P(None, ('seq', 'chan')), may hold values from -1.5 to 1.5, as said below
- vectors_m: float32 [5, 1024], P(None, ('seq', 'chan')), may hold values from -1000 to 1000, as said below
- vectors_v: float32 [5, 1024], P(None, ('seq', 'chan')), may hold values from 2457.6 to 9830.4
Outputs:
- block_out: float32 [24576, 1024], P('seq')
- input_grad: float32 [24576, 1024], P('seq')
- w_in_new: float32 [1024, 3, 1024], P('seq', None, 'chan')
- w_in_m_new: float32 [1024, 3, 1024], P('seq', None, 'chan')
- w_in_v_new: float32 [1024, 3, 1024], P('seq', None, 'chan')
- w_out_new: float32 [1024, 1024], P('seq', 'chan')
- w_out_m_new: float32 [1024, 1024], P('seq', 'chan')
- w_out_v_new: float32 [1024, 1024], P('seq', 'chan')
- w_gu_new: float32 [1024, 2, 4608], P('seq', None, 'chan')
- w_gu_m_new: float32 [1024, 2, 4608], P('seq', None, 'chan')
- w_gu_v_new: float32 [1024, 2, 4608], P('seq', None, 'chan')
- w_down_new: float32 [1024, 4608], P('seq', 'chan')
- w_down_m_new: float32 [1024, 4608], P('seq', 'chan')
- w_down_v_new: float32 [1024, 4608], P('seq', 'chan')
- vectors_new: float32 [5, 1024], P(None, ('seq', 'chan'))
- vectors_m_new: float32 [5, 1024], P(None, ('seq', 'chan'))
- vectors_v_new: float32 [5, 1024], P(None, ('seq', 'chan'))
Inputs may be any that keep to these rules, and one draw needn't show every extreme that they name: `vectors`: rows 0 and 1 lie within 0.83 to 1.17, rows 2 to 4 within -1.5 to 1.5. `w_in_m`: both signs. `w_out_m`: both signs. `w_gu_m`: both signs. `w_down_m`: both signs. `vectors_m`: both signs.
All inputs are finite; a program needn't handle non-finite values.
Results may differ from a plain program's by a relative error of at most 0.011.
Values may be sent and summed in bfloat16 or wider, within the bound.
A program may use at most 256 MiB of HBM per device.

v0:
```python
import math

import jax
import jax.numpy as jnp
from jax import lax
from jax.sharding import PartitionSpec as P

STEP = 10


norm_eps = 1e-05
beta_one = 0.9
beta_two = 0.95
adam_eps = 1e-08
rate_matrix = 0.05
rate_vector = 0.5
decay_matrix = 0.1


def side_by_side(arrays, axis, dim, along):
    columns = [a.reshape(*a.shape[:along], -1) for a in arrays]
    both = jnp.concatenate(columns, axis=along)
    out, at, finished = (lax.all_gather(both, axis, axis=dim, tiled=True), 0, [])
    for a, column in zip(arrays, columns):
        section = out[..., at : at + column.shape[along]]
        finished.append(section.reshape(*section.shape[:along], *a.shape[along:]))
        at += column.shape[along]
    return tuple(finished)


def shifted(block, axis, distance):
    devices = range(lax.axis_size(axis))
    route = [(i - distance, i) for i in devices if i - distance in devices]
    return lax.ppermute(block, axis, route)


def copy_for_each(x, axis):
    peers = lax.axis_size(axis)
    return lax.all_to_all(jnp.broadcast_to(x[None], (peers, *x.shape)), axis, 0, 0, tiled=True)


def of_everyone(x, axis):
    everything = copy_for_each(x, axis)
    return jnp.sum(everything, axis=0)


def taken_together(x, axis):
    everything = copy_for_each(x, axis)
    return jnp.sum(everything.astype(jnp.float32), axis=0)


def sent_together(arrays, axis, dim, along):
    widths = [math.prod(a.shape[along:]) for a in arrays]
    both = jnp.concatenate(
        [a.reshape(*a.shape[:along], w) for a, w in zip(arrays, widths)], axis=along
    )
    out = lax.psum_scatter(both, axis, scatter_dimension=dim, tiled=True)
    pieces = jnp.split(out, [sum(widths[:k]) for k in range(1, len(widths))], axis=along)
    return tuple((b.reshape(*out.shape[:along], *a.shape[along:]) for a, b in zip(arrays, pieces)))


def rms_norm(values, gain_vector):
    inverse = lax.rsqrt(jnp.mean(values * values, axis=-1, keepdims=True) + norm_eps)
    return values * inverse * gain_vector


def swiglu(gate_up):
    return jax.nn.silu(gate_up[:, 0]) * gate_up[:, 1]


def adam_update(weight, moment_one, second, gradient, step_rate, weight_decay):
    first_new = beta_one * moment_one + (1.0 - beta_one) * gradient
    second_new = beta_two * second + (1.0 - beta_two) * gradient * gradient
    first_hat = first_new / (1.0 - beta_one**STEP)
    second_hat = second_new / (1.0 - beta_two**STEP)
    weight_new = weight - step_rate * (
        first_hat / (jnp.sqrt(second_hat) + adam_eps) + weight_decay * weight
    )
    return (weight_new, first_new, second_new)


def body(
    tokens,
    cotangent,
    w_in,
    w_in_m,
    w_in_v,
    w_out,
    w_out_m,
    w_out_v,
    w_gu,
    w_gu_m,
    w_gu_v,
    w_down,
    w_down_m,
    w_down_v,
    vectors,
    vectors_m,
    vectors_v,
):
    seq_count = lax.axis_size("seq")
    seq_index = lax.axis_index("seq")
    chan_index = lax.axis_index("chan")
    half_seq = seq_count // 2
    half_width = w_in.shape[2]
    full_in, full_out, full_gu, full_down = side_by_side(
        (
            w_in.astype(jnp.bfloat16),
            w_out.astype(jnp.bfloat16),
            w_gu.astype(jnp.bfloat16),
            w_down.astype(jnp.bfloat16),
        ),
        "seq",
        0,
        1,
    )
    all_vectors = lax.all_gather(vectors, ("seq", "chan"), axis=1, tiled=True)
    width = all_vectors.shape[1]
    taps = lax.dynamic_slice_in_dim(all_vectors[2:5], chan_index * half_width, half_width, 1)
    inputs = tokens.astype(jnp.float32)
    normed, norm_pull = jax.vjp(rms_norm, inputs, all_vectors[0])
    normed_low = normed.astype(jnp.bfloat16)
    mixed = jnp.einsum("tk,kcj->tcj", normed_low, full_in, preferred_element_type=jnp.float32)
    gate_b = mixed[:, 0]
    gate_c = mixed[:, 1]
    values = mixed[:, 2]
    gated = (gate_b * values).astype(jnp.bfloat16)
    carried = shifted(gated[-2:], "seq", 1)
    carried = jnp.where(seq_index % half_seq == 0, jnp.zeros_like(carried), carried)
    extended = jnp.concatenate([carried, gated], axis=0).astype(jnp.float32)
    convolved = taps[0] * extended[:-2] + taps[1] * extended[1:-1] + taps[2] * extended[2:]
    gated_inner = (gate_c * convolved).astype(jnp.bfloat16)
    branch_part = jnp.einsum("tj,oj->to", gated_inner, full_out, preferred_element_type=jnp.float32)
    branch = of_everyone(branch_part, "chan")
    middle = inputs + branch
    normed_two, norm_two_pull = jax.vjp(rms_norm, middle, all_vectors[1])
    normed_two_low = normed_two.astype(jnp.bfloat16)
    gate_up = jnp.einsum("tk,kcf->tcf", normed_two_low, full_gu, preferred_element_type=jnp.float32)
    hidden_wide, hidden_pull = jax.vjp(swiglu, gate_up)
    hidden = hidden_wide.astype(jnp.bfloat16)
    feed_part = jnp.dot(hidden, full_down.T, preferred_element_type=jnp.float32)
    feed_out = taken_together(feed_part.astype(jnp.bfloat16), "chan").astype(jnp.float32)
    block_out = middle + feed_out
    back_hidden = jnp.dot(cotangent, full_down, preferred_element_type=jnp.float32)
    (back_gate_up,) = hidden_pull(back_hidden)
    back_gate_low = back_gate_up.astype(jnp.bfloat16)
    back_normed_two_part = jnp.einsum(
        "tcf,kcf->tk", back_gate_low, full_gu, preferred_element_type=jnp.float32
    )
    back_normed_two = of_everyone(back_normed_two_part, "chan")
    back_middle_norm, gain_two_grad = norm_two_pull(back_normed_two)
    back_middle = cotangent.astype(jnp.float32) + back_middle_norm
    back_branch = back_middle.astype(jnp.bfloat16)
    back_inner = jnp.dot(back_branch, full_out, preferred_element_type=jnp.float32)
    back_gate_c = back_inner * convolved
    back_conv = (back_inner * gate_c).astype(jnp.bfloat16)
    ahead = shifted(back_conv[:2], "seq", -1)
    ahead = jnp.where(seq_index % half_seq == half_seq - 1, jnp.zeros_like(ahead), ahead)
    back_extended = jnp.concatenate([back_conv, ahead], axis=0).astype(jnp.float32)
    back_gated = (
        taps[0] * back_extended[2:] + taps[1] * back_extended[1:-1] + taps[2] * back_extended[:-2]
    )
    back_conv_wide = back_conv.astype(jnp.float32)
    tap_grads = jnp.stack(
        [
            jnp.sum(back_conv_wide * extended[:-2], axis=0),
            jnp.sum(back_conv_wide * extended[1:-1], axis=0),
            jnp.sum(back_conv_wide * extended[2:], axis=0),
        ],
        axis=0,
    )
    back_mixed = jnp.stack([back_gated * values, back_gate_c, back_gated * gate_b], axis=1).astype(
        jnp.bfloat16
    )
    back_normed_part = jnp.einsum(
        "tcj,kcj->tk", back_mixed, full_in, preferred_element_type=jnp.float32
    )
    back_normed = taken_together(back_normed_part.astype(jnp.bfloat16), "chan").astype(jnp.float32)
    back_inputs_norm, gain_one_grad = norm_pull(back_normed)
    input_grad = back_middle + back_inputs_norm
    owner = jnp.arange(width, dtype=jnp.int32) // half_width == chan_index
    gain_rows = jnp.where(owner[None, :], jnp.stack([gain_one_grad, gain_two_grad], axis=0), 0.0)
    tap_rows = lax.dynamic_update_slice_in_dim(
        jnp.zeros((3, width), jnp.float32), tap_grads, chan_index * half_width, 1
    )
    vector_term = jnp.concatenate([gain_rows, tap_rows], axis=0)
    grad_vectors = lax.psum_scatter(vector_term, ("seq", "chan"), scatter_dimension=1, tiled=True)
    term_in = jnp.einsum("tk,tcj->kcj", normed_low, back_mixed, preferred_element_type=jnp.float32)
    term_out = jnp.einsum("to,tj->oj", back_branch, gated_inner, preferred_element_type=jnp.float32)
    term_gu = jnp.einsum(
        "tk,tcf->kcf", normed_two_low, back_gate_low, preferred_element_type=jnp.float32
    )
    term_down = jnp.einsum("to,tf->of", cotangent, hidden, preferred_element_type=jnp.float32)
    grad_in, grad_out, grad_gu, grad_down = sent_together(
        (term_in, term_out, term_gu, term_down), "seq", 0, 1
    )
    in_new, in_m_new, in_v_new = adam_update(
        w_in, w_in_m, w_in_v, grad_in, rate_matrix, decay_matrix
    )
    out_new, out_m_new, out_v_new = adam_update(
        w_out, w_out_m, w_out_v, grad_out, rate_matrix, decay_matrix
    )
    gu_new, gu_m_new, gu_v_new = adam_update(
        w_gu, w_gu_m, w_gu_v, grad_gu, rate_matrix, decay_matrix
    )
    down_new, down_m_new, down_v_new = adam_update(
        w_down, w_down_m, w_down_v, grad_down, rate_matrix, decay_matrix
    )
    vec_new, vec_m_new, vec_v_new = adam_update(
        vectors, vectors_m, vectors_v, grad_vectors, rate_vector, 0.0
    )
    return (
        block_out,
        input_grad,
        in_new,
        in_m_new,
        in_v_new,
        out_new,
        out_m_new,
        out_v_new,
        gu_new,
        gu_m_new,
        gu_v_new,
        down_new,
        down_m_new,
        down_v_new,
        vec_new,
        vec_m_new,
        vec_v_new,
    )


def solution(mesh):
    return jax.shard_map(
        body,
        mesh=mesh,
        in_specs=(
            P("seq", None),
            P("seq", None),
            P("seq", None, "chan"),
            P("seq", None, "chan"),
            P("seq", None, "chan"),
            P("seq", "chan"),
            P("seq", "chan"),
            P("seq", "chan"),
            P("seq", None, "chan"),
            P("seq", None, "chan"),
            P("seq", None, "chan"),
            P("seq", "chan"),
            P("seq", "chan"),
            P("seq", "chan"),
            P(None, ("seq", "chan")),
            P(None, ("seq", "chan")),
            P(None, ("seq", "chan")),
        ),
        out_specs=(
            P("seq", None),
            P("seq", None),
            P("seq", None, "chan"),
            P("seq", None, "chan"),
            P("seq", None, "chan"),
            P("seq", "chan"),
            P("seq", "chan"),
            P("seq", "chan"),
            P("seq", None, "chan"),
            P("seq", None, "chan"),
            P("seq", None, "chan"),
            P("seq", "chan"),
            P("seq", "chan"),
            P("seq", "chan"),
            P(None, ("seq", "chan")),
            P(None, ("seq", "chan")),
            P(None, ("seq", "chan")),
        ),
        check_vma=False,
    )
```

profile of v0, /device:TPU:1, one launch (start us, length us, event | category | flops | bytes accessed | tf_op | source)
XLA Modules:
  0.0 935.7 jit_solution(16986986217888383400)
XLA Ops:
  11.8 318.6 %all_gather.6 = f32[5,1024]{0,1:T(8,128)S(1)} all-gather(f32[5,8]{0,1:T(8,128)S(1)} %copy.216), channel_id=1, replica_groups=mesh['seq'=64,'chan'=2] {'seq','chan'}, dimensions={1}, use_global_device_ids=true | all-gather | bytes 20640 | tf_op jit(solution)/shard_map/all_gather | solution.py:117
  335.5 4.7 copy.254
  357.1 5.7 all-to-all-start
  362.9 7.9 slice.110
  370.8 12.6 %copy.255 = bf16[1024,4608]{0,1:T(8,128)(2,1)} copy(bf16[1024,4608]{1,0:T(8,128)(2,1)} %slice.110) | data formatting | bytes 18874368
  383.4 17.1 %all-to-all-done = f32[2,384,1024]{2,1,0:T(8,128)} async-done(((f32[2,384,1024]{2,1,0:T(8,128)}), f32[2,384,1024]{2,1,0:T(8,128)}, u32[]{:S(2)}, u32[]{:S(2)}) %all-to-all-start) | async-done | bytes 3145760 | tf_op jit(solution)/shard_map/all_to_all | solution.py:39
  405.7 6.6 fusion.45
  412.3 8.2 multiply_bitcast_fusion
  420.5 5.0 fusion.15
  426.9 4.6 all-to-all-start.1
  431.5 10.7 %convolution_bitcast_fusion.2 = f32[384,1024]{1,0:T(8,128)} fusion(bf16[1024,2,2304]{0,2,1:T(8,128)(2,1)} %bitcast.102, f32[384,1,2304]{2,0,1:T(8,128)} %get-tuple-element.120, f32[384,1,2304]{2,0,1:T(8,128)} %get-tuple-element.119), kind=kOutput, calls=%fused_computation.39 | convolution fusion | flops 3627417600 | bytes 18087936 | tf_op jit(solution)/shard_map/tcf,kcf->tk/dot_general | solution.py:147
  442.2 9.1 all-to-all-done.1
  454.8 5.2 all-to-all-start.2
  460.3 8.1 convolution_bitcast_fusion
  468.4 9.1 fusion.29
  480.6 15.2 %all-to-all-done.2 = f32[2,384,1024]{2,1,0:T(8,128)} async-done(((f32[2,384,1024]{2,1,0:T(8,128)}), f32[2,384,1024]{2,1,0:T(8,128)}, u32[]{:S(2)}, u32[]{:S(2)}) %all-to-all-start.2) | async-done | bytes 3145760 | tf_op jit(solution)/shard_map/all_to_all | solution.py:39
  508.9 5.1 collective-permute-start.1
  516.2 4.6 fusion.30
  520.8 26.7 %pad_maximum_fusion = f32[1024,8960]{0,1:T(8,128)} fusion(f32[1024,2304]{0,1:T(8,128)} %convolution_bitcast_fusion, f32[1024,4608]{0,1:T(8,128)S(1)} %bitcast.99, f32[1024,512]{0,1:T(8,128)S(1)} %fusion.37, f32[1024,1536]{0,1:T(8,128)} %bitcast.100), kind=kLoop, calls=%fused_computation | loop fusion | flops 27525120 | bytes 73400320 | tf_op jit(solution)/shard_map/concatenate | solution.py:54
  547.5 36.3 %copy.250 = f32[1024,8960]{1,0:T(8,128)} copy(f32[1024,8960]{0,1:T(8,128)} %pad_maximum_fusion) | data formatting | bytes 73400320
  589.8 3.8 all-to-all-start.3
  593.7 20.9 %all-to-all-done.3 = bf16[2,384,1024]{2,1,0:T(8,128)(2,1)S(1)} async-done(((bf16[2,384,1024]{2,1,0:T(8,128)(2,1)}), bf16[2,384,1024]{2,1,0:T(8,128)(2,1)S(1)}, u32[]{:S(2)}, u32[]{:S(2)}) %all-to-all-start.3) | async-done | bytes 1572896 | tf_op jit(solution)/shard_map/all_to_all | solution.py:39
  616.8 67.5 %all-reduce.2 = f32[5,1024]{1,0:T(8,128)S(1)} all-reduce(f32[5,1024]{1,0:T(8,128)S(1)} %pad_maximum_fusion.5), channel_id=3, replica_groups=mesh['seq'=64,'chan'=2] {'seq','chan'}, use_global_device_ids=true, to_apply=%region_14.15.clone | all-reduce | flops 5120 | bytes 40960
  688.1 231.3 %reduce-scatter.5.cloned.1.call-done = f32[16,8960]{1,0:T(8,128)} async-done(((f32[1024,8960]{1,0:T(8,128)}), f32[16,8960]{1,0:T(8,128)}) %reduce-scatter.5.cloned.1.call-update) | async-done | bytes 573456 | tf_op jit(solution)/shard_map/reduce_scatter | solution.py:57
  (190 shorter events, 75.9 us)
Async XLA Ops:
  7.2 324.6 %all-gather.2.cloned.1.call-start = ((), (), s32[]{:S(2)}) async-start(), calls=%async_computation.5 | async-start | bytes 18636800 | tf_op jit(solution)/shard_map/all_gather | solution.py:23
  10.9 320.6 %copy-start.2 = (bf16[384,1024]{1,0:T(8,128)(2,1)S(1)}, bf16[384,1024]{1,0:T(8,128)(2,1)}, u32[]{:S(2)}) copy-start(bf16[384,1024]{1,0:T(8,128)(2,1)} %param.17) | copy-start | bytes 2359300
  331.5 8.7 copy-start.27
  331.8 8.5 copy-start.34
  345.1 5.7 collective-permute-start
  357.1 43.3 %all-to-all-start = ((f32[2,384,1024]{2,1,0:T(8,128)}), f32[2,384,1024]{2,1,0:T(8,128)}, u32[]{:S(2)}, u32[]{:S(2)}) async-start(f32[2,384,1024]{2,1,0:T(8,128)} %broadcast_in_dim.26), calls=%async_computation | async-start | bytes 6291456 | tf_op jit(solution)/shard_map/all_to_all | solution.py:39
  426.9 24.5 %all-to-all-start.1 = ((bf16[2,384,1024]{2,1,0:T(8,128)(2,1)}), bf16[2,384,1024]{2,1,0:T(8,128)(2,1)}, u32[]{:S(2)}, u32[]{:S(2)}) async-start(bf16[2,384,1024]{2,1,0:T(8,128)(2,1)} %broadcast_in_dim.27), calls=%async_computation.1 | async-start | bytes 3145728 | tf_op jit(solution)/shard_map/all_to_all | solution.py:39
  454.8 41.0 %all-to-all-start.2 = ((f32[2,384,1024]{2,1,0:T(8,128)}), f32[2,384,1024]{2,1,0:T(8,128)}, u32[]{:S(2)}, u32[]{:S(2)}) async-start(f32[2,384,1024]{2,1,0:T(8,128)} %broadcast_in_dim.58), calls=%async_computation.2 | async-start | bytes 6291456 | tf_op jit(solution)/shard_map/all_to_all | solution.py:39
  460.0 459.3 %reduce-scatter.5.cloned.1.call-start = ((), (), s32[]{:S(2)}) async-start(), calls=%async_computation.6 | async-start | bytes 37273600 | tf_op jit(solution)/shard_map/reduce_scatter | solution.py:57
  460.2 8.1 copy-start.8
  460.3 8.1 copy-start.9
  460.3 8.1 copy-start.21
  460.3 8.1 copy-start.30
  501.9 18.8 %slice-start = ((s8[18874368]{0:T(1024)(128)(4,1)}), s8[4194304]{0:T(1024)(128)(4,1)S(1)}, s32[]{:S(2)}) async-start(s8[18874368]{0:T(1024)(128)(4,1)} %bitcast.97), calls=%async_computation.7 | async-start | bytes 8388608
  501.9 18.8 %slice-start.1 = ((s8[18874368]{0:T(1024)(128)(4,1)}), s8[4194304]{0:T(1024)(128)(4,1)S(1)}, s32[]{:S(2)}) async-start(s8[18874368]{0:T(1024)(128)(4,1)} %bitcast.97), calls=%async_computation.8 | async-start | bytes 8388608
  504.9 9.1 copy-start
  507.9 12.8 %slice-start.2 = ((s8[18874368]{0:T(1024)(128)(4,1)}), s8[4194304]{0:T(1024)(128)(4,1)S(1)}, s32[]{:S(2)}) async-start(s8[18874368]{0:T(1024)(128)(4,1)} %bitcast.97), calls=%async_computation.9 | async-start | bytes 8388608
  508.9 5.9 collective-permute-start.1
  589.8 24.8 %all-to-all-start.3 = ((bf16[2,384,1024]{2,1,0:T(8,128)(2,1)}), bf16[2,384,1024]{2,1,0:T(8,128)(2,1)S(1)}, u32[]{:S(2)}, u32[]{:S(2)}) async-start(bf16[2,384,1024]{2,1,0:T(8,128)(2,1)} %broadcast_in_dim.60), calls=%async_computation.3 | async-start | bytes 3145728 | tf_op jit(solution)/shard_map/all_to_all | solution.py:39
  616.1 68.3 %copy-start.45 = (f32[384]{0:T(512)S(1)}, f32[384]{0:T(512)}, u32[]{:S(2)}) copy-start(f32[384]{0:T(512)} %copy-done.44) | copy-start | bytes 4612
  616.1 68.3 %copy-start.48 = (f32[5,8]{1,0:T(8,128)S(1)}, f32[5,8]{1,0:T(8,128)}, u32[]{:S(2)}) copy-start(f32[5,8]{1,0:T(8,128)} %param.31) | copy-start | bytes 484
  616.1 68.3 %copy-start.52 = (f32[5,8]{1,0:T(8,128)S(1)}, f32[5,8]{1,0:T(8,128)}, u32[]{:S(2)}) copy-start(f32[5,8]{1,0:T(8,128)} %param.32) | copy-start | bytes 484
  616.1 68.3 %copy-start.53 = (f32[5,8]{1,0:T(8,128)S(1)}, f32[5,8]{1,0:T(8,128)}, u32[]{:S(2)}) copy-start(f32[5,8]{1,0:T(8,128)} %param.33) | copy-start | bytes 484
  616.1 69.0 %copy-start.1 = (f32[384,1024]{1,0:T(8,128)S(1)}, f32[384,1024]{1,0:T(8,128)}, u32[]{:S(2)}) copy-start(f32[384,1024]{1,0:T(8,128)} %copy-done) | copy-start | bytes 4718596
  (44 other events, 166.7 us)
Sparse Core Ops, SparseCore 0:
  11.8 128.7 all-gather.1
  583.9 335.3 reduce-scatter.4
where the time goes:
time: 945 us; the launch traced here: 936 us
  blocking collectives  386 us (41%)
  waiting for transfers between devices  297 us (31%)
  local copies, waits for them, and re-layouts  83.2 us (9%)
  matrix products  64.6 us (7%)
  other arithmetic  63.2 us (7%)
  starting transfers between devices  26.5 us (3%)
  between operations  15.2 us (2%)
    all_gather x1, blocking collectives, body(): all_vectors = lax.all_gather(vectors, ('seq', 'chan'), axis=1, tiled=True)  319 us
    reduce_scatter x1, waiting for transfers between devices, sent_together(): out = lax.psum_scatter(both, axis, scatter_dimension=dim, tiled=True)  231 us
    unnamed x1, blocking collectives  67.5 us
    all_to_all x4, waiting for transfers between devices, copy_for_each(): lax.all_to_all(jnp.broadcast_to(x[None], (peers, *x.shape)), axis, 0, 0,...  62.4 us
    unnamed x125, local copies, waits for them, and re-layouts  59.5 us
    concatenate x1, other arithmetic, sent_together(): jnp.concatenate([a.reshape(*a.shape[:along], w) for a, w in zip(arrays, w...  26.7 us
    all_to_all x4, starting transfers between devices, copy_for_each(): lax.all_to_all(jnp.broadcast_to(x[None], (peers, *x.shape)), axis, 0, 0,...  19.3 us
  transfers between devices with their start and end apart: 8, of which 6 were waited for; matrix products, arithmetic and copies ran while one was open for 7% of the time, Pallas kernels for 0%

commit v1 on v0

v1 whole, which is shorter than its diff:
```python
import functools

import jax
import jax.numpy as jnp
from jax import lax
from jax.experimental import pallas as pl
from jax.experimental.pallas import tpu as pltpu
from jax.sharding import PartitionSpec as P

STEP = 10
norm_eps = 1e-05
beta_one = 0.9
beta_two = 0.95
adam_eps = 1e-08
rate_matrix = 0.05
rate_vector = 0.5
decay_matrix = 0.1

MESH = pl.DeviceIdType.MESH
BF = jnp.bfloat16
F32 = jnp.float32

RING = 4


class Place:
    def __init__(self):
        s = lax.axis_index("seq")
        core = s % 2
        z = (s // 2) % RING
        x = (s // (2 * RING)) % RING
        y = s // (2 * RING * RING)
        self.s, self.core, self.y = s, core, y
        self.pa = x + core * (z - x)
        self.pb = z + core * (x - z)
        self.x, self.z = x, z
        step_x, step_z = 2 * RING, 2
        self.step_a = step_x + core * (step_z - step_x)
        self.step_b = step_z + core * (step_x - step_z)
        self.sibling = s + 1 - 2 * core
        self.other_y = s + (1 - 2 * y) * 2 * RING * RING

    def on_a(self, off):
        return self.s + ((self.pa + off) % RING - self.pa) * self.step_a

    def on_b(self, off):
        return self.s + ((self.pb + off) % RING - self.pb) * self.step_b

    def row(self, rr):
        return self.y + rr * (1 - 2 * self.y)

    def spot(self, rr, a, b):
        xi = a + self.core * (b - a)
        zi = b + self.core * (a - b)
        return self.row(rr), xi, zi

    def greet(self):
        barrier = pltpu.get_barrier_semaphore()
        peers = (self.sibling, self.other_y, self.on_a(1), self.on_a(3), self.on_b(1), self.on_b(3))
        for peer in peers:
            pl.semaphore_signal(barrier, inc=1, device_id={"seq": peer}, device_id_type=MESH)
        pl.semaphore_wait(barrier, len(peers))


def remote(src, dst, send_sem, recv_sem, target):
    return pltpu.make_async_remote_copy(
        src_ref=src,
        dst_ref=dst,
        send_sem=send_sem,
        recv_sem=recv_sem,
        device_id={"seq": target},
        device_id_type=MESH,
    )


def gather_kernel(w_ref, g_ref, local_sem, first_sem, send, recv, sib_recv):
    me = Place()
    me.greet()
    targets = (me.sibling, me.other_y, me.on_a(1), me.on_a(3), me.on_b(1), me.on_b(3))
    SIB, YY, AR, AL, BR, BL = range(6)

    def copy(kind, rr, a, b):
        yy, xi, zi = me.spot(rr, a % RING, b % RING)
        block = g_ref.at[me.core, yy, xi, zi]
        at = (yy * RING + xi) * RING + zi
        got = sib_recv if kind == SIB else recv
        return remote(block, block, send.at[kind, at], got.at[at], targets[kind])

    def arrived(rr, a, b):
        copy(AR, rr, a, b).wait_recv()

    def start(kinds, rr, a, b):
        for kind in kinds:
            copy(kind, rr, a, b).start()

    pa, pb = me.pa, me.pb
    mine = pltpu.make_async_copy(
        w_ref.at[me.core], g_ref.at[me.core, me.y, me.x, me.z, me.core], local_sem
    )
    mine.start()
    first = remote(
        w_ref.at[1 - me.core],
        g_ref.at[1 - me.core, me.y, me.x, me.z, me.core],
        first_sem.at[0],
        first_sem.at[1],
        me.sibling,
    )
    first.start()
    arriving = remote(
        w_ref.at[me.core],
        g_ref.at[me.core, me.y, me.x, me.z, 1 - me.core],
        first_sem.at[0],
        first_sem.at[1],
        me.sibling,
    )
    mine.wait()
    arriving.wait_recv()
    start((YY, AR, AL, BR, BL, SIB), 0, pa, pb)
    copy(YY, 1, pa, pb).wait_recv()
    start((AR, AL, BR, BL, SIB), 1, pa, pb)
    for rr in range(2):
        arrived(rr, pa, pb + 3)
        start((BR, AR, AL, SIB) if rr == 0 else (AR, AL, SIB), rr, pa, pb + 3)
        arrived(rr, pa, pb + 1)
        start((BL, AR, AL, SIB) if rr == 1 else (AR, AL, SIB), rr, pa, pb + 1)
    for rr in range(2):
        arrived(rr, pa, pb + 2)
        start((AR, AL, SIB), rr, pa, pb + 2)

    def order(j):
        return (j * 3) % 4 - (j // 2) * ((j * 3) % 4 - (j - 1))

    def along_a(j, carry):
        b = pb + order(j)
        arrived(0, pa + 3, b)
        start((AR, SIB), 0, pa + 3, b)
        arrived(0, pa + 1, b)
        start((SIB,), 0, pa + 1, b)
        arrived(1, pa + 3, b)
        start((SIB,), 1, pa + 3, b)
        arrived(1, pa + 1, b)
        start((AL, SIB), 1, pa + 1, b)
        return carry

    lax.fori_loop(0, RING, along_a, 0)

    def across_a(j, carry):
        b = pb + order(j)
        for rr in range(2):
            arrived(rr, pa + 2, b)
            start((SIB,), rr, pa + 2, b)
        return carry

    lax.fori_loop(0, RING, across_a, 0)

    def from_sibling(at, carry):
        block = g_ref.at[1 - me.core, at // 16, (at // 4) % 4, at % 4]
        remote(block, block, send.at[SIB, at], sib_recv.at[at], me.sibling).wait_recv()
        mine_out = g_ref.at[me.core, at // 16, (at // 4) % 4, at % 4]
        remote(mine_out, mine_out, send.at[SIB, at], sib_recv.at[at], me.sibling).wait_send()
        return carry

    lax.fori_loop(0, 2 * RING * RING, from_sibling, 0)
    first.wait_send()
    copy(YY, 0, pa, pb).wait_send()
    for rr in range(2):
        copy(BR, rr, pa, pb).wait_send()
        copy(BL, rr, pa, pb).wait_send()
    copy(BR, 0, pa, pb + 3).wait_send()
    copy(BL, 1, pa, pb + 1).wait_send()

    def sent_a(b, carry):
        for rr in range(2):
            copy(AR, rr, pa, b).wait_send()
            copy(AL, rr, pa, b).wait_send()
        copy(AR, 0, pa + 3, b).wait_send()
        copy(AL, 1, pa + 1, b).wait_send()
        return carry

    lax.fori_loop(0, RING, sent_a, 0)


def gather(shard):
    halves, rows, width = shard.shape
    blocks = 2 * RING * RING
    out = pl.pallas_call(
        gather_kernel,
        out_shape=jax.ShapeDtypeStruct((halves, 2, RING, RING, 2, rows, width), shard.dtype),
        in_specs=[pl.BlockSpec(memory_space=pl.ANY)],
        out_specs=pl.BlockSpec(memory_space=pl.ANY),
        scratch_shapes=[
            pltpu.SemaphoreType.DMA,
            pltpu.SemaphoreType.DMA((2,)),
            pltpu.SemaphoreType.DMA((6, blocks)),
            pltpu.SemaphoreType.DMA((blocks,)),
            pltpu.SemaphoreType.DMA((blocks,)),
        ],
        compiler_params=pltpu.CompilerParams(collective_id=0, has_side_effects=True),
        name="gather_weights",
    )(shard)
    return out.reshape(halves, blocks * 2 * rows, width)


def scatter_kernel(
    p_ref,
    o_ref,
    own,
    sib,
    from_a,
    from_b,
    from_y,
    from_core,
    load_sem,
    sib_send,
    sib_recv,
    a_send,
    a_recv,
    b_send,
    b_recv,
    last_sem,
):
    me = Place()
    pa, pb = me.pa, me.pb
    load = pltpu.make_async_copy(p_ref.at[me.core], own, load_sem)
    load.start()
    me.greet()

    def to_sibling(at):
        group = at // 8
        a = (pb + 2 + group + (group // 2) * (5 - 2 * group)) % RING
        b = (pa + 2 + (at // 2) % RING) % RING
        peer_core = 1 - me.core
        xi = a + peer_core * (b - a)
        zi = b + peer_core * (a - b)
        yy = me.row(at % 2)
        where = (yy * RING + xi) * RING + zi
        return remote(
            p_ref.at[1 - me.core, yy, xi, zi],
            sib.at[yy, xi, zi],
            sib_send.at[where],
            sib_recv.at[where],
            me.sibling,
        )

    blocks = 2 * RING * RING

    def send_all(at, carry):
        to_sibling(at).start()
        return carry

    lax.fori_loop(0, blocks, send_all, 0)
    load.wait()

    def with_sibling(rr, a, b):
        yy, xi, zi = me.spot(rr, a % RING, b % RING)
        where = (yy * RING + xi) * RING + zi
        remote(
            sib.at[yy, xi, zi], sib.at[yy, xi, zi], sib_send.at[where], sib_recv.at[where], me.sibling
        ).wait_recv()
        own[yy, xi, zi] = (
            own[yy, xi, zi].astype(F32) + sib[yy, xi, zi].astype(F32)
        ).astype(own.dtype)

    def send_a(side, slot, rr, a, b):
        yy, xi, zi = me.spot(rr, a % RING, b % RING)
        return remote(
            own.at[yy, xi, zi],
            from_a.at[side, slot],
            a_send.at[side, slot],
            a_recv.at[side, slot],
            me.on_a(1 if side == 0 else 3),
        )

    def add_a(side, slot, rr, a, b):
        yy, xi, zi = me.spot(rr, a % RING, b % RING)
        send_a(side, slot, rr, a, b).wait_recv()
        own[yy, xi, zi] = (
            own[yy, xi, zi].astype(F32) + from_a[side, slot].astype(F32)
        ).astype(own.dtype)

    def opposite(j, carry):
        b = (pb + 2 + j) % RING
        with_sibling(0, pa + 2, b)
        send_a(0, b, 0, pa + 2, b).start()
        with_sibling(1, pa + 2, b)
        send_a(1, b, 1, pa + 2, b).start()
        return carry

    def direct(j, carry):
        b = (pb + 2 + j) % RING
        with_sibling(1, pa + 1, b)
        send_a(0, 8 + b, 1, pa + 1, b).start()
        with_sibling(0, pa + 3, b)
        send_a(1, 4 + b, 0, pa + 3, b).start()
        return carry

    def onward(j, carry):
        b = (pb + 2 + j) % RING
        with_sibling(0, pa + 1, b)
        add_a(0, b, 0, pa + 1, b)
        send_a(0, 4 + b, 0, pa + 1, b).start()
        with_sibling(1, pa + 3, b)
        add_a(1, b, 1, pa + 3, b)
        send_a(1, 8 + b, 1, pa + 3, b).start()
        return carry

    def finish_a(rr, b):
        yy, xi, zi = me.spot(rr, pa, b % RING)
        slot = 4 + 4 * rr + b % RING
        send_a(0, slot, rr, pa, b).wait_recv()
        send_a(1, slot, rr, pa, b).wait_recv()
        own[yy, xi, zi] = (
            own[yy, xi, zi].astype(F32)
            + from_a[0, slot].astype(F32)
            + from_a[1, slot].astype(F32)
        ).astype(own.dtype)

    lax.fori_loop(0, RING, opposite, 0)
    lax.fori_loop(0, RING, direct, 0)
    lax.fori_loop(0, RING, onward, 0)

    def kept(at, carry):
        yy, xi, zi = me.spot(at % 2, pa, (pb + at // 2) % RING)
        where = (yy * RING + xi) * RING + zi
        remote(
            sib.at[yy, xi, zi], sib.at[yy, xi, zi], sib_send.at[where], sib_recv.at[where], me.sibling
        ).wait_recv()
        own[yy, xi, zi] = (
            own[yy, xi, zi].astype(F32) + sib[yy, xi, zi].astype(F32)
        ).astype(own.dtype)
        return carry

    lax.fori_loop(0, 2 * RING, kept, 0)

    def send_b(side, slot, rr, b):
        yy, xi, zi = me.spot(rr, pa, b % RING)
        return remote(
            own.at[yy, xi, zi],
            from_b.at[side, slot],
            b_send.at[side, slot],
            b_recv.at[side, slot],
            me.on_b(1 if side == 0 else 3),
        )

    def add_b(side, slot, rr, b):
        yy, xi, zi = me.spot(rr, pa, b % RING)
        send_b(side, slot, rr, b).wait_recv()
        own[yy, xi, zi] = (
            own[yy, xi, zi].astype(F32) + from_b[side, slot].astype(F32)
        ).astype(own.dtype)

    finish_a(0, pb + 2)
    send_b(0, 0, 0, pb + 2).start()
    finish_a(1, pb + 2)
    send_b(1, 0, 1, pb + 2).start()
    finish_a(1, pb + 1)
    send_b(0, 2, 1, pb + 1).start()
    finish_a(0, pb + 3)
    send_b(1, 1, 0, pb + 3).start()
    finish_a(0, pb + 1)
    add_b(0, 0, 0, pb + 1)
    send_b(0, 1, 0, pb + 1).start()
    finish_a(1, pb + 3)
    add_b(1, 0, 1, pb + 3)
    send_b(1, 2, 1, pb + 3).start()
    finish_a(1, pb)
    add_b(0, 2, 1, pb)
    add_b(1, 2, 1, pb)
    yy, xi, zi = me.spot(1, pa, pb)
    over = remote(own.at[yy, xi, zi], from_y, last_sem.at[0], last_sem.at[1], me.other_y)
    over.start()
    finish_a(0, pb)
    add_b(0, 1, 0, pb)
    add_b(1, 1, 0, pb)
    over.wait_recv()
    yy, xi, zi = me.spot(0, pa, pb)
    own[yy, xi, zi] = (own[yy, xi, zi].astype(F32) + from_y[...].astype(F32)).astype(own.dtype)
    last = remote(
        own.at[yy, xi, zi, 1 - me.core], from_core, last_sem.at[2], last_sem.at[3], me.sibling
    )
    last.start()
    o_ref[me.core] = own[yy, xi, zi, me.core].astype(F32)
    last.wait_recv()
    o_ref[1 - me.core] = from_core[...].astype(F32)
    last.wait_send()
    over.wait_send()

    def sent_sibling(at, carry):
        to_sibling(at).wait_send()
        return carry

    lax.fori_loop(0, blocks, sent_sibling, 0)

    def sent_a(slot, carry):
        for side in range(2):
            remote(
                own.at[0, 0, 0],
                from_a.at[side, slot],
                a_send.at[side, slot],
                a_recv.at[side, slot],
                me.on_a(1 if side == 0 else 3),
            ).wait_send()
        return carry

    lax.fori_loop(0, 3 * RING, sent_a, 0)
    for slot in range(3):
        for side in range(2):
            remote(
                own.at[0, 0, 0],
                from_b.at[side, slot],
                b_send.at[side, slot],
                b_recv.at[side, slot],
                me.on_b(1 if side == 0 else 3),
            ).wait_send()


def scatter(partial):
    halves, whole, width = partial.shape
    blocks = 2 * RING * RING
    rows = whole // (2 * blocks)
    return pl.pallas_call(
        scatter_kernel,
        out_shape=jax.ShapeDtypeStruct((halves, rows, width), F32),
        in_specs=[pl.BlockSpec(memory_space=pl.ANY)],
        out_specs=pl.BlockSpec(memory_space=pltpu.VMEM),
        scratch_shapes=[
            pltpu.VMEM((2, RING, RING, 2, rows, width), partial.dtype),
            pltpu.VMEM((2, RING, RING, 2, rows, width), partial.dtype),
            pltpu.VMEM((2, 3 * RING, 2, rows, width), partial.dtype),
            pltpu.VMEM((2, 3, 2, rows, width), partial.dtype),
            pltpu.VMEM((2, rows, width), partial.dtype),
            pltpu.VMEM((rows, width), partial.dtype),
            pltpu.SemaphoreType.DMA,
            pltpu.SemaphoreType.DMA((blocks,)),
            pltpu.SemaphoreType.DMA((blocks,)),
            pltpu.SemaphoreType.DMA((2, 3 * RING)),
            pltpu.SemaphoreType.DMA((2, 3 * RING)),
            pltpu.SemaphoreType.DMA((2, 3)),
            pltpu.SemaphoreType.DMA((2, 3)),
            pltpu.SemaphoreType.DMA((4,)),
        ],
        compiler_params=pltpu.CompilerParams(
            collective_id=1, has_side_effects=True, vmem_limit_bytes=48 * 1024 * 1024
        ),
        name="scatter_gradients",
    )(partial.reshape(halves, 2, RING, RING, 2, rows, width))


def shifted(block, axis, distance):
    devices = range(lax.axis_size(axis))
    route = [(i - distance, i) for i in devices if i - distance in devices]
    return lax.ppermute(block, axis, route)


def swapped(block):
    return lax.ppermute(block, "chan", [(0, 1), (1, 0)])


def low(x):
    return lax.reduce_precision(x, 8, 7)


def both_sum(part):
    rounded = low(part)
    return rounded + swapped(rounded.astype(BF)).astype(F32)


def dot(a, b, dims):
    return lax.dot_general(a, b, (dims, ((), ())), preferred_element_type=F32)


def norm_back(values, inverse, gain, back):
    scaled = back * gain
    mean = jnp.mean(scaled * values, axis=-1, keepdims=True)
    return inverse * (scaled - values * (inverse * inverse) * mean)


def adam_update(weight, moment_one, second, gradient, step_rate, weight_decay):
    first_new = beta_one * moment_one + (1.0 - beta_one) * gradient
    second_new = beta_two * second + (1.0 - beta_two) * gradient * gradient
    first_hat = first_new / (1.0 - beta_one**STEP)
    second_hat = second_new / (1.0 - beta_two**STEP)
    weight_new = weight - step_rate * (
        first_hat / (jnp.sqrt(second_hat) + adam_eps) + weight_decay * weight
    )
    return (weight_new, first_new, second_new)


def body(
    tokens,
    cotangent,
    w_in,
    w_in_m,
    w_in_v,
    w_out,
    w_out_m,
    w_out_v,
    w_gu,
    w_gu_m,
    w_gu_v,
    w_down,
    w_down_m,
    w_down_v,
    vectors,
    vectors_m,
    vectors_v,
):
    seq_count = lax.axis_size("seq")
    seq_index = lax.axis_index("seq")
    chan = lax.axis_index("chan")
    half_seq = seq_count // 2
    rows = w_in.shape[0]
    n_in = 3 * w_in.shape[2]
    n_out = w_out.shape[1]
    n_gu = 2 * w_gu.shape[2]
    n_down = w_down.shape[1]
    wide = n_out
    hid = n_down
    n_vec = n_gu - n_in - n_out - n_down

    theirs = swapped(vectors)
    first = jnp.where(chan == 0, vectors, theirs)
    second = jnp.where(chan == 0, theirs, vectors)
    vec_rows = jnp.concatenate([first, second], axis=1).T
    vec_high = low(vec_rows)
    vec_low = vec_rows - vec_high
    vec_cols = jnp.pad(
        jnp.concatenate([vec_high, vec_low], axis=1).astype(BF), ((0, 0), (0, n_vec - 10))
    )
    shard = jnp.stack(
        [
            w_gu.astype(BF).reshape(rows, n_gu),
            jnp.concatenate(
                [
                    w_in.astype(BF).reshape(rows, n_in),
                    w_out.astype(BF),
                    w_down.astype(BF),
                    vec_cols,
                ],
                axis=1,
            ),
        ],
        axis=0,
    )
    full = gather(shard)
    full_gu = full[0]
    full_in = full[1, :, :n_in]
    full_out = full[1, :, n_in : n_in + n_out]
    full_down = full[1, :, n_in + n_out : n_in + n_out + n_down]
    vec_all = full[1, :, n_in + n_out + n_down : n_in + n_out + n_down + 10].astype(F32)
    vec_all = (vec_all[:, :5] + vec_all[:, 5:]).T
    taps = lax.dynamic_slice_in_dim(vec_all[2:5], chan * wide, wide, 1)
    gain_one, gain_two = vec_all[0], vec_all[1]

    inputs = tokens.astype(F32)
    inverse_one = lax.rsqrt(jnp.mean(inputs * inputs, axis=-1, keepdims=True) + norm_eps)
    normed = (inputs * inverse_one * gain_one).astype(BF)
    mixed = dot(normed, full_in, ((1,), (0,)))
    gate_b = mixed[:, :wide]
    gate_c = mixed[:, wide : 2 * wide]
    values = mixed[:, 2 * wide :]
    gated = (gate_b * values).astype(BF)
    carried = shifted(gated[-2:], "seq", 1)
    carried = jnp.where(seq_index % half_seq == 0, jnp.zeros_like(carried), carried)
    extended = jnp.concatenate([carried, gated], axis=0).astype(F32)
    convolved = taps[0] * extended[:-2] + taps[1] * extended[1:-1] + taps[2] * extended[2:]
    inner = (gate_c * convolved).astype(BF)
    middle = inputs + both_sum(dot(inner, full_out, ((1,), (1,))))
    inverse_two = lax.rsqrt(jnp.mean(middle * middle, axis=-1, keepdims=True) + norm_eps)
    normed_two = (middle * inverse_two * gain_two).astype(BF)
    gate_up = dot(normed_two, full_gu, ((1,), (0,)))
    gate = gate_up[:, :hid]
    up = gate_up[:, hid:]
    back_hidden = dot(cotangent, full_down, ((1,), (0,)))
    sig = jax.nn.sigmoid(gate)
    act = gate * sig
    hidden = (act * up).astype(BF)
    back_gate = (back_hidden * up * sig * (1.0 + gate * (1.0 - sig))).astype(BF)
    back_up = (back_hidden * act).astype(BF)
    back_gate_up = jnp.concatenate([back_gate, back_up], axis=1)
    block_out = middle + both_sum(dot(hidden, full_down, ((1,), (1,))))
    back_normed_two = both_sum(dot(back_gate_up, full_gu, ((1,), (1,))))
    term_gu = dot(normed_two, back_gate_up, ((0,), (0,))).astype(BF)
    term_down = dot(cotangent, hidden, ((0,), (0,))).astype(BF)
    back_out = cotangent.astype(F32)
    back_middle = back_out + norm_back(middle, inverse_two, gain_two, back_normed_two)
    gain_two_grad = jnp.sum(back_normed_two * middle * inverse_two, axis=0)
    back_branch = back_middle.astype(BF)
    back_inner = dot(back_branch, full_out, ((1,), (0,)))
    back_gate_c = back_inner * convolved
    back_conv = (back_inner * gate_c).astype(BF)
    ahead = shifted(back_conv[:2], "seq", -1)
    ahead = jnp.where(seq_index % half_seq == half_seq - 1, jnp.zeros_like(ahead), ahead)
    back_extended = jnp.concatenate([back_conv, ahead], axis=0).astype(F32)
    back_gated = (
        taps[0] * back_extended[2:] + taps[1] * back_extended[1:-1] + taps[2] * back_extended[:-2]
    )
    back_conv_wide = back_conv.astype(F32)
    tap_grads = jnp.stack(
        [
            jnp.sum(back_conv_wide * extended[:-2], axis=0),
            jnp.sum(back_conv_wide * extended[1:-1], axis=0),
            jnp.sum(back_conv_wide * extended[2:], axis=0),
        ],
        axis=0,
    )
    back_mixed = jnp.concatenate(
        [
            (back_gated * values).astype(BF),
            back_gate_c.astype(BF),
            (back_gated * gate_b).astype(BF),
        ],
        axis=1,
    )
    back_normed = both_sum(dot(back_mixed, full_in, ((1,), (1,))))
    input_grad = back_middle + norm_back(inputs, inverse_one, gain_one, back_normed)
    gain_one_grad = jnp.sum(back_normed * inputs * inverse_one, axis=0)
    term_in = dot(normed, back_mixed, ((0,), (0,))).astype(BF)
    term_out = dot(back_branch, inner, ((0,), (0,))).astype(BF)

    width = inputs.shape[1]
    tap_rows = lax.dynamic_update_slice_in_dim(
        jnp.zeros((3, width), F32), tap_grads, chan * wide, 1
    )
    vec_grad = jnp.concatenate([gain_one_grad[None], gain_two_grad[None], tap_rows], axis=0)
    vec_term = jnp.pad(vec_grad.T.astype(BF), ((0, 0), (0, n_vec - 5)))
    summed = scatter(
        jnp.stack(
            [term_gu, jnp.concatenate([term_in, term_out, term_down, vec_term], axis=1)], axis=0
        )
    )
    grad_gu = summed[0].reshape(w_gu.shape)
    grad_in = summed[1, :, :n_in].reshape(w_in.shape)
    grad_out = summed[1, :, n_in : n_in + n_out]
    grad_down = summed[1, :, n_in + n_out : n_in + n_out + n_down]
    sum_vec = summed[1, :, n_in + n_out + n_down : n_in + n_out + n_down + 5].T
    sum_taps = jnp.where(
        chan == seq_index // half_seq, sum_vec[2:], swapped(sum_vec[2:])
    )
    grad_vectors = lax.dynamic_slice_in_dim(
        jnp.concatenate([sum_vec[:2], sum_taps], axis=0), chan * (rows // 2), rows // 2, 1
    )
    in_new = adam_update(w_in, w_in_m, w_in_v, grad_in, rate_matrix, decay_matrix)
    out_new = adam_update(w_out, w_out_m, w_out_v, grad_out, rate_matrix, decay_matrix)
    gu_new = adam_update(w_gu, w_gu_m, w_gu_v, grad_gu, rate_matrix, decay_matrix)
    down_new = adam_update(w_down, w_down_m, w_down_v, grad_down, rate_matrix, decay_matrix)
    vec_new = adam_update(vectors, vectors_m, vectors_v, grad_vectors, rate_vector, 0.0)
    return (block_out, input_grad, *in_new, *out_new, *gu_new, *down_new, *vec_new)


def solution(mesh):
    matrices = [P("seq", None, "chan")] * 3 + [P("seq", "chan")] * 3
    weights = (*matrices, *matrices, *[P(None, ("seq", "chan"))] * 3)
    return jax.shard_map(
        body,
        mesh=mesh,
        in_specs=(P("seq", None), P("seq", None), *weights),
        out_specs=(P("seq", None), P("seq", None), *weights),
        check_vma=False,
    )
```

time: 945 us -> 334 us (0.35)
  blocking collectives: 386 us -> 0 us
  waiting for transfers between devices: 297 us -> 42 us
  Pallas kernels: 0 us -> 132 us
  local copies, waits for them, and re-layouts: 83.2 us -> 32.2 us
  between operations: 15.2 us -> 1.21 us
  other arithmetic: 63.2 us -> 51.5 us
  starting transfers between devices: 26.5 us -> 16.7 us
    all_gather x1 -> x0, blocking collectives: 319 us -> none  [body(): all_vectors = lax.all_gather(vectors, ('seq', 'chan'), axis=1, tiled=True)]
    reduce_scatter x1 -> x0, waiting for transfers between devices: 231 us -> none  [sent_together(): out = lax.psum_scatter(both, axis, scatter_dimension=dim, tiled=True)]
    pallas_call x0 -> x2, Pallas kernels: none -> 132 us  [the longest x1 66.2 us: scatter(): pl.pallas_call(scatter_kernel, out_shape=jax.ShapeDtypeStruct((halves, ro...]
    unnamed x1 -> x0, blocking collectives: 67.5 us -> none
    all_to_all x4 -> x0, waiting for transfers between devices: 62.4 us -> none  [copy_for_each(): lax.all_to_all(jnp.broadcast_to(x[None], (peers, *x.shape)), axis, 0, 0,...]
    unnamed x125 -> x74, local copies, waits for them, and re-layouts: 59.5 us -> 2.02 us
    ppermute x0 -> x6, waiting for transfers between devices: none -> 41 us  [swapped(): return lax.ppermute(block, 'chan', [(0, 1), (1, 0)])]
    concatenate x3, other arithmetic: 27.5 us -> 6.93 us  [the longest x1 6.84 us: body(): jnp.concatenate([term_in, term_out, term_down, vec_term], axis=1)]
  transfers between devices with their start and end apart: 8 -> 8, of which waited for: 6 -> 5; matrix products, arithmetic and copies ran while one was open for 7% -> 16% of each run, Pallas kernels for 0% -> 0%
where the time goes in v1:
time: 334 us; the launch traced here: 332 us
  Pallas kernels  132 us (40%)
  matrix products  56.3 us (17%)
  other arithmetic  51.5 us (15%)
  waiting for transfers between devices  42 us (13%)
  local copies, waits for them, and re-layouts  32.2 us (10%)
  starting transfers between devices  16.7 us (5%)
    pallas_call x1, Pallas kernels, scatter(): pl.pallas_call(scatter_kernel, out_shape=jax.ShapeDtypeStruct((halves, ro...  66.2 us
    pallas_call x1, Pallas kernels, gather(): pl.pallas_call(gather_kernel, out_shape=jax.ShapeDtypeStruct((halves, 2,...  66 us
    dot_general x12, matrix products, dot(): return lax.dot_general(a, b, (dims, ((), ())), preferred_element_type=F32)  56.3 us
    ppermute x6, waiting for transfers between devices, swapped(): return lax.ppermute(block, 'chan', [(0, 1), (1, 0)])  41 us
    another operation x1, other arithmetic, body(): jnp.stack([term_gu, jnp.concatenate([term_in, term_out, term_down, vec_te...  16.5 us
    concatenate x1, local copies, waits for them, and re-layouts, body(): jnp.concatenate([term_in, term_out, term_down, vec_term], axis=1)  12.7 us
    ppermute x6, starting transfers between devices, swapped(): return lax.ppermute(block, 'chan', [(0, 1), (1, 0)])  10.7 us
    slice x1, local copies, waits for them, and re-layouts, body(): full_gu = full[0]  8.3 us
  transfers between devices with their start and end apart: 8, of which 5 were waited for; matrix products, arithmetic and copies ran while one was open for 16% of the time, Pallas kernels for 0%

profile of v1, /device:TPU:1, one launch (start us, length us, event | category | flops | bytes accessed | tf_op | source)
XLA Modules:
  0.0 332.1 jit_solution(8905425911223564195)
XLA Ops:
  1.5 3.7 %collective-permute-start = (f32[5,8]{0,1:T(8,128)S(1)}, f32[5,8]{0,1:T(8,128)S(1)}, u32[]{:S(2)}, u32[]{:S(2)}) collective-permute-start(f32[5,8]{0,1:T(8,128)S(1)} %copy.63), channel_id=1, source_target_pairs={{0,1},{1,0},{2,3},{3,2},{4,5},{5,4},{6,7},{7,6},{8,9},{9,8},{10,11... | collective-permute-start | bytes 488 | tf_op jit(solution)/shard_map/ppermute | solution.py:456
  10.7 66.0 %gather_weights.1 = bf16[2,2,4,4,2,16,4608]{6,5,4,3,2,1,0:T(8,128)(2,1)} custom-call(bf16[2,16,4608]{2,1,0:T(8,128)(2,1)} %pad_maximum_fusion.9.w_ref), custom_call_target="tpu_custom_call" | custom-call | tf_op jit(solution)/shard_map/gather_weights/pallas_call | solution.py:186
  77.9 3.3 %fusion.6 = f32[384,1536]{1,0:T(8,128)S(1)} fusion(bf16[2,1024,4608]{2,1,0:T(8,128)(2,1)} %bitcast.86, bf16[384,1024]{1,0:T(8,128)(2,1)S(1)} %copy-done.3, f32[1024]{0:T(1024)S(1)} %bitcast.103, f32[384]{0:T(512)S(1)} %get-tuple-element.79), kind=kOutput, calls=%fused_computation.25 | convolution fusion | flops 1209532416 | bytes 6297088 | tf_op jit(solution)/shard_map/dot_general | solution.py:469
  85.8 3.0 fusion.59
  90.3 8.3 %slice.125 = bf16[1,2,4,4,2,16,4608]{6,5,4,3,2,1,0:T(8,128)(2,1)} slice(bf16[2,2,4,4,2,16,4608]{6,5,4,3,2,1,0:T(8,128)(2,1)} %gather_weights.1), slice={[0:1], [0:2], [0:4], [0:4], [0:2], [0:16], [0:4608]} | slice | bytes 18874368 | tf_op jit(solution)/shard_map/slice | solution.py:546
  98.6 10.6 %collective-permute-done.2 = bf16[384,1024]{1,0:T(8,128)(2,1)S(1)} collective-permute-done((bf16[384,1024]{1,0:T(8,128)(2,1)S(1)}, bf16[384,1024]{1,0:T(8,128)(2,1)S(1)}, u32[]{:S(2)}, u32[]{:S(2)}) %collective-permute-start.2) | collective-permute-done | bytes 786464 | tf_op jit(solution)/shard_map/ppermute | solution.py:456
  112.4 7.1 %fusion.49 = f32[384,4608]{1,0:T(8,128)S(1)} fusion(bf16[1024,4608]{1,0:T(8,128)(2,1)} %bitcast.94, f32[384,1024]{1,0:T(8,128)S(1)} %get-tuple-element.60, f32[1024]{0:T(1024)S(1)} %bitcast.98, f32[384]{0:T(512)S(1)} %get-tuple-element.81), kind=kOutput, calls=%fused_computation.130 | convolution fusion | flops 3625058304 | bytes 18093568 | tf_op jit(solution)/shard_map/dot_general | solution.py:469
  119.5 6.7 %multiply_convert_fusion.1 = (bf16[384,2304]{1,0:T(8,128)(2,1)S(1)}, bf16[384,2304]{1,0:T(8,128)(2,1)S(1)}, bf16[384,2304]{1,0:T(8,128)(2,1)}) fusion(f32[384,4608]{1,0:T(8,128)S(1)} %fusion.49, bf16[384,1024]{1,0:T(8,128)(2,1)S(1)} %copy-done.17, bf16[2,1024,4608]{2,1,0:T(8,128)(2,1)} %bitcast.88), kind=kOutput, calls=%fused_computation.13 | convolution fusion | flops 1825210368 | bytes 17891328 | tf_op jit(solution)/shard_map/dot_general | solution.py:469
  126.2 5.3 %fusion.60 = (bf16[384,1024]{1,0:T(8,128)(2,1)}, f32[384,1024]{1,0:T(8,128)}) fusion(bf16[1024,4608]{1,0:T(8,128)(2,1)S(1)} %bitcast.97, bf16[384,2304]{1,0:T(8,128)(2,1)S(1)} %get-tuple-element.64, bf16[384,2304]{1,0:T(8,128)(2,1)S(1)} %get-tuple-element.63), kind=kOutput, calls=%fused_computation.133 | convolution fusion | flops 3631742976 | bytes 15335424 | tf_op jit(solution)/shard_map/dot_general | solution.py:469
  133.1 6.3 %fusion.61 = (bf16[384,1024]{1,0:T(8,128)(2,1)}, f32[384,1024]{1,0:T(8,128)}) fusion(bf16[384,2304]{1,0:T(8,128)(2,1)} %get-tuple-element.65, bf16[2,1024,4608]{2,1,0:T(8,128)(2,1)} %bitcast.89), kind=kOutput, calls=%fused_computation.134 | convolution fusion | flops 1812725760 | bytes 8847360 | tf_op jit(solution)/shard_map/dot_general | solution.py:469
  140.8 10.6 %collective-permute-done.4 = bf16[384,1024]{1,0:T(8,128)(2,1)} collective-permute-done((bf16[384,1024]{1,0:T(8,128)(2,1)}, bf16[384,1024]{1,0:T(8,128)(2,1)}, u32[]{:S(2)}, u32[]{:S(2)}) %collective-permute-start.4) | collective-permute-done | bytes 786464 | tf_op jit(solution)/shard_map/ppermute | solution.py:456
  153.7 14.6 %collective-permute-done.3 = bf16[384,1024]{1,0:T(8,128)(2,1)} collective-permute-done((bf16[384,1024]{1,0:T(8,128)(2,1)}, bf16[384,1024]{1,0:T(8,128)(2,1)}, u32[]{:S(2)}, u32[]{:S(2)}) %collective-permute-start.3) | collective-permute-done | bytes 786464 | tf_op jit(solution)/shard_map/ppermute | solution.py:456
  168.3 3.7 %multiply_add_fusion = (f32[384,1024]{1,0:T(8,128)S(1)}, f32[384,1024]{1,0:T(8,128)}) fusion(f32[384,1024]{1,0:T(8,128)} %copy-done, bf16[384,1024]{1,0:T(8,128)(2,1)S(1)} %copy-done.18, f32[384]{0:T(512)S(1)} %broadcast_multiply_fusion.1, f32[384]{0:T(512)S(1)} %get-tuple-element.80, f32[1024]{0:T(1024)S(1)} %bitcast.100, f32[384]{0:T(512)S(1)} %get-tuple-element.81, ...), kind=kLoop, calls=%fused_computation.39 | loop fusion | flops 4718592 | bytes 10232320 | tf_op jit(solution)/shard_map/add | solution.py:586
  174.3 4.0 %collective-permute-start.5 = (bf16[2,512]{1,0:T(2,128)(2,1)S(1)}, bf16[2,512]{1,0:T(2,128)(2,1)S(1)}, u32[]{:S(2)}, u32[]{:S(2)}) collective-permute-start(bf16[2,512]{1,0:T(2,128)(2,1)S(1)} %slice.158), channel_id=1, source_target_pairs={{2,0},{4,2},{6,4},{8,6},{10,8},{12,10},{14,12},{16,14},{18,16},{20... | collective-permute-start | bytes 6152 | tf_op jit(solution)/shard_map/ppermute | solution.py:452
  178.3 7.9 %convolution_convert_fusion = bf16[1024,4608]{1,0:T(8,128)(2,1)} fusion(bf16[384,2304]{1,0:T(8,128)(2,1)S(1)} %copy-done.13, bf16[384,2304]{1,0:T(8,128)(2,1)S(1)} %copy-done.11, f32[384,1024]{1,0:T(8,128)S(1)} %copy-done.1, f32[1024]{0:T(1024)S(1)} %bitcast.101, f32[384]{0:T(512)S(1)} %get-tuple-element.81), kind=kOutput, calls=%fused_computation.3 | convolution fusion | flops 3636854784 | bytes 14554624 | tf_op jit(solution)/shard_map/dot_general | solution.py:469
  186.9 4.9 %fusion.62 = (bf16[384,1024]{1,0:T(8,128)(2,1)}, f32[384,1024]{1,0:T(8,128)}) fusion(bf16[2,1024,4608]{2,1,0:T(8,128)(2,1)} %bitcast.91, bf16[384,512]{1,0:T(8,128)(2,1)S(1)} %multiply_convert_fusion.4, bf16[384,512]{1,0:T(8,128)(2,1)S(1)} %get-tuple-element.68, bf16[384,512]{1,0:T(8,128)(2,1)S(1)} %get-tuple-element.57), kind=kOutput, calls=%fused_computation.135 | convolution fusion | flops 1212284928 | bytes 6684672 | tf_op jit(solution)/shard_map/dot_general | solution.py:469
  193.3 4.3 %fusion.2 = bf16[1024,2304]{0,1:T(8,128)(2,1)} fusion(bf16[384,2304]{1,0:T(8,128)(2,1)S(1)} %copy-done.32, bf16[384,1024]{1,0:T(8,128)(2,1)S(1)} %copy-done.18), kind=kOutput, calls=%fused_computation.6 | convolution fusion | flops 1814298624 | bytes 7274496 | tf_op jit(solution)/shard_map/dot_general | solution.py:469
  199.4 3.6 %convolution_convert_fusion.2 = bf16[1024,1536]{1,0:T(8,128)(2,1)} fusion(bf16[384,512]{1,0:T(8,128)(2,1)S(1)} %multiply_convert_fusion.4, bf16[384,512]{1,0:T(8,128)(2,1)S(1)} %get-tuple-element.68, bf16[384,512]{1,0:T(8,128)(2,1)S(1)} %get-tuple-element.57, bf16[384,1024]{1,0:T(8,128)(2,1)S(1)} %copy-done.4, f32[1024]{0:T(1024)S(1)} %bitcast.104, ...), kind=kOutput, calls=%fused_computation.10 | convolution fusion | flops 1214644224 | bytes 5117440 | tf_op jit(solution)/shard_map/dot_general | solution.py:469
  202.9 4.6 %copy.67 = bf16[1024,1536]{0,1:T(8,128)(2,1)} copy(bf16[1024,1536]{1,0:T(8,128)(2,1)} %convolution_convert_fusion.2) | data formatting | bytes 6291456 | tf_op jit(solution)/shard_map/convert_element_type | solution.py:618
  207.6 5.2 %collective-permute-done.6 = bf16[384,1024]{1,0:T(8,128)(2,1)} collective-permute-done((bf16[384,1024]{1,0:T(8,128)(2,1)}, bf16[384,1024]{1,0:T(8,128)(2,1)}, u32[]{:S(2)}, u32[]{:S(2)}) %collective-permute-start.6) | collective-permute-done | bytes 786464 | tf_op jit(solution)/shard_map/ppermute | solution.py:456
  215.0 6.8 %fusion.1 = bf16[1024,4608]{0,1:T(8,128)(2,1)} fusion(bf16[1024,5]{0,1:T(8,128)(2,1)S(1)} %maximum_bitcast_fusion.1, bf16[1024,2304]{0,1:T(8,128)(2,1)} %fusion.2, bf16[1024,512]{0,1:T(8,128)(2,1)} %convolution_convert_fusion.3, bf16[1024,1536]{0,1:T(8,128)(2,1)S(1)} %copy-done.2), kind=kLoop, calls=%fused_computation.4 | loop fusion | flops 47185920 | bytes 18360320 | tf_op jit(solution)/shard_map/concatenate | solution.py:629
  221.8 12.7 %copy.68 = bf16[1024,4608]{1,0:T(8,128)(2,1)} copy(bf16[1024,4608]{0,1:T(8,128)(2,1)} %fusion.1) | data formatting | bytes 18874368 | tf_op jit(solution)/shard_map/concatenate | solution.py:629
  234.6 16.5 %pad_maximum_fusion.p_ref = bf16[2,2,4,4,2,16,4608]{6,5,4,3,2,1,0:T(8,128)(2,1)} fusion(bf16[1,2,4,4,2,16,4608]{6,5,4,3,2,1,0:T(8,128)(2,1)} %bitcast.93, bf16[1,2,4,4,2,16,4608]{6,5,4,3,2,1,0:T(8,128)(2,1)} %bitcast.92), kind=kLoop, calls=%fused_computation.1 | loop fusion | flops 9437184 | bytes 37748736 | tf_op jit(solution)/shard_map/stack | solution.py:628
  251.1 66.2 %scatter_gradients.1 = f32[2,16,4608]{2,1,0:T(8,128)S(1)} custom-call(bf16[2,2,4,4,2,16,4608]{6,5,4,3,2,1,0:T(8,128)(2,1)} %pad_maximum_fusion.p_ref), custom_call_target="tpu_custom_call" | custom-call | tf_op jit(solution)/shard_map/scatter_gradients/pallas_call | solution.py:421
  (143 shorter events, 44.8 us)
Async XLA Ops:
  0.7 8.4 %copy-start.3 = (bf16[384,1024]{1,0:T(8,128)(2,1)S(1)}, bf16[384,1024]{1,0:T(8,128)(2,1)}, u32[]{:S(2)}) copy-start(bf16[384,1024]{1,0:T(8,128)(2,1)} %param.17) | copy-start | bytes 2359300
  1.5 8.4 %collective-permute-start = (f32[5,8]{0,1:T(8,128)S(1)}, f32[5,8]{0,1:T(8,128)S(1)}, u32[]{:S(2)}, u32[]{:S(2)}) collective-permute-start(f32[5,8]{0,1:T(8,128)S(1)} %copy.63), channel_id=1, source_target_pairs={{0,1},{1,0},{2,3},{3,2},{4,5},{5,4},{6,7},{7,6},{8,9},{9,8},{10,11... | collective-permute-start | bytes 488 | tf_op jit(solution)/shard_map/ppermute | solution.py:456
  9.8 202.9 %copy-start.25 = (f32[384]{0:T(512)}, f32[384]{0:T(512)S(1)}, u32[]{:S(2)}) copy-start(f32[384]{0:T(512)S(1)} %get-tuple-element.79) | copy-start | bytes 4612
  81.4 3.1 collective-permute-start.1
  88.8 20.5 %collective-permute-start.2 = (bf16[384,1024]{1,0:T(8,128)(2,1)S(1)}, bf16[384,1024]{1,0:T(8,128)(2,1)S(1)}, u32[]{:S(2)}, u32[]{:S(2)}) collective-permute-start(bf16[384,1024]{1,0:T(8,128)(2,1)S(1)} %get-tuple-element.82), channel_id=1, source_target_pairs={{0,1},{1,0},{2,3},{3,2},{4,5},{5,4},{6,7},{7,6},{8,9},{9,8},{10,11... | collective-permute-start | bytes 2359304 | tf_op jit(solution)/shard_map/ppermute | solution.py:456
  112.3 39.1 %copy-start = (f32[384,1024]{1,0:T(8,128)}, f32[384,1024]{1,0:T(8,128)S(1)}, u32[]{:S(2)}) copy-start(f32[384,1024]{1,0:T(8,128)S(1)} %get-tuple-element.60) | copy-start | bytes 4718596
  112.4 7.1 %copy-start.17 = (bf16[384,1024]{1,0:T(8,128)(2,1)S(1)}, bf16[384,1024]{1,0:T(8,128)(2,1)}, u32[]{:S(2)}) copy-start(bf16[384,1024]{1,0:T(8,128)(2,1)} %param.18) | copy-start | bytes 2359300
  112.4 13.8 %slice-start = ((s8[9437184]{0:T(1024)(128)(4,1)}), s8[4194304]{0:T(1024)(128)(4,1)S(1)}, s32[]{:S(2)}) async-start(s8[9437184]{0:T(1024)(128)(4,1)} %bitcast.95), calls=%async_computation | async-start | bytes 8388608
  119.5 6.7 %slice-start.1 = ((s8[9437184]{0:T(1024)(128)(4,1)}), s8[4194304]{0:T(1024)(128)(4,1)S(1)}, s32[]{:S(2)}) async-start(s8[9437184]{0:T(1024)(128)(4,1)} %bitcast.95), calls=%async_computation.1 | async-start | bytes 8388608
  119.5 6.7 %slice-start.2 = ((s8[9437184]{0:T(1024)(128)(4,1)}), s8[1048576]{0:T(1024)(128)(4,1)S(1)}, s32[]{:S(2)}) async-start(s8[9437184]{0:T(1024)(128)(4,1)} %bitcast.95), calls=%async_computation.2 | async-start | bytes 2097152
  131.5 19.9 %collective-permute-start.4 = (bf16[384,1024]{1,0:T(8,128)(2,1)}, bf16[384,1024]{1,0:T(8,128)(2,1)}, u32[]{:S(2)}, u32[]{:S(2)}) collective-permute-start(bf16[384,1024]{1,0:T(8,128)(2,1)} %get-tuple-element.84), channel_id=1, source_target_pairs={{0,1},{1,0},{2,3},{3,2},{4,5},{5,4},{6,7},{7,6},{8,9},{9,8},{10,11... | collective-permute-start | bytes 2359304 | tf_op jit(solution)/shard_map/ppermute | solution.py:456
  139.4 28.9 %collective-permute-start.3 = (bf16[384,1024]{1,0:T(8,128)(2,1)}, bf16[384,1024]{1,0:T(8,128)(2,1)}, u32[]{:S(2)}, u32[]{:S(2)}) collective-permute-start(bf16[384,1024]{1,0:T(8,128)(2,1)} %get-tuple-element.86), channel_id=1, source_target_pairs={{0,1},{1,0},{2,3},{3,2},{4,5},{5,4},{6,7},{7,6},{8,9},{9,8},{10,11... | collective-permute-start | bytes 2359304 | tf_op jit(solution)/shard_map/ppermute | solution.py:456
  151.4 16.9 %copy-start.7 = (f32[384,1024]{1,0:T(8,128)S(1)}, f32[384,1024]{1,0:T(8,128)}, u32[]{:S(2)}) copy-start(f32[384,1024]{1,0:T(8,128)} %get-tuple-element.85) | copy-start | bytes 4718596
  151.4 16.9 %copy-start.14 = (f32[384,1024]{1,0:T(8,128)S(1)}, f32[384,1024]{1,0:T(8,128)}, u32[]{:S(2)}) copy-start(f32[384,1024]{1,0:T(8,128)} %get-tuple-element.87) | copy-start | bytes 4718596
  151.4 16.9 %copy-start.18 = (bf16[384,1024]{1,0:T(8,128)(2,1)S(1)}, bf16[384,1024]{1,0:T(8,128)(2,1)}, u32[]{:S(2)}) copy-start(bf16[384,1024]{1,0:T(8,128)(2,1)} %param.18) | copy-start | bytes 2359300
  174.3 12.0 %collective-permute-start.5 = (bf16[2,512]{1,0:T(2,128)(2,1)S(1)}, bf16[2,512]{1,0:T(2,128)(2,1)S(1)}, u32[]{:S(2)}, u32[]{:S(2)}) collective-permute-start(bf16[2,512]{1,0:T(2,128)(2,1)S(1)} %slice.158), channel_id=1, source_target_pairs={{2,0},{4,2},{6,4},{8,6},{10,8},{12,10},{14,12},{16,14},{18,16},{20... | collective-permute-start | bytes 6152 | tf_op jit(solution)/shard_map/ppermute | solution.py:452
  191.7 21.1 %collective-permute-start.6 = (bf16[384,1024]{1,0:T(8,128)(2,1)}, bf16[384,1024]{1,0:T(8,128)(2,1)}, u32[]{:S(2)}, u32[]{:S(2)}) collective-permute-start(bf16[384,1024]{1,0:T(8,128)(2,1)} %get-tuple-element.88), channel_id=1, source_target_pairs={{0,1},{1,0},{2,3},{3,2},{4,5},{5,4},{6,7},{7,6},{8,9},{9,8},{10,11... | collective-permute-start | bytes 2359304 | tf_op jit(solution)/shard_map/ppermute | solution.py:456
  207.6 7.4 %copy-start.2 = (bf16[1024,1536]{0,1:T(8,128)(2,1)S(1)}, bf16[1024,1536]{0,1:T(8,128)(2,1)}, u32[]{:S(2)}) copy-start(bf16[1024,1536]{0,1:T(8,128)(2,1)} %copy.67) | copy-start | bytes 9437188
  317.4 8.5 %copy-start.15 = (f32[16,2,2304]{2,1,0:T(2,128)S(1)}, f32[16,2,2304]{2,1,0:T(2,128)}, u32[]{:S(2)}) copy-start(f32[16,2,2304]{2,1,0:T(2,128)} %param.25) | copy-start | bytes 884740
  321.2 6.5 %copy-start.8 = (f32[384,1024]{1,0:T(8,128)S(1)}, f32[384,1024]{1,0:T(8,128)}, u32[]{:S(2)}) copy-start(f32[384,1024]{1,0:T(8,128)} %get-tuple-element.89) | copy-start | bytes 4718596
  321.3 6.5 %copy-start.26 = (f32[384]{0:T(512)S(1)}, f32[384]{0:T(512)}, u32[]{:S(2)}) copy-start(f32[384]{0:T(512)} %copy-done.25) | copy-start | bytes 4612
  321.3 6.5 %copy-start.28 = (f32[384]{0:T(512)S(1)}, f32[384]{0:T(512)}, u32[]{:S(2)}) copy-start(f32[384]{0:T(512)} %get-tuple-element.78) | copy-start | bytes 4612
  321.3 6.5 %copy-start.29 = (f32[384]{0:T(512)S(1)}, f32[384]{0:T(512)}, u32[]{:S(2)}) copy-start(f32[384]{0:T(512)} %broadcast_multiply_fusion) | copy-start | bytes 4612
  321.3 10.1 %collective-permute-start.7 = (f32[3,16]{1,0:T(4,128)S(1)}, f32[3,16]{1,0:T(4,128)S(1)}, u32[]{:S(2)}, u32[]{:S(2)}) collective-permute-start(f32[3,16]{1,0:T(4,128)S(1)} %slice.139), channel_id=1, source_target_pairs={{0,1},{1,0},{2,3},{3,2},{4,5},{5,4},{6,7},{7,6},{8,9},{9,8},{10,11... | collective-permute-start | bytes 584 | tf_op jit(solution)/shard_map/ppermute | solution.py:456
  (20 other events, 84.1 us)

commit v2 on v0

v2 whole, which is shorter than its diff:
```python
import jax
import jax.numpy as jnp
from jax import lax
from jax.experimental import pallas as pl
from jax.experimental.pallas import tpu as pltpu
from jax.sharding import PartitionSpec as P

STEP = 10
norm_eps = 1e-05
beta_one = 0.9
beta_two = 0.95
adam_eps = 1e-08
rate_matrix = 0.05
rate_vector = 0.5
decay_matrix = 0.1

MESH = pl.DeviceIdType.MESH
BF = jnp.bfloat16
F32 = jnp.float32

RING = 4


class Place:
    def __init__(self):
        s = lax.axis_index("seq")
        core = s % 2
        z = (s // 2) % RING
        x = (s // (2 * RING)) % RING
        y = s // (2 * RING * RING)
        self.s, self.core, self.y = s, core, y
        self.pa = x + core * (z - x)
        self.pb = z + core * (x - z)
        self.x, self.z = x, z
        step_x, step_z = 2 * RING, 2
        self.step_a = step_x + core * (step_z - step_x)
        self.step_b = step_z + core * (step_x - step_z)
        self.sibling = s + 1 - 2 * core
        self.other_y = s + (1 - 2 * y) * 2 * RING * RING

    def on_a(self, off):
        return self.s + ((self.pa + off) % RING - self.pa) * self.step_a

    def on_b(self, off):
        return self.s + ((self.pb + off) % RING - self.pb) * self.step_b

    def row(self, rr):
        return self.y + rr * (1 - 2 * self.y)

    def spot(self, rr, a, b):
        xi = a + self.core * (b - a)
        zi = b + self.core * (a - b)
        return self.row(rr), xi, zi

    def greet(self):
        barrier = pltpu.get_barrier_semaphore()
        peers = (self.sibling, self.other_y, self.on_a(1), self.on_a(3), self.on_b(1), self.on_b(3))
        for peer in peers:
            pl.semaphore_signal(barrier, inc=1, device_id={"seq": peer}, device_id_type=MESH)
        pl.semaphore_wait(barrier, len(peers))


def remote(src, dst, send_sem, recv_sem, target):
    return pltpu.make_async_remote_copy(
        src_ref=src,
        dst_ref=dst,
        send_sem=send_sem,
        recv_sem=recv_sem,
        device_id={"seq": target},
        device_id_type=MESH,
    )


class Gathering:
    def __init__(self, me, shard, out, sems, lead):
        self.me, self.shard, self.out, self.lead = me, shard, out, lead
        self.local_sem, self.first_sem, self.send, self.recv, self.sib_recv = sems
        self.targets = (
            me.sibling, me.other_y, me.on_a(1), me.on_a(3), me.on_b(1), me.on_b(3)
        )

    def block(self, half, *where):
        return self.out.at[(half, *self.lead, *where)]

    def copy(self, kind, rr, a, b):
        yy, xi, zi = self.me.spot(rr, a % RING, b % RING)
        block = self.block(self.me.core, yy, xi, zi)
        at = (yy * RING + xi) * RING + zi
        got = self.sib_recv if kind == SIB else self.recv
        return remote(block, block, self.send.at[kind, at], got.at[at], self.targets[kind])

    def arrived(self, rr, a, b):
        self.copy(AR, rr, a, b).wait_recv()

    def start(self, kinds, rr, a, b):
        for kind in kinds:
            self.copy(kind, rr, a, b).start()

    def own(self):
        me = self.me
        return pltpu.make_async_copy(
            self.shard.at[me.core],
            self.block(me.core, me.y, me.x, me.z, me.core),
            self.local_sem,
        )

    def first(self, half, core):
        me = self.me
        return remote(
            self.shard.at[half],
            self.block(half, me.y, me.x, me.z, core),
            self.first_sem.at[0],
            self.first_sem.at[1],
            me.sibling,
        )

    def begin(self):
        me = self.me
        self.own().start()
        self.first(1 - me.core, me.core).start()

    def enter(self):
        me = self.me
        self.own().wait()
        self.first(me.core, 1 - me.core).wait_recv()
        self.start((YY, AR, AL, BR, BL, SIB), 0, me.pa, me.pb)

    def second_row(self):
        me = self.me
        self.copy(YY, 1, me.pa, me.pb).wait_recv()
        self.start((AR, AL, BR, BL, SIB), 1, me.pa, me.pb)

    def along_b(self):
        pa, pb = self.me.pa, self.me.pb
        for rr in range(2):
            self.arrived(rr, pa, pb + 3)
            self.start((BR, AR, AL, SIB) if rr == 0 else (AR, AL, SIB), rr, pa, pb + 3)
            self.arrived(rr, pa, pb + 1)
            self.start((BL, AR, AL, SIB) if rr == 1 else (AR, AL, SIB), rr, pa, pb + 1)

    def across_b(self):
        pa, pb = self.me.pa, self.me.pb
        for rr in range(2):
            self.arrived(rr, pa, pb + 2)
            self.start((AR, AL, SIB), rr, pa, pb + 2)

    def order(self, j):
        return self.me.pb + (j * 3) % 4 - (j // 2) * ((j * 3) % 4 - (j - 1))

    def along_a(self):
        pa = self.me.pa

        def step(j, carry):
            b = self.order(j)
            self.arrived(0, pa + 3, b)
            self.start((AR, SIB), 0, pa + 3, b)
            self.arrived(0, pa + 1, b)
            self.start((SIB,), 0, pa + 1, b)
            self.arrived(1, pa + 3, b)
            self.start((SIB,), 1, pa + 3, b)
            self.arrived(1, pa + 1, b)
            self.start((AL, SIB), 1, pa + 1, b)
            return carry

        lax.fori_loop(0, RING, step, 0)

    def across_a(self):
        pa = self.me.pa

        def step(j, carry):
            b = self.order(j)
            for rr in range(2):
                self.arrived(rr, pa + 2, b)
                self.start((SIB,), rr, pa + 2, b)
            return carry

        lax.fori_loop(0, RING, step, 0)

    def from_sibling(self):
        me = self.me

        def step(at, carry):
            where = (at // 16, (at // 4) % 4, at % 4)
            for half, wait in ((1 - me.core, "r"), (me.core, "s")):
                block = self.block(half, *where)
                copy = remote(block, block, self.send.at[SIB, at], self.sib_recv.at[at], me.sibling)
                copy.wait_recv() if wait == "r" else copy.wait_send()
            return carry

        lax.fori_loop(0, 2 * RING * RING, step, 0)

    def sent(self):
        me = self.me
        pa, pb = me.pa, me.pb
        self.first(1 - me.core, me.core).wait_send()
        self.copy(YY, 0, pa, pb).wait_send()
        for rr in range(2):
            self.copy(BR, rr, pa, pb).wait_send()
            self.copy(BL, rr, pa, pb).wait_send()
        self.copy(BR, 0, pa, pb + 3).wait_send()
        self.copy(BL, 1, pa, pb + 1).wait_send()

        def step(b, carry):
            for rr in range(2):
                self.copy(AR, rr, pa, b).wait_send()
                self.copy(AL, rr, pa, b).wait_send()
            self.copy(AR, 0, pa + 3, b).wait_send()
            self.copy(AL, 1, pa + 1, b).wait_send()
            return carry

        lax.fori_loop(0, RING, step, 0)


SIB, YY, AR, AL, BR, BL = range(6)
EVERY = (slice(None),)


def gather_sems():
    blocks = 2 * RING * RING
    return [
        pltpu.SemaphoreType.DMA,
        pltpu.SemaphoreType.DMA((2,)),
        pltpu.SemaphoreType.DMA((6, blocks)),
        pltpu.SemaphoreType.DMA((blocks,)),
        pltpu.SemaphoreType.DMA((blocks,)),
    ]


def gather_kernel(wm_ref, wf_ref, m_ref, f_ref, *sems):
    me = Place()
    me.greet()
    mixer = Gathering(me, wm_ref, m_ref, sems[:5], ())
    feed = Gathering(me, wf_ref, f_ref, sems[5:], EVERY)
    mixer.begin()
    feed.begin()
    mixer.enter()
    mixer.second_row()
    feed.enter()
    mixer.along_b()
    feed.second_row()
    mixer.across_b()
    feed.along_b()
    mixer.along_a()
    feed.across_b()
    mixer.across_a()
    feed.along_a()
    feed.across_a()
    for part in (mixer, feed):
        part.from_sibling()
        part.sent()


def gather(mixer_rows, feed_rows):
    halves, rows, width = mixer_rows.shape
    kinds = feed_rows.shape[1]
    whole = (2, RING, RING, 2, rows, width)
    mixer, feed = pl.pallas_call(
        gather_kernel,
        out_shape=(
            jax.ShapeDtypeStruct((halves, *whole), BF),
            jax.ShapeDtypeStruct((halves, kinds, *whole), BF),
        ),
        in_specs=[pl.BlockSpec(memory_space=pl.ANY)] * 2,
        out_specs=[pl.BlockSpec(memory_space=pl.ANY)] * 2,
        scratch_shapes=gather_sems() + gather_sems(),
        compiler_params=pltpu.CompilerParams(collective_id=0, has_side_effects=True),
        name="gather_weights",
    )(mixer_rows, feed_rows)
    total = 4 * RING * RING * rows
    return mixer.reshape(halves, total, width), feed.reshape(halves, kinds, total, width)


class Scattering:
    def __init__(self, me, partial, out, refs, lead):
        self.me, self.partial, self.out, self.lead = me, partial, out, lead
        (
            self.mine,
            self.sib,
            self.from_a,
            self.from_b,
            self.from_y,
            self.from_core,
            self.load_sem,
            self.sib_send,
            self.sib_recv,
            self.a_send,
            self.a_recv,
            self.b_send,
            self.b_recv,
            self.last_sem,
        ) = refs

    def at(self, rr, a, b):
        return self.me.spot(rr, a % RING, b % RING)

    def add(self, where, *others):
        index = (*self.lead, *where)
        total = self.mine[index].astype(F32)
        for ref, i in others:
            total = total + ref[i].astype(F32)
        self.mine[index] = total.astype(self.mine.dtype)

    def load(self):
        return pltpu.make_async_copy(self.partial.at[self.me.core], self.mine, self.load_sem)

    def to_sibling(self, at):
        me = self.me
        group = at // 8
        a = (me.pb + 2 + group + (group // 2) * (5 - 2 * group)) % RING
        b = (me.pa + 2 + (at // 2) % RING) % RING
        peer_core = 1 - me.core
        where = (me.row(at % 2), a + peer_core * (b - a), b + peer_core * (a - b))
        index = (*self.lead, *where)
        return self.sibling_copy(self.partial.at[(peer_core, *index)], where)

    def sibling_copy(self, src, where):
        i = (where[0] * RING + where[1]) * RING + where[2]
        return remote(
            src,
            self.sib.at[(*self.lead, *where)],
            self.sib_send.at[i],
            self.sib_recv.at[i],
            self.me.sibling,
        )

    def begin(self):
        self.load().start()

        def step(at, carry):
            self.to_sibling(at).start()
            return carry

        lax.fori_loop(0, 2 * RING * RING, step, 0)

    def with_sibling(self, rr, a, b):
        where = self.at(rr, a, b)
        index = (*self.lead, *where)
        self.sibling_copy(self.sib.at[index], where).wait_recv()
        self.add(where, (self.sib, index))

    def send_a(self, side, slot, rr, a, b):
        return remote(
            self.mine.at[(*self.lead, *self.at(rr, a, b))],
            self.from_a.at[side, slot],
            self.a_send.at[side, slot],
            self.a_recv.at[side, slot],
            self.me.on_a(1 if side == 0 else 3),
        )

    def add_a(self, side, slot, rr, a, b):
        self.send_a(side, slot, rr, a, b).wait_recv()
        self.add(self.at(rr, a, b), (self.from_a, (side, slot)))

    def over_b(self, step):
        def body(j, carry):
            step((self.me.pb + 2 + j) % RING)
            return carry

        lax.fori_loop(0, RING, body, 0)

    def opposite(self):
        pa = self.me.pa

        def step(b):
            self.with_sibling(0, pa + 2, b)
            self.send_a(0, b, 0, pa + 2, b).start()
            self.with_sibling(1, pa + 2, b)
            self.send_a(1, b, 1, pa + 2, b).start()

        self.over_b(step)

    def direct(self):
        pa = self.me.pa

        def step(b):
            self.with_sibling(1, pa + 1, b)
            self.send_a(0, 8 + b, 1, pa + 1, b).start()
            self.with_sibling(0, pa + 3, b)
            self.send_a(1, 4 + b, 0, pa + 3, b).start()

        self.over_b(step)

    def onward(self):
        pa = self.me.pa

        def step(b):
            self.with_sibling(0, pa + 1, b)
            self.add_a(0, b, 0, pa + 1, b)
            self.send_a(0, 4 + b, 0, pa + 1, b).start()
            self.with_sibling(1, pa + 3, b)
            self.add_a(1, b, 1, pa + 3, b)
            self.send_a(1, 8 + b, 1, pa + 3, b).start()

        self.over_b(step)

    def kept(self):
        pa = self.me.pa

        def step(b):
            self.with_sibling(0, pa, b)
            self.with_sibling(1, pa, b)

        self.over_b(step)

    def finish_a(self, rr, b):
        slot = 4 + 4 * rr + b % RING
        pa = self.me.pa
        self.send_a(0, slot, rr, pa, b).wait_recv()
        self.send_a(1, slot, rr, pa, b).wait_recv()
        self.add(self.at(rr, pa, b), (self.from_a, (0, slot)), (self.from_a, (1, slot)))

    def send_b(self, side, slot, rr, b):
        return remote(
            self.mine.at[(*self.lead, *self.at(rr, self.me.pa, b))],
            self.from_b.at[side, slot],
            self.b_send.at[side, slot],
            self.b_recv.at[side, slot],
            self.me.on_b(1 if side == 0 else 3),
        )

    def add_b(self, side, slot, rr, b):
        self.send_b(side, slot, rr, b).wait_recv()
        self.add(self.at(rr, self.me.pa, b), (self.from_b, (side, slot)))

    def ring_b(self):
        pb = self.me.pb
        self.finish_a(0, pb + 2)
        self.send_b(0, 0, 0, pb + 2).start()
        self.finish_a(1, pb + 2)
        self.send_b(1, 0, 1, pb + 2).start()
        self.finish_a(1, pb + 1)
        self.send_b(0, 2, 1, pb + 1).start()
        self.finish_a(0, pb + 3)
        self.send_b(1, 1, 0, pb + 3).start()
        self.finish_a(0, pb + 1)
        self.add_b(0, 0, 0, pb + 1)
        self.send_b(0, 1, 0, pb + 1).start()
        self.finish_a(1, pb + 3)
        self.add_b(1, 0, 1, pb + 3)
        self.send_b(1, 2, 1, pb + 3).start()
        self.finish_a(1, pb)
        self.finish_a(0, pb)

    def over(self):
        me = self.me
        return remote(
            self.mine.at[(*self.lead, *self.at(1, me.pa, me.pb))],
            self.from_y,
            self.last_sem.at[0],
            self.last_sem.at[1],
            me.other_y,
        )

    def last(self):
        me = self.me
        return remote(
            self.mine.at[(*self.lead, *self.at(0, me.pa, me.pb), 1 - me.core)],
            self.from_core,
            self.last_sem.at[2],
            self.last_sem.at[3],
            me.sibling,
        )

    def across_y(self):
        pb = self.me.pb
        self.add_b(0, 2, 1, pb)
        self.add_b(1, 2, 1, pb)
        self.over().start()
        self.add_b(0, 1, 0, pb)
        self.add_b(1, 1, 0, pb)

    def across_cores(self):
        me = self.me
        self.over().wait_recv()
        self.add(self.at(0, me.pa, me.pb), (self.from_y, ...))
        self.last().start()
        self.out[me.core] = self.mine[
            (*self.lead, *self.at(0, me.pa, me.pb), me.core)
        ].astype(F32)

    def finish(self):
        self.last().wait_recv()
        self.out[1 - self.me.core] = self.from_core[...].astype(F32)
        self.last().wait_send()
        self.over().wait_send()

        def sent_sibling(at, carry):
            self.to_sibling(at).wait_send()
            return carry

        lax.fori_loop(0, 2 * RING * RING, sent_sibling, 0)

        def sent_a(slot, carry):
            self.send_a(0, slot, 0, 0, 0).wait_send()
            self.send_a(1, slot, 0, 0, 0).wait_send()
            return carry

        lax.fori_loop(0, 3 * RING, sent_a, 0)
        for slot in range(3):
            self.send_b(0, slot, 0, 0).wait_send()
            self.send_b(1, slot, 0, 0).wait_send()


def scatter_scratch(kinds, rows, width):
    blocks = 2 * RING * RING
    dma = pltpu.SemaphoreType.DMA
    return [
        pltpu.VMEM((*kinds, 2, RING, RING, 2, rows, width), BF),
        pltpu.VMEM((*kinds, 2, RING, RING, 2, rows, width), BF),
        pltpu.VMEM((2, 3 * RING, *kinds, 2, rows, width), BF),
        pltpu.VMEM((2, 3, *kinds, 2, rows, width), BF),
        pltpu.VMEM((*kinds, 2, rows, width), BF),
        pltpu.VMEM((*kinds, rows, width), BF),
        dma,
        dma((blocks,)),
        dma((blocks,)),
        dma((2, 3 * RING)),
        dma((2, 3 * RING)),
        dma((2, 3)),
        dma((2, 3)),
        dma((4,)),
    ]


def scatter_kernel(pm_ref, pf_ref, om_ref, of_ref, *refs):
    me = Place()
    mixer = Scattering(me, pm_ref, om_ref, refs[:14], ())
    feed = Scattering(me, pf_ref, of_ref, refs[14:], EVERY)
    me.greet()
    feed.begin()
    mixer.begin()
    feed.load().wait()
    mixer.load().wait()
    feed.opposite()
    feed.direct()
    feed.onward()
    feed.kept()
    mixer.opposite()
    mixer.direct()
    feed.ring_b()
    mixer.onward()
    mixer.kept()
    feed.across_y()
    mixer.ring_b()
    feed.across_cores()
    mixer.across_y()
    mixer.across_cores()
    feed.finish()
    mixer.finish()


def scatter(mixer, feed):
    halves, total, width = mixer.shape
    kinds = feed.shape[1]
    rows = total // (4 * RING * RING)
    whole = (2, RING, RING, 2, rows, width)
    return pl.pallas_call(
        scatter_kernel,
        out_shape=(
            jax.ShapeDtypeStruct((halves, rows, width), F32),
            jax.ShapeDtypeStruct((halves, kinds, rows, width), F32),
        ),
        in_specs=[pl.BlockSpec(memory_space=pl.ANY)] * 2,
        out_specs=[pl.BlockSpec(memory_space=pltpu.VMEM)] * 2,
        scratch_shapes=scatter_scratch((), rows, width) + scatter_scratch((kinds,), rows, width),
        compiler_params=pltpu.CompilerParams(
            collective_id=1, has_side_effects=True, vmem_limit_bytes=48 * 1024 * 1024
        ),
        cost_estimate=pl.CostEstimate(flops=0, bytes_accessed=200_000_000, transcendentals=0),
        name="scatter_gradients",
    )(mixer.reshape(halves, *whole), feed.reshape(halves, kinds, *whole))


def feed_kernel(n_ref, c_ref, w_ref, t_ref, out_ref, back_ref, n_turned, c_turned, out_sum, back_sum):
    step = pl.program_id(0)

    @pl.when(step == 0)
    def _():
        n_turned[...] = n_ref[...].T
        c_turned[...] = c_ref[...].T
        out_sum[...] = jnp.zeros_like(out_sum)
        back_sum[...] = jnp.zeros_like(back_sum)

    def weight(kind):
        return jnp.concatenate([w_ref[0, kind], w_ref[1, kind]], axis=1)

    def keep(kind, term):
        term = term.astype(BF)
        lanes = term.shape[1] // 2
        t_ref[0, kind] = term[:, :lanes]
        t_ref[1, kind] = term[:, lanes:]

    w_gate, w_up, w_down = weight(0), weight(1), weight(2)
    normed = n_ref[...]
    back_out = c_ref[...]
    gate = dot(normed, w_gate, ((1,), (0,)))
    up = dot(normed, w_up, ((1,), (0,)))
    back_hidden = dot(back_out, w_down, ((1,), (0,)))
    sig = jax.nn.sigmoid(gate)
    act = gate * sig
    hidden = (act * up).astype(BF)
    back_gate = (back_hidden * up * sig * (1.0 + gate * (1.0 - sig))).astype(BF)
    back_up = (back_hidden * act).astype(BF)
    out_sum[...] += dot(hidden, w_down, ((1,), (1,)))
    back_sum[...] += dot(back_gate, w_gate, ((1,), (1,))) + dot(back_up, w_up, ((1,), (1,)))
    keep(0, dot(n_turned[...], back_gate, ((1,), (0,))))
    keep(1, dot(n_turned[...], back_up, ((1,), (0,))))
    keep(2, dot(c_turned[...], hidden, ((1,), (0,))))

    @pl.when(step == pl.num_programs(0) - 1)
    def _():
        out_ref[...] = out_sum[...].astype(BF)
        back_ref[...] = back_sum[...].astype(BF)


def feed_forward(normed, cotangent, weights):
    halves, kinds, total, width = weights.shape
    tokens = normed.shape[0]
    lanes = 128
    whole = pl.BlockSpec((tokens, total), lambda j: (0, 0))
    part = pl.BlockSpec((halves, kinds, total, lanes), lambda j: (0, 0, 0, j))
    flops = 9 * 2 * tokens * total * halves * width
    return pl.pallas_call(
        feed_kernel,
        grid=(width // lanes,),
        out_shape=(
            jax.ShapeDtypeStruct(weights.shape, BF),
            jax.ShapeDtypeStruct((tokens, total), BF),
            jax.ShapeDtypeStruct((tokens, total), BF),
        ),
        in_specs=[whole, whole, part],
        out_specs=[part, whole, whole],
        scratch_shapes=[
            pltpu.VMEM((total, tokens), BF),
            pltpu.VMEM((total, tokens), BF),
            pltpu.VMEM((tokens, total), F32),
            pltpu.VMEM((tokens, total), F32),
        ],
        compiler_params=pltpu.CompilerParams(vmem_limit_bytes=48 * 1024 * 1024),
        cost_estimate=pl.CostEstimate(
            flops=flops, bytes_accessed=4 * halves * kinds * total * width, transcendentals=0
        ),
        name="feed_forward",
    )(normed, cotangent, weights)


def shifted(block, axis, distance):
    devices = range(lax.axis_size(axis))
    route = [(i - distance, i) for i in devices if i - distance in devices]
    return lax.ppermute(block, axis, route)


def swapped(block):
    return lax.ppermute(block, "chan", [(0, 1), (1, 0)])


def low(x):
    return lax.reduce_precision(x, 8, 7)


def both_sum(part):
    rounded = low(part)
    return rounded + swapped(rounded.astype(BF)).astype(F32)


def dot(a, b, dims):
    return lax.dot_general(a, b, (dims, ((), ())), preferred_element_type=F32)


def norm_back(values, inverse, gain, back):
    scaled = back * gain
    mean = jnp.mean(scaled * values, axis=-1, keepdims=True)
    return inverse * (scaled - values * (inverse * inverse) * mean)


def adam_update(weight, moment_one, second, gradient, step_rate, weight_decay):
    first_new = beta_one * moment_one + (1.0 - beta_one) * gradient
    second_new = beta_two * second + (1.0 - beta_two) * gradient * gradient
    first_hat = first_new / (1.0 - beta_one**STEP)
    second_hat = second_new / (1.0 - beta_two**STEP)
    weight_new = weight - step_rate * (
        first_hat / (jnp.sqrt(second_hat) + adam_eps) + weight_decay * weight
    )
    return (weight_new, first_new, second_new)


def body(
    tokens,
    cotangent,
    w_in,
    w_in_m,
    w_in_v,
    w_out,
    w_out_m,
    w_out_v,
    w_gu,
    w_gu_m,
    w_gu_v,
    w_down,
    w_down_m,
    w_down_v,
    vectors,
    vectors_m,
    vectors_v,
):
    seq_count = lax.axis_size("seq")
    seq_index = lax.axis_index("seq")
    chan = lax.axis_index("chan")
    half_seq = seq_count // 2
    rows = w_in.shape[0]
    wide = w_in.shape[2]
    n_in = 3 * wide
    n_out = wide
    hid = w_down.shape[1]
    part = hid // 2
    n_vec = hid - n_in - n_out

    theirs = swapped(vectors)
    first = jnp.where(chan == 0, vectors, theirs)
    second = jnp.where(chan == 0, theirs, vectors)
    vec_rows = jnp.concatenate([first, second], axis=1).T
    vec_high = low(vec_rows)
    vec_low = vec_rows - vec_high
    vec_cols = jnp.pad(
        jnp.concatenate([vec_high, vec_low], axis=1).astype(BF), ((0, 0), (0, n_vec - 10))
    )
    mixer_rows = jnp.concatenate(
        [w_in.astype(BF).reshape(rows, n_in), w_out.astype(BF), vec_cols], axis=1
    )
    mixer_rows = jnp.stack([mixer_rows[:, :part], mixer_rows[:, part:]], axis=0)
    low_gu = w_gu.astype(BF)
    low_down = w_down.astype(BF)
    feed_rows = jnp.stack(
        [
            jnp.stack([low_gu[:, 0, at], low_gu[:, 1, at], low_down[:, at]], axis=0)
            for at in (slice(0, part), slice(part, hid))
        ],
        axis=0,
    )
    full_mixer, full_feed = gather(mixer_rows, feed_rows)
    cut = n_in - part
    full_in = jnp.concatenate([full_mixer[0], full_mixer[1, :, :cut]], axis=1)
    full_out = full_mixer[1, :, cut : cut + n_out]
    vec_all = full_mixer[1, :, cut + n_out : cut + n_out + 10].astype(F32)
    vec_all = (vec_all[:, :5] + vec_all[:, 5:]).T
    taps = lax.dynamic_slice_in_dim(vec_all[2:5], chan * wide, wide, 1)
    gain_one, gain_two = vec_all[0], vec_all[1]

    inputs = tokens.astype(F32)
    inverse_one = lax.rsqrt(jnp.mean(inputs * inputs, axis=-1, keepdims=True) + norm_eps)
    normed = (inputs * inverse_one * gain_one).astype(BF)
    mixed = dot(normed, full_in, ((1,), (0,)))
    gate_b = mixed[:, :wide]
    gate_c = mixed[:, wide : 2 * wide]
    values = mixed[:, 2 * wide :]
    gated = (gate_b * values).astype(BF)
    carried = shifted(gated[-2:], "seq", 1)
    carried = jnp.where(seq_index % half_seq == 0, jnp.zeros_like(carried), carried)
    extended = jnp.concatenate([carried, gated], axis=0).astype(F32)
    convolved = taps[0] * extended[:-2] + taps[1] * extended[1:-1] + taps[2] * extended[2:]
    inner = (gate_c * convolved).astype(BF)
    middle = inputs + both_sum(dot(inner, full_out, ((1,), (1,))))
    inverse_two = lax.rsqrt(jnp.mean(middle * middle, axis=-1, keepdims=True) + norm_eps)
    normed_two = (middle * inverse_two * gain_two).astype(BF)

    term_feed, feed_part, back_two_part = feed_forward(normed_two, cotangent, full_feed)
    back_two_theirs = swapped(back_two_part)
    back_normed_two = back_two_part.astype(F32) + back_two_theirs.astype(F32)
    feed_part, _ = lax.optimization_barrier((feed_part, back_two_theirs))
    block_out = middle + (feed_part.astype(F32) + swapped(feed_part).astype(F32))

    back_out = cotangent.astype(F32)
    back_middle = back_out + norm_back(middle, inverse_two, gain_two, back_normed_two)
    gain_two_grad = jnp.sum(back_two_part.astype(F32) * middle * inverse_two, axis=0)
    back_branch = back_middle.astype(BF)
    back_inner = dot(back_branch, full_out, ((1,), (0,)))
    back_gate_c = back_inner * convolved
    back_conv = (back_inner * gate_c).astype(BF)
    ahead = shifted(back_conv[:2], "seq", -1)
    ahead = jnp.where(seq_index % half_seq == half_seq - 1, jnp.zeros_like(ahead), ahead)
    back_extended = jnp.concatenate([back_conv, ahead], axis=0).astype(F32)
    back_gated = (
        taps[0] * back_extended[2:] + taps[1] * back_extended[1:-1] + taps[2] * back_extended[:-2]
    )
    back_conv_wide = back_conv.astype(F32)
    tap_grads = jnp.stack(
        [
            jnp.sum(back_conv_wide * extended[:-2], axis=0),
            jnp.sum(back_conv_wide * extended[1:-1], axis=0),
            jnp.sum(back_conv_wide * extended[2:], axis=0),
        ],
        axis=0,
    )
    back_mixed = jnp.concatenate(
        [
            (back_gated * values).astype(BF),
            back_gate_c.astype(BF),
            (back_gated * gate_b).astype(BF),
        ],
        axis=1,
    )
    back_one_part = low(dot(back_mixed, full_in, ((1,), (1,))))
    back_normed = back_one_part + swapped(back_one_part.astype(BF)).astype(F32)
    input_grad = back_middle + norm_back(inputs, inverse_one, gain_one, back_normed)
    gain_one_grad = jnp.sum(back_one_part * inputs * inverse_one, axis=0)
    term_in = dot(normed, back_mixed, ((0,), (0,))).astype(BF)
    term_out = dot(back_branch, inner, ((0,), (0,))).astype(BF)

    width = inputs.shape[1]
    tap_rows = lax.dynamic_update_slice_in_dim(
        jnp.zeros((3, width), F32), tap_grads, chan * wide, 1
    )
    vec_grad = jnp.concatenate([gain_one_grad[None], gain_two_grad[None], tap_rows], axis=0)
    vec_term = jnp.pad(vec_grad.T.astype(BF), ((0, 0), (0, n_vec - 5)))
    term_mixer = jnp.stack(
        [term_in[:, :part], jnp.concatenate([term_in[:, part:], term_out, vec_term], axis=1)],
        axis=0,
    )
    sum_mixer, sum_feed = scatter(term_mixer, term_feed)
    grad_in = jnp.concatenate([sum_mixer[0], sum_mixer[1, :, :cut]], axis=1).reshape(w_in.shape)
    grad_out = sum_mixer[1, :, cut : cut + n_out]
    both = jnp.concatenate([sum_feed[0], sum_feed[1]], axis=2)
    grad_gu = jnp.stack([both[0], both[1]], axis=1)
    grad_down = both[2]
    sum_vec = sum_mixer[1, :, cut + n_out : cut + n_out + 5].T
    sum_vec = sum_vec + swapped(sum_vec)
    grad_vectors = lax.dynamic_slice_in_dim(sum_vec, chan * (rows // 2), rows // 2, 1)
    in_new = adam_update(w_in, w_in_m, w_in_v, grad_in, rate_matrix, decay_matrix)
    out_new = adam_update(w_out, w_out_m, w_out_v, grad_out, rate_matrix, decay_matrix)
    gu_new = adam_update(w_gu, w_gu_m, w_gu_v, grad_gu, rate_matrix, decay_matrix)
    down_new = adam_update(w_down, w_down_m, w_down_v, grad_down, rate_matrix, decay_matrix)
    vec_new = adam_update(vectors, vectors_m, vectors_v, grad_vectors, rate_vector, 0.0)
    return (block_out, input_grad, *in_new, *out_new, *gu_new, *down_new, *vec_new)


def solution(mesh):
    matrices = [P("seq", None, "chan")] * 3 + [P("seq", "chan")] * 3
    weights = (*matrices, *matrices, *[P(None, ("seq", "chan"))] * 3)
    return jax.shard_map(
        body,
        mesh=mesh,
        in_specs=(P("seq", None), P("seq", None), *weights),
        out_specs=(P("seq", None), P("seq", None), *weights),
        check_vma=False,
    )
```

time: 945 us -> 302 us (0.32)
  blocking collectives: 386 us -> 0 us
  waiting for transfers between devices: 297 us -> 65.4 us
  Pallas kernels: 0 us -> 157 us
  local copies, waits for them, and re-layouts: 83.2 us -> 20.5 us
  matrix products: 64.6 us -> 13.7 us
  other arithmetic: 63.2 us -> 23.8 us
  between operations: 15.2 us -> 1.26 us
    all_gather x1 -> x0, blocking collectives: 319 us -> none  [body(): all_vectors = lax.all_gather(vectors, ('seq', 'chan'), axis=1, tiled=True)]
    reduce_scatter x1 -> x0, waiting for transfers between devices: 231 us -> none  [sent_together(): out = lax.psum_scatter(both, axis, scatter_dimension=dim, tiled=True)]
    pallas_call x0 -> x3, Pallas kernels: none -> 157 us  [the longest x1 67.4 us: scatter(): pl.pallas_call(scatter_kernel, out_shape=(jax.ShapeDtypeStruct((halves, r...]
    unnamed x1 -> x0, blocking collectives: 67.5 us -> none
    ppermute x0 -> x6, waiting for transfers between devices: none -> 63.7 us  [swapped(): return lax.ppermute(block, 'chan', [(0, 1), (1, 0)])]
    all_to_all x4 -> x0, waiting for transfers between devices: 62.4 us -> none  [copy_for_each(): lax.all_to_all(jnp.broadcast_to(x[None], (peers, *x.shape)), axis, 0, 0,...]
    unnamed x125 -> x66, local copies, waits for them, and re-layouts: 59.5 us -> 6.06 us
    dot_general x12 -> x6, matrix products: 64.6 us -> 13.7 us  [dot(): return lax.dot_general(a, b, (dims, ((), ())), preferred_element_type=F32)]
where the time goes in v2:
time: 302 us; the launch traced here: 299 us
  Pallas kernels  157 us (52%)
  waiting for transfers between devices  65.4 us (22%)
  other arithmetic  23.8 us (8%)
  local copies, waits for them, and re-layouts  20.5 us (7%)
  starting transfers between devices  17.6 us (6%)
  matrix products  13.7 us (5%)
    pallas_call x1, Pallas kernels, scatter(): pl.pallas_call(scatter_kernel, out_shape=(jax.ShapeDtypeStruct((halves, r...  67.4 us
    pallas_call x1, Pallas kernels, gather(): pl.pallas_call(gather_kernel, out_shape=(jax.ShapeDtypeStruct((halves, *w...  65.6 us
    ppermute x6, waiting for transfers between devices, swapped(): return lax.ppermute(block, 'chan', [(0, 1), (1, 0)])  63.7 us
    pallas_call x1, Pallas kernels, feed_forward(): pl.pallas_call(feed_kernel, grid=(width // lanes,), out_shape=(jax.ShapeD...  24.1 us
    dot_general x6, matrix products, dot(): return lax.dot_general(a, b, (dims, ((), ())), preferred_element_type=F32)  13.7 us
    ppermute x6, starting transfers between devices, swapped(): return lax.ppermute(block, 'chan', [(0, 1), (1, 0)])  10.7 us
    ppermute x2, starting transfers between devices, shifted(): return lax.ppermute(block, axis, route)  6.83 us
    unnamed x66, local copies, waits for them, and re-layouts  6.06 us
  transfers between devices with their start and end apart: 8, of which 6 were waited for; matrix products, arithmetic and copies ran while one was open for 7% of the time, Pallas kernels for 0%

profile of v2, /device:TPU:1, one launch (start us, length us, event | category | flops | bytes accessed | tf_op | source)
XLA Modules:
  0.0 299.3 jit_solution(12695525983963040786)
XLA Ops:
  1.5 3.7 %collective-permute-start = (f32[5,8]{0,1:T(8,128)S(1)}, f32[5,8]{0,1:T(8,128)S(1)}, u32[]{:S(2)}, u32[]{:S(2)}) collective-permute-start(f32[5,8]{0,1:T(8,128)S(1)} %copy.77), channel_id=1, source_target_pairs={{0,1},{1,0},{2,3},{3,2},{4,5},{5,4},{6,7},{7,6},{8,9},{9,8},{10,11... | collective-permute-start | bytes 488 | tf_op jit(solution)/shard_map/ppermute | solution.py:654
  10.6 65.6 %gather_weights.1 = (bf16[2,2,4,4,2,16,1152]{6,5,4,3,2,1,0:T(8,128)(2,1)}, bf16[2,3,2,4,4,2,16,1152]{7,6,5,4,3,2,1,0:T(8,128)(2,1)}) custom-call(bf16[2,16,1152]{2,1,0:T(8,128)(2,1)} %pad_maximum_fusion.13.wm_ref, bf16[2,3,16,1152]{3,2,1,0:T(8,128)(2,1)} %pad_maximum_fusion.10.wf_ref), custom_call_target="tpu_custom_call" | custom-call | tf_op jit(solution)/shard_map/gather_weights/pallas_call | solution.py:257
  77.2 2.1 slice_bitcast_fusion.3
  79.3 1.9 slice.145
  81.4 3.2 %fusion.3 = f32[384,1536]{1,0:T(8,128)S(1)} fusion(bf16[1024,384]{1,0:T(8,128)(2,1)} %slice_bitcast_fusion.3, bf16[1024,1152]{1,0:T(8,128)(2,1)S(1)} %bitcast.108, bf16[384,1024]{1,0:T(8,128)(2,1)S(1)} %copy-done.1, f32[1024]{0:T(1024)S(1)} %bitcast.115, f32[384]{0:T(512)S(1)} %get-tuple-element.138), kind=kOutput, calls=%fused_computation.13 | convolution fusion | flops 1215823872 | bytes 6297088 | tf_op jit(solution)/shard_map/dot_general | solution.py:667
  84.7 1.9 collective-permute-start.1
  88.2 2.0 fusion.62
  91.8 18.9 %collective-permute-done.2 = bf16[384,1024]{1,0:T(8,128)(2,1)S(1)} collective-permute-done((bf16[384,1024]{1,0:T(8,128)(2,1)S(1)}, bf16[384,1024]{1,0:T(8,128)(2,1)S(1)}, u32[]{:S(2)}, u32[]{:S(2)}) %collective-permute-start.2) | collective-permute-done | bytes 786464 | tf_op jit(solution)/shard_map/ppermute | solution.py:654
  112.3 24.1 %feed_forward.1 = (bf16[2,3,1024,1152]{3,2,1,0:T(8,128)(2,1)}, bf16[384,1024]{1,0:T(8,128)(2,1)S(1)}, bf16[384,1024]{1,0:T(8,128)(2,1)S(1)}) custom-call(bf16[384,1024]{1,0:T(8,128)(2,1)S(1)} %multiply_convert_fusion.n_ref, bf16[384,1024]{1,0:T(8,128)(2,1)S(1)} %copy-done, bf16[2,3,1024,1152]{3,2,1,0:T(8,128)(2,1)} %bitcast.129), custom_call_target="tpu_custom_call" | custom-call | flops 16307453952 | bytes 28311552 | tf_op jit(solution)/shard_map/feed_forward/pallas_call | solution.py:623
  138.0 18.0 %collective-permute-done.3 = bf16[384,1024]{1,0:T(8,128)(2,1)S(1)} collective-permute-done((bf16[384,1024]{1,0:T(8,128)(2,1)S(1)}, bf16[384,1024]{1,0:T(8,128)(2,1)S(1)}, u32[]{:S(2)}, u32[]{:S(2)}) %collective-permute-start.3) | collective-permute-done | bytes 786464 | tf_op jit(solution)/shard_map/ppermute | solution.py:654
  158.1 16.5 %collective-permute-done.4 = bf16[384,1024]{1,0:T(8,128)(2,1)S(1)} collective-permute-done((bf16[384,1024]{1,0:T(8,128)(2,1)S(1)}, bf16[384,1024]{1,0:T(8,128)(2,1)S(1)}, u32[]{:S(2)}, u32[]{:S(2)}) %collective-permute-start.4) | collective-permute-done | bytes 786464 | tf_op jit(solution)/shard_map/ppermute | solution.py:654
  174.6 1.8 multiply_add_fusion
  176.4 2.0 fusion.19
  178.4 4.9 %collective-permute-start.5 = (bf16[2,512]{1,0:T(2,128)(2,1)S(1)}, bf16[2,512]{1,0:T(2,128)(2,1)S(1)}, u32[]{:S(2)}, u32[]{:S(2)}) collective-permute-start(bf16[2,512]{1,0:T(2,128)(2,1)S(1)} %slice.197), channel_id=1, source_target_pairs={{2,0},{4,2},{6,4},{8,6},{10,8},{12,10},{14,12},{16,14},{18,16},{20... | collective-permute-start | bytes 6152 | tf_op jit(solution)/shard_map/ppermute | solution.py:650
  187.3 2.8 fusion.63
  191.7 1.8 convolution_convert_fusion.1
  193.6 1.9 convolution_convert_fusion
  198.1 2.3 copy.81
  200.4 10.3 %collective-permute-done.6 = bf16[384,1024]{1,0:T(8,128)(2,1)} collective-permute-done((bf16[384,1024]{1,0:T(8,128)(2,1)}, bf16[384,1024]{1,0:T(8,128)(2,1)}, u32[]{:S(2)}, u32[]{:S(2)}) %collective-permute-start.6) | collective-permute-done | bytes 786464 | tf_op jit(solution)/shard_map/ppermute | solution.py:654
  210.7 2.3 fusion.16
  214.7 4.3 %copy.82 = bf16[1024,1152]{1,0:T(8,128)(2,1)} copy(bf16[1024,1152]{0,1:T(8,128)(2,1)} %fusion.1) | data formatting | bytes 4718592 | tf_op jit(solution)/shard_map/concatenate | solution.py:816
  219.0 2.8 pad_maximum_fusion.pm_ref
  221.9 67.4 %scatter_gradients.1 = (f32[2,16,1152]{2,1,0:T(8,128)S(1)}, f32[2,3,16,1152]{3,2,1,0:T(8,128)S(1)}) custom-call(bf16[2,2,4,4,2,16,1152]{6,5,4,3,2,1,0:T(8,128)(2,1)S(1)} %pad_maximum_fusion.pm_ref, bf16[2,3,2,4,4,2,16,1152]{7,6,5,4,3,2,1,0:T(8,128)(2,1)} %bitcast.101), custom_call_target="tpu_custom_call" | custom-call | bytes 200000000 | tf_op jit(solution)/shard_map/scatter_gradients/pallas_call | solution.py:557
  292.9 2.8 fusion.13
  (133 shorter events, 32.6 us)
Async XLA Ops:
  0.7 8.2 %copy-start.1 = (bf16[384,1024]{1,0:T(8,128)(2,1)S(1)}, bf16[384,1024]{1,0:T(8,128)(2,1)}, u32[]{:S(2)}) copy-start(bf16[384,1024]{1,0:T(8,128)(2,1)} %param.17) | copy-start | bytes 2359300
  1.5 8.4 %collective-permute-start = (f32[5,8]{0,1:T(8,128)S(1)}, f32[5,8]{0,1:T(8,128)S(1)}, u32[]{:S(2)}, u32[]{:S(2)}) collective-permute-start(f32[5,8]{0,1:T(8,128)S(1)} %copy.77), channel_id=1, source_target_pairs={{0,1},{1,0},{2,3},{3,2},{4,5},{5,4},{6,7},{7,6},{8,9},{9,8},{10,11... | collective-permute-start | bytes 488 | tf_op jit(solution)/shard_map/ppermute | solution.py:654
  81.2 3.4 %copy-start.6 = (bf16[1,2,4,4,2,16,1152]{6,5,4,3,2,1,0:T(8,128)(2,1)}, bf16[1,2,4,4,2,16,1152]{6,5,4,3,2,1,0:T(8,128)(2,1)S(1)}, u32[]{:S(2)}) copy-start(bf16[1,2,4,4,2,16,1152]{6,5,4,3,2,1,0:T(8,128)(2,1)S(1)} %slice.145) | copy-start | bytes 7077892
  84.6 91.8 %copy-start.2 = (f32[384,1536]{1,0:T(8,128)}, f32[384,1536]{1,0:T(8,128)S(1)}, u32[]{:S(2)}) copy-start(f32[384,1536]{1,0:T(8,128)S(1)} %fusion.3) | copy-start | bytes 7077892
  84.7 3.1 %collective-permute-start.1 = (bf16[2,512]{1,0:T(2,128)(2,1)S(1)}, bf16[2,512]{1,0:T(2,128)(2,1)S(1)}, u32[]{:S(2)}, u32[]{:S(2)}) collective-permute-start(bf16[2,512]{1,0:T(2,128)(2,1)S(1)} %slice.191), channel_id=1, source_target_pairs={{0,2},{2,4},{4,6},{6,8},{8,10},{10,12},{12,14},{14,16},{16,18},{18... | collective-permute-start | bytes 6152 | tf_op jit(solution)/shard_map/ppermute | solution.py:650
  88.2 2.0 copy-start.4
  90.2 20.6 %collective-permute-start.2 = (bf16[384,1024]{1,0:T(8,128)(2,1)S(1)}, bf16[384,1024]{1,0:T(8,128)(2,1)S(1)}, u32[]{:S(2)}, u32[]{:S(2)}) collective-permute-start(bf16[384,1024]{1,0:T(8,128)(2,1)S(1)} %get-tuple-element.141), channel_id=1, source_target_pairs={{0,1},{1,0},{2,3},{3,2},{4,5},{5,4},{6,7},{7,6},{8,9},{9,8},{10,11... | collective-permute-start | bytes 2359304 | tf_op jit(solution)/shard_map/ppermute | solution.py:654
  136.4 19.6 %collective-permute-start.3 = (bf16[384,1024]{1,0:T(8,128)(2,1)S(1)}, bf16[384,1024]{1,0:T(8,128)(2,1)S(1)}, u32[]{:S(2)}, u32[]{:S(2)}) collective-permute-start(bf16[384,1024]{1,0:T(8,128)(2,1)S(1)} %get-tuple-element.28), channel_id=1, source_target_pairs={{0,1},{1,0},{2,3},{3,2},{4,5},{5,4},{6,7},{7,6},{8,9},{9,8},{10,11... | collective-permute-start | bytes 2359304 | tf_op jit(solution)/shard_map/ppermute | solution.py:654
  156.0 18.6 %collective-permute-start.4 = (bf16[384,1024]{1,0:T(8,128)(2,1)S(1)}, bf16[384,1024]{1,0:T(8,128)(2,1)S(1)}, u32[]{:S(2)}, u32[]{:S(2)}) collective-permute-start(bf16[384,1024]{1,0:T(8,128)(2,1)S(1)} %get-tuple-element.29), channel_id=1, source_target_pairs={{0,1},{1,0},{2,3},{3,2},{4,5},{5,4},{6,7},{7,6},{8,9},{9,8},{10,11... | collective-permute-start | bytes 2359304 | tf_op jit(solution)/shard_map/ppermute | solution.py:654
  178.4 8.7 %copy-start.11 = (bf16[384,512]{1,0:T(8,128)(2,1)}, bf16[384,512]{1,0:T(8,128)(2,1)S(1)}, u32[]{:S(2)}) copy-start(bf16[384,512]{1,0:T(8,128)(2,1)S(1)} %get-tuple-element.115) | copy-start | bytes 1179652
  178.4 5.5 %collective-permute-start.5 = (bf16[2,512]{1,0:T(2,128)(2,1)S(1)}, bf16[2,512]{1,0:T(2,128)(2,1)S(1)}, u32[]{:S(2)}, u32[]{:S(2)}) collective-permute-start(bf16[2,512]{1,0:T(2,128)(2,1)S(1)} %slice.197), channel_id=1, source_target_pairs={{2,0},{4,2},{6,4},{8,6},{10,8},{12,10},{14,12},{16,14},{18,16},{20... | collective-permute-start | bytes 6152 | tf_op jit(solution)/shard_map/ppermute | solution.py:650
  184.1 3.0 %copy-start.7 = (bf16[1,2,4,4,2,16,1152]{6,5,4,3,2,1,0:T(8,128)(2,1)S(1)}, bf16[1,2,4,4,2,16,1152]{6,5,4,3,2,1,0:T(8,128)(2,1)}, u32[]{:S(2)}) copy-start(bf16[1,2,4,4,2,16,1152]{6,5,4,3,2,1,0:T(8,128)(2,1)} %copy-done.6) | copy-start | bytes 7077892
  185.7 4.4 %copy-start.13 = (bf16[384,512]{1,0:T(8,128)(2,1)}, bf16[384,512]{1,0:T(8,128)(2,1)S(1)}, u32[]{:S(2)}) copy-start(bf16[384,512]{1,0:T(8,128)(2,1)S(1)} %get-tuple-element.107) | copy-start | bytes 1179652
  187.1 3.0 copy-start.16
  190.1 20.6 %collective-permute-start.6 = (bf16[384,1024]{1,0:T(8,128)(2,1)}, bf16[384,1024]{1,0:T(8,128)(2,1)}, u32[]{:S(2)}, u32[]{:S(2)}) collective-permute-start(bf16[384,1024]{1,0:T(8,128)(2,1)} %get-tuple-element.143), channel_id=1, source_target_pairs={{0,1},{1,0},{2,3},{3,2},{4,5},{5,4},{6,7},{7,6},{8,9},{9,8},{10,11... | collective-permute-start | bytes 2359304 | tf_op jit(solution)/shard_map/ppermute | solution.py:654
  191.7 1.9 copy-start.17
  210.7 2.3 copy-start.5
  289.4 9.1 %collective-permute-start.7 = (f32[5,16]{1,0:T(8,128)S(1)}, f32[5,16]{1,0:T(8,128)S(1)}, u32[]{:S(2)}, u32[]{:S(2)}) collective-permute-start(f32[5,16]{1,0:T(8,128)S(1)} %bitcast.125), channel_id=1, source_target_pairs={{0,1},{1,0},{2,3},{3,2},{4,5},{5,4},{6,7},{7,6},{8,9},{9,8},{10,11... | collective-permute-start | bytes 968 | tf_op jit(solution)/shard_map/ppermute | solution.py:654
  290.2 2.5 copy-start.8
  290.2 2.5 copy-start.18
  290.2 2.5 copy-start.19
  295.7 2.8 copy-start.27
  295.7 2.8 copy-start.28
  295.7 2.9 copy-start.29
  (14 other events, 19.9 us)

commit v3 on v2

--- a/solution.py
+++ b/solution.py
@@ -52,11 +52,22 @@
         zi = b + self.core * (a - b)
         return self.row(rr), xi, zi
 
-    def greet(self):
+    def peers(self):
+        near = (self.sibling, self.other_y, self.on_a(1), self.on_a(3), self.on_b(1), self.on_b(3))
+        return [{"seq": peer} for peer in near]
+
+    def along(self):
+        count = lax.axis_size("seq")
+        return {"seq": (self.s + 1) % count}, {"seq": (self.s + count - 1) % count}
+
+    def pair(self):
+        return {"chan": 1 - lax.axis_index("chan")}
+
+    def greet(self, more=()):
         barrier = pltpu.get_barrier_semaphore()
-        peers = (self.sibling, self.other_y, self.on_a(1), self.on_a(3), self.on_b(1), self.on_b(3))
+        peers = [*self.peers(), *more]
         for peer in peers:
-            pl.semaphore_signal(barrier, inc=1, device_id={"seq": peer}, device_id_type=MESH)
+            pl.semaphore_signal(barrier, inc=1, device_id=peer, device_id_type=MESH)
         pl.semaphore_wait(barrier, len(peers))
 
 
@@ -66,7 +77,7 @@
         dst_ref=dst,
         send_sem=send_sem,
         recv_sem=recv_sem,
-        device_id={"seq": target},
+        device_id=target if isinstance(target, dict) else {"seq": target},
         device_id_type=MESH,
     )
 
@@ -271,8 +282,12 @@
 
 
 class Scattering:
-    def __init__(self, me, partial, out, refs, lead):
+    def __init__(self, me, partial, out, refs, lead, in_place=False):
         self.me, self.partial, self.out, self.lead = me, partial, out, lead
+        self.in_place = in_place
+        self.head = (me.core, *lead) if in_place else lead
+        if in_place:
+            refs = (partial, *refs[:5], None, *refs[5:])
         (
             self.mine,
             self.sib,
@@ -294,7 +309,7 @@
         return self.me.spot(rr, a % RING, b % RING)
 
     def add(self, where, *others):
-        index = (*self.lead, *where)
+        index = (*self.head, *where)
         total = self.mine[index].astype(F32)
         for ref, i in others:
             total = total + ref[i].astype(F32)
@@ -324,7 +339,8 @@
         )
 
     def begin(self):
-        self.load().start()
+        if not self.in_place:
+            self.load().start()
 
         def step(at, carry):
             self.to_sibling(at).start()
@@ -340,7 +356,7 @@
 
     def send_a(self, side, slot, rr, a, b):
         return remote(
-            self.mine.at[(*self.lead, *self.at(rr, a, b))],
+            self.mine.at[(*self.head, *self.at(rr, a, b))],
             self.from_a.at[side, slot],
             self.a_send.at[side, slot],
             self.a_recv.at[side, slot],
@@ -411,7 +427,7 @@
 
     def send_b(self, side, slot, rr, b):
         return remote(
-            self.mine.at[(*self.lead, *self.at(rr, self.me.pa, b))],
+            self.mine.at[(*self.head, *self.at(rr, self.me.pa, b))],
             self.from_b.at[side, slot],
             self.b_send.at[side, slot],
             self.b_recv.at[side, slot],
@@ -444,7 +460,7 @@
     def over(self):
         me = self.me
         return remote(
-            self.mine.at[(*self.lead, *self.at(1, me.pa, me.pb))],
+            self.mine.at[(*self.head, *self.at(1, me.pa, me.pb))],
             self.from_y,
             self.last_sem.at[0],
             self.last_sem.at[1],
@@ -454,7 +470,7 @@
     def last(self):
         me = self.me
         return remote(
-            self.mine.at[(*self.lead, *self.at(0, me.pa, me.pb), 1 - me.core)],
+            self.mine.at[(*self.head, *self.at(0, me.pa, me.pb), 1 - me.core)],
             self.from_core,
             self.last_sem.at[2],
             self.last_sem.at[3],
@@ -475,7 +491,7 @@
         self.add(self.at(0, me.pa, me.pb), (self.from_y, ...))
         self.last().start()
         self.out[me.core] = self.mine[
-            (*self.lead, *self.at(0, me.pa, me.pb), me.core)
+            (*self.head, *self.at(0, me.pa, me.pb), me.core)
         ].astype(F32)
 
     def finish(self):
@@ -501,17 +517,18 @@
             self.send_b(1, slot, 0, 0).wait_send()
 
 
-def scatter_scratch(kinds, rows, width):
+def scatter_scratch(kinds, rows, width, in_place=False):
     blocks = 2 * RING * RING
     dma = pltpu.SemaphoreType.DMA
+    mine = [] if in_place else [pltpu.VMEM((*kinds, 2, RING, RING, 2, rows, width), BF)]
     return [
-        pltpu.VMEM((*kinds, 2, RING, RING, 2, rows, width), BF),
+        *mine,
         pltpu.VMEM((*kinds, 2, RING, RING, 2, rows, width), BF),
         pltpu.VMEM((2, 3 * RING, *kinds, 2, rows, width), BF),
         pltpu.VMEM((2, 3, *kinds, 2, rows, width), BF),
         pltpu.VMEM((*kinds, 2, rows, width), BF),
         pltpu.VMEM((*kinds, rows, width), BF),
-        dma,
+        *([] if in_place else [dma]),
         dma((blocks,)),
         dma((blocks,)),
         dma((2, 3 * RING)),
@@ -522,53 +539,310 @@
     ]
 
 
-def scatter_kernel(pm_ref, pf_ref, om_ref, of_ref, *refs):
+def rows_of(count, step):
+    return [slice(i, i + step) for i in range(0, count, step)]
+
+
+def mean_square(values):
+    return jnp.mean(values * values, axis=-1, keepdims=True)
+
+
+ROWS = 32
+HALO = 16
+
+
+def backward_kernel(
+    pf_ref,
+    back_hbm,
+    feed_hbm,
+    middle_hbm,
+    cot_hbm,
+    tokens_hbm,
+    mixed_hbm,
+    gated_hbm,
+    weights_hbm,
+    vec_hbm,
+    om_ref,
+    of_ref,
+    block_ref,
+    grad_ref,
+    *refs,
+):
+    (
+        back_own,
+        feed_own,
+        middle,
+        cot,
+        tokens,
+        mixed,
+        gated,
+        weights,
+        vec,
+        back_theirs,
+        feed_theirs,
+        one_theirs,
+        branch,
+        turned,
+        inner,
+        wide_gated,
+        wide_conv,
+        back_inner,
+        back_mixed,
+        sums,
+        halo_out,
+        halo_in,
+        pm_ref,
+        loads,
+        pairs,
+        halo_sem,
+    ) = refs[:26]
     me = Place()
-    mixer = Scattering(me, pm_ref, om_ref, refs[:14], ())
-    feed = Scattering(me, pf_ref, of_ref, refs[14:], EVERY)
-    me.greet()
+    pair = me.pair()
+    ahead_of, behind = me.along()
+    chan = lax.axis_index("chan")
+    mixer = Scattering(me, pm_ref, om_ref, refs[26:38], (), in_place=True)
+    feed = Scattering(me, pf_ref, of_ref, refs[38:], EVERY)
+    one_own, one_sum = cot, block_ref
+    count, width = middle.shape
+    wide = back_inner.shape[1]
+    part = weights.shape[2]
+
+    def load(i):
+        src, dst = (
+            (back_hbm, back_own),
+            (middle_hbm, middle),
+            (cot_hbm, cot),
+            (vec_hbm, vec),
+            (weights_hbm, weights),
+            (mixed_hbm, mixed),
+            (gated_hbm, gated),
+            (tokens_hbm, tokens),
+            (feed_hbm, feed_own),
+        )[i]
+        return pltpu.make_async_copy(src, dst, loads.at[i])
+
+    def exchange(i):
+        src, dst = ((back_own, back_theirs), (feed_own, feed_theirs), (one_own, one_theirs))[i]
+        return remote(src, dst, pairs.at[0, i], pairs.at[1, i], pair)
+
+    for i in range(9):
+        load(i).start()
+    me.greet((pair, ahead_of, behind))
+    load(0).wait()
+    exchange(0).start()
     feed.begin()
-    mixer.begin()
+    for i in range(1, 9):
+        load(i).wait()
     feed.load().wait()
-    mixer.load().wait()
     feed.opposite()
+
+    gain_one = vec[0:1, :]
+    gain_two = vec[1:2, :]
+    taps = [vec[2 + i : 3 + i, :wide] for i in range(3)]
+    sums[...] = jnp.zeros_like(sums)
+    wide_gated[...] = gated[...].astype(F32)
+
+    def convolved(at):
+        total = taps[0] * wide_gated[at.start + HALO - 2 : at.stop + HALO - 2, :]
+        total = total + taps[1] * wide_gated[at.start + HALO - 1 : at.stop + HALO - 1, :]
+        return total + taps[2] * wide_gated[at.start + HALO : at.stop + HALO, :]
+
+    for at in rows_of(count, ROWS):
+        inner[at, :] = (mixed[at, wide : 2 * wide] * convolved(at)).astype(BF)
     feed.direct()
     feed.onward()
+
+    exchange(0).wait_recv()
+    exchange(1).start()
+
+    def norm_step(i, carry):
+        at = pl.ds(pl.multiple_of(i * ROWS, ROWS), ROWS)
+        mid = middle[at, :]
+        inverse = lax.rsqrt(mean_square(mid) + norm_eps)
+        own = back_own[at, :].astype(F32)
+        back = own + back_theirs[at, :].astype(F32)
+        total = cot[at, :].astype(F32) + norm_back(mid, inverse, gain_two, back)
+        grad_ref[at, :] = total
+        branch[at, :] = total.astype(BF)
+        sums[1:2, :] += jnp.sum(own * mid * inverse, axis=0, keepdims=True)
+        return carry
+
+    lax.fori_loop(0, count // ROWS, norm_step, 0)
+    cut = 3 * wide - part
+    w_out = weights[1, :, cut : cut + wide]
+    back_inner[...] = dot(branch[...], w_out, ((1,), (0,)))
+    for at in rows_of(count, ROWS):
+        wide_conv[at, :] = (back_inner[at, :] * mixed[at, wide : 2 * wide]).astype(BF).astype(F32)
+    halo_out[...] = wide_conv[0:HALO, :].astype(BF)
+    halo = remote(halo_out, halo_in, halo_sem.at[0], halo_sem.at[1], behind)
+    halo.start()
+    turned[...] = branch[...].T
+    term_out = dot(turned[...], inner[...], ((1,), (0,))).astype(BF)
+    shape = pm_ref.shape[1:-1]
+    pm_ref[1, :, :, :, :, :, cut : cut + wide] = term_out.reshape(*shape, wide)
+    for at in rows_of(count, ROWS):
+        values = tokens[at, :].astype(F32)
+        inverse = lax.rsqrt(mean_square(values) + norm_eps)
+        branch[at, :] = (values * inverse * gain_one).astype(BF)
+    turned[...] = branch[...].T
     feed.kept()
+    halo.wait_recv()
+    last = me.s % (lax.axis_size("seq") // 2) == lax.axis_size("seq") // 2 - 1
+    wide_conv[count : count + HALO, :] = jnp.where(last, 0.0, halo_in[...].astype(F32))
+    tap_at = pl.ds(pl.multiple_of(chan * wide, wide), wide)
+    for at in rows_of(count, ROWS):
+        back_gated = (
+            taps[0] * wide_conv[at.start + 2 : at.stop + 2, :]
+            + taps[1] * wide_conv[at.start + 1 : at.stop + 1, :]
+            + taps[2] * wide_conv[at, :]
+        )
+        back_mixed[at, :wide] = (back_gated * mixed[at, 2 * wide :]).astype(BF)
+        back_mixed[at, wide : 2 * wide] = (back_inner[at, :] * convolved(at)).astype(BF)
+        back_mixed[at, 2 * wide :] = (back_gated * mixed[at, :wide]).astype(BF)
+        for i in range(3):
+            shift = HALO - 2 + i
+            term = wide_conv[at, :] * wide_gated[at.start + shift : at.stop + shift, :]
+            sums[2 + i : 3 + i, tap_at] += jnp.sum(term, axis=0, keepdims=True)
+
+    def in_tile(j):
+        lanes = part // 3
+        at = pl.ds(pl.multiple_of((j % 3) * lanes, 128), lanes)
+        return j // 3, at, pl.ds(pl.multiple_of(j * lanes, 128), lanes)
+
+    one_sum[...] = jnp.zeros_like(one_sum)
+
+    def back_step(j, carry):
+        half, at, lanes = in_tile(j)
+        one_sum[...] += dot(back_mixed[:, lanes], weights[half, :, at], ((1,), (1,)))
+        return carry
+
+    lax.fori_loop(0, 4, back_step, 0)
+
+    def gain_step(i, carry):
+        at = pl.ds(pl.multiple_of(i * ROWS, ROWS), ROWS)
+        values = tokens[at, :].astype(F32)
+        inverse = lax.rsqrt(mean_square(values) + norm_eps)
+        own = one_sum[at, :]
+        one_own[at, :] = own.astype(BF)
+        sums[0:1, :] += jnp.sum(own * values * inverse, axis=0, keepdims=True)
+        return carry
+
+    lax.fori_loop(0, count // ROWS, gain_step, 0)
+    exchange(2).start()
+
+    def term_step(j, carry):
+        half, at, lanes = in_tile(j)
+        term = dot(turned[...], back_mixed[:, lanes], ((1,), (0,))).astype(BF)
+        pm_ref[half, :, :, :, :, :, at] = term.reshape(*shape, part // 3)
+        return carry
+
+    lax.fori_loop(0, 4, term_step, 0)
+    vec_term = sums[...].T.astype(BF)
+    lanes = vec_term.shape[1]
+    pm_ref[1, :, :, :, :, :, cut + wide : cut + wide + lanes] = vec_term.reshape(*shape, lanes)
+    pm_ref[1, :, :, :, :, :, cut + wide + lanes :] = jnp.zeros(
+        (*shape, part - cut - wide - lanes), BF
+    )
+    mixer.begin()
+    feed.ring_b()
     mixer.opposite()
     mixer.direct()
-    feed.ring_b()
+    feed.across_y()
     mixer.onward()
     mixer.kept()
-    feed.across_y()
+    feed.across_cores()
+    exchange(1).wait_recv()
+
+    def out_step(i, carry):
+        at = pl.ds(pl.multiple_of(i * ROWS, ROWS), ROWS)
+        total = feed_own[at, :].astype(F32) + feed_theirs[at, :].astype(F32)
+        block_ref[at, :] = middle[at, :] + total
+        return carry
+
+    lax.fori_loop(0, count // ROWS, out_step, 0)
     mixer.ring_b()
-    feed.across_cores()
     mixer.across_y()
     mixer.across_cores()
+    exchange(2).wait_recv()
+
+    def grad_step(i, carry):
+        at = pl.ds(pl.multiple_of(i * ROWS, ROWS), ROWS)
+        values = tokens[at, :].astype(F32)
+        inverse = lax.rsqrt(mean_square(values) + norm_eps)
+        back = one_own[at, :].astype(F32) + one_theirs[at, :].astype(F32)
+        grad_ref[at, :] += norm_back(values, inverse, gain_one, back)
+        return carry
+
+    lax.fori_loop(0, count // ROWS, grad_step, 0)
     feed.finish()
     mixer.finish()
-
-
-def scatter(mixer, feed):
-    halves, total, width = mixer.shape
-    kinds = feed.shape[1]
+    halo.wait_send()
+    for i in range(3):
+        exchange(i).wait_send()
+
+
+def backward(term_feed, back_two, feed_part, middle, cotangent, tokens, mixed, gated, weights, vec):
+    halves, kinds, total, width = term_feed.shape
     rows = total // (4 * RING * RING)
     whole = (2, RING, RING, 2, rows, width)
+    count, features = middle.shape
+    wide = gated.shape[1]
+    dma = pltpu.SemaphoreType.DMA
+
+    def like(x):
+        return pltpu.VMEM(x.shape, x.dtype)
+
+    low_act = pltpu.VMEM((count, features), BF)
     return pl.pallas_call(
-        scatter_kernel,
+        backward_kernel,
         out_shape=(
             jax.ShapeDtypeStruct((halves, rows, width), F32),
             jax.ShapeDtypeStruct((halves, kinds, rows, width), F32),
+            jax.ShapeDtypeStruct((count, features), F32),
+            jax.ShapeDtypeStruct((count, features), F32),
         ),
-        in_specs=[pl.BlockSpec(memory_space=pl.ANY)] * 2,
-        out_specs=[pl.BlockSpec(memory_space=pltpu.VMEM)] * 2,
-        scratch_shapes=scatter_scratch((), rows, width) + scatter_scratch((kinds,), rows, width),
+        in_specs=[pl.BlockSpec(memory_space=pl.ANY)] * 10,
+        out_specs=[pl.BlockSpec(memory_space=pltpu.VMEM)] * 4,
+        scratch_shapes=[
+            *[like(x) for x in (back_two, feed_part, middle, cotangent, tokens, mixed, gated)],
+            like(weights),
+            like(vec),
+            low_act,
+            low_act,
+            low_act,
+            low_act,
+            pltpu.VMEM((features, count), BF),
+            pltpu.VMEM((count, wide), BF),
+            pltpu.VMEM((count + HALO, wide), F32),
+            pltpu.VMEM((count + HALO, wide), F32),
+            pltpu.VMEM((count, wide), F32),
+            pltpu.VMEM((count, 3 * wide), BF),
+            pltpu.VMEM((128, features), F32),
+            pltpu.VMEM((HALO, wide), BF),
+            pltpu.VMEM((HALO, wide), BF),
+            pltpu.VMEM((halves, *whole), BF),
+            dma((9,)),
+            dma((2, 3)),
+            dma((2,)),
+            *scatter_scratch((), rows, width, in_place=True),
+            *scatter_scratch((kinds,), rows, width),
+        ],
         compiler_params=pltpu.CompilerParams(
-            collective_id=1, has_side_effects=True, vmem_limit_bytes=48 * 1024 * 1024
+            collective_id=1, has_side_effects=True, vmem_limit_bytes=60 * 1024 * 1024
         ),
-        cost_estimate=pl.CostEstimate(flops=0, bytes_accessed=200_000_000, transcendentals=0),
-        name="scatter_gradients",
-    )(mixer.reshape(halves, *whole), feed.reshape(halves, kinds, *whole))
+        name="backward_and_scatter",
+    )(
+        term_feed.reshape(halves, kinds, *whole),
+        back_two,
+        feed_part,
+        middle,
+        cotangent,
+        tokens,
+        mixed,
+        gated,
+        weights,
+        vec,
+    )
 
 
 def feed_kernel(n_ref, c_ref, w_ref, t_ref, out_ref, back_ref, n_turned, c_turned, out_sum, back_sum):
@@ -754,9 +1028,10 @@
     gate_c = mixed[:, wide : 2 * wide]
     values = mixed[:, 2 * wide :]
     gated = (gate_b * values).astype(BF)
-    carried = shifted(gated[-2:], "seq", 1)
+    carried = shifted(gated[-HALO:], "seq", 1)
     carried = jnp.where(seq_index % half_seq == 0, jnp.zeros_like(carried), carried)
-    extended = jnp.concatenate([carried, gated], axis=0).astype(F32)
+    gated = jnp.concatenate([carried, gated], axis=0)
+    extended = gated[HALO - 2 :].astype(F32)
     convolved = taps[0] * extended[:-2] + taps[1] * extended[1:-1] + taps[2] * extended[2:]
     inner = (gate_c * convolved).astype(BF)
     middle = inputs + both_sum(dot(inner, full_out, ((1,), (1,))))
@@ -764,59 +1039,13 @@
     normed_two = (middle * inverse_two * gain_two).astype(BF)
 
     term_feed, feed_part, back_two_part = feed_forward(normed_two, cotangent, full_feed)
-    back_two_theirs = swapped(back_two_part)
-    back_normed_two = back_two_part.astype(F32) + back_two_theirs.astype(F32)
-    feed_part, _ = lax.optimization_barrier((feed_part, back_two_theirs))
-    block_out = middle + (feed_part.astype(F32) + swapped(feed_part).astype(F32))
-
-    back_out = cotangent.astype(F32)
-    back_middle = back_out + norm_back(middle, inverse_two, gain_two, back_normed_two)
-    gain_two_grad = jnp.sum(back_two_part.astype(F32) * middle * inverse_two, axis=0)
-    back_branch = back_middle.astype(BF)
-    back_inner = dot(back_branch, full_out, ((1,), (0,)))
-    back_gate_c = back_inner * convolved
-    back_conv = (back_inner * gate_c).astype(BF)
-    ahead = shifted(back_conv[:2], "seq", -1)
-    ahead = jnp.where(seq_index % half_seq == half_seq - 1, jnp.zeros_like(ahead), ahead)
-    back_extended = jnp.concatenate([back_conv, ahead], axis=0).astype(F32)
-    back_gated = (
-        taps[0] * back_extended[2:] + taps[1] * back_extended[1:-1] + taps[2] * back_extended[:-2]
+    width = inputs.shape[1]
+    vec = jnp.concatenate(
+        [vec_all[:2], jnp.pad(taps, ((0, 0), (0, width - wide))), jnp.zeros((3, width), F32)], axis=0
     )
-    back_conv_wide = back_conv.astype(F32)
-    tap_grads = jnp.stack(
-        [
-            jnp.sum(back_conv_wide * extended[:-2], axis=0),
-            jnp.sum(back_conv_wide * extended[1:-1], axis=0),
-            jnp.sum(back_conv_wide * extended[2:], axis=0),
-        ],
-        axis=0,
+    sum_mixer, sum_feed, block_out, input_grad = backward(
+        term_feed, back_two_part, feed_part, middle, cotangent, tokens, mixed, gated, full_mixer, vec
     )
-    back_mixed = jnp.concatenate(
-        [
-            (back_gated * values).astype(BF),
-            back_gate_c.astype(BF),
-            (back_gated * gate_b).astype(BF),
-        ],
-        axis=1,
-    )
-    back_one_part = low(dot(back_mixed, full_in, ((1,), (1,))))
-    back_normed = back_one_part + swapped(back_one_part.astype(BF)).astype(F32)
-    input_grad = back_middle + norm_back(inputs, inverse_one, gain_one, back_normed)
-    gain_one_grad = jnp.sum(back_one_part * inputs * inverse_one, axis=0)
-    term_in = dot(normed, back_mixed, ((0,), (0,))).astype(BF)
-    term_out = dot(back_branch, inner, ((0,), (0,))).astype(BF)
-
-    width = inputs.shape[1]
-    tap_rows = lax.dynamic_update_slice_in_dim(
-        jnp.zeros((3, width), F32), tap_grads, chan * wide, 1
-    )
-    vec_grad = jnp.concatenate([gain_one_grad[None], gain_two_grad[None], tap_rows], axis=0)
-    vec_term = jnp.pad(vec_grad.T.astype(BF), ((0, 0), (0, n_vec - 5)))
-    term_mixer = jnp.stack(
-        [term_in[:, :part], jnp.concatenate([term_in[:, part:], term_out, vec_term], axis=1)],
-        axis=0,
-    )
-    sum_mixer, sum_feed = scatter(term_mixer, term_feed)
     grad_in = jnp.concatenate([sum_mixer[0], sum_mixer[1, :, :cut]], axis=1).reshape(w_in.shape)
     grad_out = sum_mixer[1, :, cut : cut + n_out]
     both = jnp.concatenate([sum_feed[0], sum_feed[1]], axis=2)

time: 302 us -> 243 us (0.80)
  waiting for transfers between devices: 65.4 us -> 17.2 us
  Pallas kernels: 157 us -> 177 us
  other arithmetic: 23.8 us -> 10.9 us
  matrix products: 13.7 us -> 4.27 us
  starting transfers between devices: 17.6 us -> 8.32 us
    ppermute x6 -> x3, waiting for transfers between devices: 63.7 us -> 16.1 us  [swapped(): return lax.ppermute(block, 'chan', [(0, 1), (1, 0)])]
    pallas_call x1, Pallas kernels: 67.4 us -> 87.2 us  [backward(): pl.pallas_call(backward_kernel, out_shape=(jax.ShapeDtypeStruct((halves,...]
    dot_general x6 -> x2, matrix products: 13.7 us -> 4.27 us  [dot(): return lax.dot_general(a, b, (dims, ((), ())), preferred_element_type=F32)]
    unnamed x66 -> x62, local copies, waits for them, and re-layouts: 6.06 us -> 11.3 us
    ppermute x2 -> x1, starting transfers between devices: 6.83 us -> 1.92 us  [shifted(): return lax.ppermute(block, axis, route)]
    add x2 -> x0, other arithmetic: 4.61 us -> none  [the longest x1 2.84 us: body(): back_middle + norm_back(inputs, inverse_one, gain_one, back_normed)]
    ppermute x6 -> x3, starting transfers between devices: 10.7 us -> 6.4 us  [swapped(): return lax.ppermute(block, 'chan', [(0, 1), (1, 0)])]
    concatenate x1, local copies, waits for them, and re-layouts: 4.33 us -> 0.08 us  [body(): jnp.concatenate([vec_all[:2], jnp.pad(taps, ((0, 0), (0, width - wide))),...]
  transfers between devices with their start and end apart: 8 -> 4, of which waited for: 6 -> 2; matrix products, arithmetic and copies ran while one was open for 7% -> 6% of each run, Pallas kernels for 0% -> 0%
where the time goes in v3:
time: 243 us; the launch traced here: 240 us
  Pallas kernels  177 us (73%)
  local copies, waits for them, and re-layouts  21.2 us (9%)
  waiting for transfers between devices  17.2 us (7%)
  other arithmetic  10.9 us (4%)
  starting transfers between devices  8.32 us (3%)
  matrix products  4.27 us (2%)
    pallas_call x1, Pallas kernels, backward(): pl.pallas_call(backward_kernel, out_shape=(jax.ShapeDtypeStruct((halves,...  87.2 us
    pallas_call x1, Pallas kernels, gather(): pl.pallas_call(gather_kernel, out_shape=(jax.ShapeDtypeStruct((halves, *w...  65.6 us
    pallas_call x1, Pallas kernels, feed_forward(): pl.pallas_call(feed_kernel, grid=(width // lanes,), out_shape=(jax.ShapeD...  24.1 us
    ppermute x3, waiting for transfers between devices, swapped(): return lax.ppermute(block, 'chan', [(0, 1), (1, 0)])  16.1 us
    unnamed x62, local copies, waits for them, and re-layouts  11.3 us
    ppermute x3, starting transfers between devices, swapped(): return lax.ppermute(block, 'chan', [(0, 1), (1, 0)])  6.4 us
  transfers between devices with their start and end apart: 4, of which 2 were waited for; matrix products, arithmetic and copies ran while one was open for 6% of the time, Pallas kernels for 0%

profile of v3, /device:TPU:1, one launch (start us, length us, event | category | flops | bytes accessed | tf_op | source)
XLA Modules:
  0.0 240.0 jit_solution(16676607971390260745)
XLA Ops:
  1.4 3.7 %collective-permute-start = (f32[5,8]{0,1:T(8,128)S(1)}, f32[5,8]{0,1:T(8,128)S(1)}, u32[]{:S(2)}, u32[]{:S(2)}) collective-permute-start(f32[5,8]{0,1:T(8,128)S(1)} %copy.76), channel_id=1, source_target_pairs={{0,1},{1,0},{2,3},{3,2},{4,5},{5,4},{6,7},{7,6},{8,9},{9,8},{10,11... | collective-permute-start | bytes 488 | tf_op jit(solution)/shard_map/ppermute | solution.py:928
  5.2 1.4 fusion.4
  8.4 1.0 copy.104
  10.9 65.6 %gather_weights.1 = (bf16[2,2,4,4,2,16,1152]{6,5,4,3,2,1,0:T(8,128)(2,1)}, bf16[2,3,2,4,4,2,16,1152]{7,6,5,4,3,2,1,0:T(8,128)(2,1)}) custom-call(bf16[2,16,1152]{2,1,0:T(8,128)(2,1)} %pad_maximum_fusion.5.wm_ref, bf16[2,3,16,1152]{3,2,1,0:T(8,128)(2,1)} %pad_maximum_fusion.2.wf_ref), custom_call_target="tpu_custom_call" | custom-call | tf_op jit(solution)/shard_map/gather_weights/pallas_call | solution.py:268
  76.5 1.0 slice.160
  78.3 1.2 slice_bitcast_fusion.2
  79.5 1.9 slice.127
  81.5 1.5 fusion.mixed_hbm
  83.1 1.9 collective-permute-start.1
  85.1 1.1 collective-permute-done.1
  86.3 2.8 %fusion.52 = (bf16[384,1024]{1,0:T(8,128)(2,1)}, f32[384,1024]{1,0:T(8,128)S(1)}) fusion(bf16[2,1024,1152]{2,1,0:T(8,128)(2,1)} %bitcast.92, f32[386,512]{1,0:T(8,128)S(1)} %fusion.16, f32[384,1536]{1,0:T(8,128)S(1)} %fusion.mixed_hbm, f32[512]{0:T(512)S(1)} %bitcast.101, f32[512]{0:T(512)S(1)} %bitcast.102, f32[512]{0:T(512)S(1)} %bitcast.100), kind=kOutput, calls=%fused_computation.115 | convolution fusion | flops 404815872 | bytes 6559744 | tf_op jit(solution)/shard_map/dot_general | solution.py:941
  89.1 1.6 collective-permute-start.2
  93.7 16.1 %collective-permute-done.2 = bf16[384,1024]{1,0:T(8,128)(2,1)S(1)} collective-permute-done((bf16[384,1024]{1,0:T(8,128)(2,1)}, bf16[384,1024]{1,0:T(8,128)(2,1)S(1)}, u32[]{:S(2)}, u32[]{:S(2)}) %collective-permute-start.2) | collective-permute-done | bytes 786464 | tf_op jit(solution)/shard_map/ppermute | solution.py:928
  110.7 1.2 copy-done
  111.9 24.1 %feed_forward.1 = (bf16[2,3,1024,1152]{3,2,1,0:T(8,128)(2,1)}, bf16[384,1024]{1,0:T(8,128)(2,1)S(1)}, bf16[384,1024]{1,0:T(8,128)(2,1)S(1)}) custom-call(bf16[384,1024]{1,0:T(8,128)(2,1)S(1)} %multiply_convert_fusion.n_ref, bf16[384,1024]{1,0:T(8,128)(2,1)S(1)} %copy-done, bf16[2,3,1024,1152]{3,2,1,0:T(8,128)(2,1)} %bitcast.103), custom_call_target="tpu_custom_call" | custom-call | flops 16307453952 | bytes 28311552 | tf_op jit(solution)/shard_map/feed_forward/pallas_call | solution.py:897
  137.8 87.2 %backward_and_scatter.1 = (f32[2,16,1152]{2,1,0:T(8,128)}, f32[2,3,16,1152]{3,2,1,0:T(8,128)}, f32[384,1024]{1,0:T(8,128)}, f32[384,1024]{1,0:T(8,128)}) custom-call(bf16[2,3,2,4,4,2,16,1152]{7,6,5,4,3,2,1,0:T(8,128)(2,1)} %bitcast.89, bf16[384,1024]{1,0:T(8,128)(2,1)} %copy-done.2, bf16[384,1024]{1,0:T(8,128)(2,1)} %copy-done.1, f32[384,1024]{1,0:T(8,128)} %copy-done.3, ...), custom_call_target="tpu_custom_call" | custom-call | tf_op jit(solution)/shard_map/backward_and_scatter/pallas_call | solution.py:796
  227.6 1.1 collective-permute-start.3
  228.7 1.1 slice_bitcast_fusion.3
  230.2 0.9 copy.88
  231.1 1.4 multiply_subtract_fusion.3
  234.2 0.9 copy.89
  235.2 0.9 copy.90
  236.8 1.1 copy.111
  238.8 1.1 copy.112
  (100 shorter events, 16.9 us)
Async XLA Ops:
  0.7 9.5 %copy-start.15 = (f32[16,512]{1,0:T(8,128)S(1)}, f32[16,512]{1,0:T(8,128)}, u32[]{:S(2)}) copy-start(f32[16,512]{1,0:T(8,128)} %param.22) | copy-start | bytes 98308
  1.4 8.7 %collective-permute-start = (f32[5,8]{0,1:T(8,128)S(1)}, f32[5,8]{0,1:T(8,128)S(1)}, u32[]{:S(2)}, u32[]{:S(2)}) collective-permute-start(f32[5,8]{0,1:T(8,128)S(1)} %copy.76), channel_id=1, source_target_pairs={{0,1},{1,0},{2,3},{3,2},{4,5},{5,4},{6,7},{7,6},{8,9},{9,8},{10,11... | collective-permute-start | bytes 488 | tf_op jit(solution)/shard_map/ppermute | solution.py:928
  78.3 6.7 %copy-start.20 = (f32[3,1024]{1,0:T(4,128)}, f32[3,1024]{1,0:T(4,128)S(1)}, u32[]{:S(2)}) copy-start(f32[3,1024]{1,0:T(4,128)S(1)} %slice.166) | copy-start | bytes 36868
  79.5 1.9 copy-start.4
  82.9 3.3 %copy-start.5 = (f32[384,1536]{1,0:T(8,128)}, f32[384,1536]{1,0:T(8,128)S(1)}, u32[]{:S(2)}) copy-start(f32[384,1536]{1,0:T(8,128)S(1)} %fusion.mixed_hbm) | copy-start | bytes 7077892
  83.1 3.1 %collective-permute-start.1 = (bf16[16,512]{1,0:T(8,128)(2,1)S(1)}, bf16[16,512]{1,0:T(8,128)(2,1)S(1)}, u32[]{:S(2)}, u32[]{:S(2)}) collective-permute-start(bf16[16,512]{1,0:T(8,128)(2,1)S(1)} %slice.169), channel_id=1, source_target_pairs={{0,2},{2,4},{4,6},{6,8},{8,10},{10,12},{12,14},{14,16},{16,18},{18... | collective-permute-start | bytes 49160 | tf_op jit(solution)/shard_map/ppermute | solution.py:924
  89.1 20.7 %collective-permute-start.2 = (bf16[384,1024]{1,0:T(8,128)(2,1)}, bf16[384,1024]{1,0:T(8,128)(2,1)S(1)}, u32[]{:S(2)}, u32[]{:S(2)}) collective-permute-start(bf16[384,1024]{1,0:T(8,128)(2,1)} %get-tuple-element.124), channel_id=1, source_target_pairs={{0,1},{1,0},{2,3},{3,2},{4,5},{5,4},{6,7},{7,6},{8,9},{9,8},{10,11... | collective-permute-start | bytes 2359304 | tf_op jit(solution)/shard_map/ppermute | solution.py:928
  110.2 25.9 %copy-start.3 = (f32[384,1024]{1,0:T(8,128)}, f32[384,1024]{1,0:T(8,128)S(1)}, u32[]{:S(2)}) copy-start(f32[384,1024]{1,0:T(8,128)S(1)} %get-tuple-element.102.middle_hbm) | copy-start | bytes 4718596
  110.2 1.7 copy-start
  225.1 4.8 %copy-start.8 = (f32[16,2,2304]{2,1,0:T(2,128)S(1)}, f32[16,2,2304]{2,1,0:T(2,128)}, u32[]{:S(2)}) copy-start(f32[16,2,2304]{2,1,0:T(2,128)} %param.25) | copy-start | bytes 884740
  225.1 4.8 %copy-start.11 = (f32[16,2,2304]{2,1,0:T(2,128)S(1)}, f32[16,2,2304]{2,1,0:T(2,128)}, u32[]{:S(2)}) copy-start(f32[16,2,2304]{2,1,0:T(2,128)} %param.26) | copy-start | bytes 884740
  225.1 4.8 %copy-start.12 = (f32[16,2,2304]{2,1,0:T(2,128)S(1)}, f32[16,2,2304]{2,1,0:T(2,128)}, u32[]{:S(2)}) copy-start(f32[16,2,2304]{2,1,0:T(2,128)} %param.27) | copy-start | bytes 884740
  227.6 8.5 %collective-permute-start.3 = (f32[5,16]{1,0:T(8,128)S(1)}, f32[5,16]{1,0:T(8,128)S(1)}, u32[]{:S(2)}, u32[]{:S(2)}) collective-permute-start(f32[5,16]{1,0:T(8,128)S(1)} %bitcast.98), channel_id=1, source_target_pairs={{0,1},{1,0},{2,3},{3,2},{4,5},{5,4},{6,7},{7,6},{8,9},{9,8},{10,11... | collective-permute-start | bytes 968 | tf_op jit(solution)/shard_map/ppermute | solution.py:928
  229.8 2.7 %copy-start.9 = (f32[16,2304]{1,0:T(8,128)S(1)}, f32[16,2304]{1,0:T(8,128)}, u32[]{:S(2)}) copy-start(f32[16,2304]{1,0:T(8,128)} %param.28) | copy-start | bytes 442372
  229.9 2.7 %copy-start.13 = (f32[16,2304]{1,0:T(8,128)S(1)}, f32[16,2304]{1,0:T(8,128)}, u32[]{:S(2)}) copy-start(f32[16,2304]{1,0:T(8,128)} %param.29) | copy-start | bytes 442372
  229.9 2.7 %copy-start.14 = (f32[16,2304]{1,0:T(8,128)S(1)}, f32[16,2304]{1,0:T(8,128)}, u32[]{:S(2)}) copy-start(f32[16,2304]{1,0:T(8,128)} %param.30) | copy-start | bytes 442372
  230.2 3.3 %copy-start.10 = (f32[16,3,512]{2,0,1:T(8,128)S(1)}, f32[16,3,512]{2,0,1:T(8,128)}, u32[]{:S(2)}) copy-start(f32[16,3,512]{2,0,1:T(8,128)} %param.19) | copy-start | bytes 294916
  230.2 3.3 %copy-start.18 = (f32[16,3,512]{2,0,1:T(8,128)S(1)}, f32[16,3,512]{2,0,1:T(8,128)}, u32[]{:S(2)}) copy-start(f32[16,3,512]{2,0,1:T(8,128)} %param.20) | copy-start | bytes 294916
  230.2 3.3 %copy-start.19 = (f32[16,3,512]{2,0,1:T(8,128)S(1)}, f32[16,3,512]{2,0,1:T(8,128)}, u32[]{:S(2)}) copy-start(f32[16,3,512]{2,0,1:T(8,128)} %param.21) | copy-start | bytes 294916
  232.6 3.5 %copy-start.24 = (f32[5,8]{1,0:T(8,128)S(1)}, f32[5,8]{1,0:T(8,128)}, u32[]{:S(2)}) copy-start(f32[5,8]{1,0:T(8,128)} %param.31) | copy-start | bytes 484
  232.6 3.5 %copy-start.25 = (f32[5,8]{1,0:T(8,128)S(1)}, f32[5,8]{1,0:T(8,128)}, u32[]{:S(2)}) copy-start(f32[5,8]{1,0:T(8,128)} %param.32) | copy-start | bytes 484
  232.6 3.5 %copy-start.26 = (f32[5,8]{1,0:T(8,128)S(1)}, f32[5,8]{1,0:T(8,128)}, u32[]{:S(2)}) copy-start(f32[5,8]{1,0:T(8,128)} %param.33) | copy-start | bytes 484
  232.6 4.2 %copy-start.7 = (f32[384,1024]{1,0:T(8,128)S(1)}, f32[384,1024]{1,0:T(8,128)}, u32[]{:S(2)}) copy-start(f32[384,1024]{1,0:T(8,128)} %get-tuple-element.145) | copy-start | bytes 4718596
  236.8 2.0 copy-start.6
  (7 other events, 7.2 us)

commit v4 on v3

--- a/solution.py
+++ b/solution.py
@@ -237,11 +237,94 @@
     ]
 
 
-def gather_kernel(wm_ref, wf_ref, m_ref, f_ref, *sems):
+def rows_of(count, step):
+    return [slice(i, i + step) for i in range(0, count, step)]
+
+
+def mean_square(values):
+    return jnp.mean(values * values, axis=-1, keepdims=True)
+
+
+def in_tile(j, part):
+    lanes = part // 3
+    at = pl.ds(pl.multiple_of((j % 3) * lanes, 128), lanes)
+    return j // 3, at, pl.ds(pl.multiple_of(j * lanes, 128), lanes)
+
+
+def row_loop(count, step):
+    def body(i, carry):
+        step(pl.ds(pl.multiple_of(i * ROWS, ROWS), ROWS))
+        return carry
+
+    lax.fori_loop(0, count // ROWS, body, 0)
+
+
+ROWS = 32
+HALO = 16
+LANES = 128
+
+
+def forward_kernel(
+    tokens_hbm,
+    in_ref,
+    out_ref,
+    gu_ref,
+    down_ref,
+    vec_rows,
+    m_ref,
+    f_ref,
+    middle,
+    normed_two,
+    mixed,
+    gated,
+    vec,
+    *refs,
+):
+    (
+        tokens,
+        mixer_rows,
+        feed_rows,
+        vec_theirs,
+        normed,
+        wide_gated,
+        inner,
+        part_own,
+        part_theirs,
+        halo_in,
+        load_sem,
+        pairs,
+        halo_sem,
+    ) = refs[:13]
     me = Place()
-    me.greet()
-    mixer = Gathering(me, wm_ref, m_ref, sems[:5], ())
-    feed = Gathering(me, wf_ref, f_ref, sems[5:], EVERY)
+    pair = me.pair()
+    ahead_of, behind = me.along()
+    mixer = Gathering(me, mixer_rows, m_ref, refs[13:18], ())
+    feed = Gathering(me, feed_rows, f_ref, refs[18:], EVERY)
+    count, width = middle.shape
+    wide = inner.shape[1]
+    part = mixer_rows.shape[2]
+    cut = 3 * wide - part
+    load = pltpu.make_async_copy(tokens_hbm, tokens, load_sem)
+    load.start()
+    swap_vec = remote(vec_rows, vec_theirs, pairs.at[0, 0], pairs.at[1, 0], pair)
+    swap_part = remote(part_own, part_theirs, pairs.at[0, 1], pairs.at[1, 1], pair)
+    me.greet((pair, ahead_of, behind))
+    swap_vec.start()
+    for kind in range(2):
+        feed_rows[0, kind] = gu_ref[:, kind, :part].astype(BF)
+        feed_rows[1, kind] = gu_ref[:, kind, part:].astype(BF)
+    feed_rows[0, 2] = down_ref[:, :part].astype(BF)
+    feed_rows[1, 2] = down_ref[:, part:].astype(BF)
+    mixer_rows[0, :, :wide] = in_ref[:, 0, :].astype(BF)
+    mixer_rows[0, :, wide : 2 * wide] = in_ref[:, 1, :].astype(BF)
+    mixer_rows[0, :, 2 * wide :] = in_ref[:, 2, : part - 2 * wide].astype(BF)
+    mixer_rows[1, :, :cut] = in_ref[:, 2, part - 2 * wide :].astype(BF)
+    mixer_rows[1, :, cut : cut + wide] = out_ref[...].astype(BF)
+    swap_vec.wait_recv()
+    both = vec_rows[...] + vec_theirs[...]
+    high = both.astype(BF)
+    mixer_rows[1, :, cut + wide : cut + wide + LANES] = high
+    mixer_rows[1, :, cut + wide + LANES :] = (both - high.astype(F32)).astype(BF)
     mixer.begin()
     feed.begin()
     mixer.enter()
@@ -254,31 +337,122 @@
     mixer.along_a()
     feed.across_b()
     mixer.across_a()
+    mixer.from_sibling()
+    load.wait()
+
+    def columns(at, lanes):
+        return m_ref[1, :, :, :, :, :, at : at + lanes].reshape(width, lanes)
+
+    vec_columns = columns(cut + wide, LANES).astype(F32)
+    vec_columns = vec_columns + columns(cut + wide + LANES, LANES).astype(F32)
+    vec[...] = vec_columns.T[:8, :]
+    gain_one = vec[0:1, :]
+    gain_two = vec[1:2, :]
+    chan = lax.axis_index("chan")
+    tap_at = pl.ds(pl.multiple_of(chan * wide, LANES), wide)
+    taps = [vec[2 + i : 3 + i, tap_at] for i in range(3)]
+
+    def norm_step(at):
+        values = tokens[at, :].astype(F32)
+        normed[at, :] = (values * lax.rsqrt(mean_square(values) + norm_eps) * gain_one).astype(BF)
+
+    row_loop(count, norm_step)
+
+    def mixed_step(j, carry):
+        half, at, lanes = in_tile(j, part)
+        block = m_ref[half, :, :, :, :, :, at].reshape(width, part // 3)
+        mixed[:, lanes] = dot(normed[...], block, ((1,), (0,)))
+        return carry
+
+    lax.fori_loop(0, 4, mixed_step, 0)
+    for at in rows_of(count, ROWS):
+        rows = slice(at.start + HALO, at.stop + HALO)
+        product = (mixed[at, :wide] * mixed[at, 2 * wide :]).astype(BF)
+        gated[rows, :] = product
+        wide_gated[rows, :] = product.astype(F32)
+    halo = remote(
+        gated.at[pl.ds(count, HALO)], halo_in, halo_sem.at[0], halo_sem.at[1], ahead_of
+    )
+    halo.start()
+    halo.wait_recv()
+    starts = me.s % (lax.axis_size("seq") // 2) == 0
+    carried = jnp.where(starts, 0.0, halo_in[...].astype(F32))
+    gated[:HALO, :] = carried.astype(BF)
+    wide_gated[:HALO, :] = carried
+    for at in rows_of(count, ROWS):
+        convolved = taps[0] * wide_gated[at.start + HALO - 2 : at.stop + HALO - 2, :]
+        convolved = convolved + taps[1] * wide_gated[at.start + HALO - 1 : at.stop + HALO - 1, :]
+        convolved = convolved + taps[2] * wide_gated[at.start + HALO : at.stop + HALO, :]
+        inner[at, :] = (mixed[at, wide : 2 * wide] * convolved).astype(BF)
+    for rr in range(2):
+        at = slice(rr * (count // 2), (rr + 1) * (count // 2))
+        part_own[at, :] = dot(inner[at, :], columns(cut, wide), ((1,), (1,))).astype(BF)
+    swap_part.start()
     feed.along_a()
     feed.across_a()
-    for part in (mixer, feed):
-        part.from_sibling()
-        part.sent()
-
-
-def gather(mixer_rows, feed_rows):
-    halves, rows, width = mixer_rows.shape
-    kinds = feed_rows.shape[1]
-    whole = (2, RING, RING, 2, rows, width)
-    mixer, feed = pl.pallas_call(
-        gather_kernel,
+    swap_part.wait_recv()
+
+    def middle_step(at):
+        total = part_own[at, :].astype(F32) + part_theirs[at, :].astype(F32)
+        total = tokens[at, :].astype(F32) + total
+        middle[at, :] = total
+        inverse = lax.rsqrt(mean_square(total) + norm_eps)
+        normed_two[at, :] = (total * inverse * gain_two).astype(BF)
+
+    row_loop(count, middle_step)
+    feed.from_sibling()
+    mixer.sent()
+    feed.sent()
+    swap_vec.wait_send()
+    swap_part.wait_send()
+    halo.wait_send()
+
+
+def forward(tokens, w_in, w_out, w_gu, w_down, vec_rows):
+    count, width = tokens.shape
+    rows, _, wide = w_in.shape
+    part = w_down.shape[1] // 2
+    whole = (2, RING, RING, 2, rows, part)
+    vmem = pl.BlockSpec(memory_space=pltpu.VMEM)
+    hbm = pl.BlockSpec(memory_space=pl.ANY)
+    dma = pltpu.SemaphoreType.DMA
+    mixer, feed, *rest = pl.pallas_call(
+        forward_kernel,
         out_shape=(
-            jax.ShapeDtypeStruct((halves, *whole), BF),
-            jax.ShapeDtypeStruct((halves, kinds, *whole), BF),
+            jax.ShapeDtypeStruct((2, *whole), BF),
+            jax.ShapeDtypeStruct((2, 3, *whole), BF),
+            jax.ShapeDtypeStruct((count, width), F32),
+            jax.ShapeDtypeStruct((count, width), BF),
+            jax.ShapeDtypeStruct((count, 3 * wide), F32),
+            jax.ShapeDtypeStruct((count + HALO, wide), BF),
+            jax.ShapeDtypeStruct((8, width), F32),
         ),
-        in_specs=[pl.BlockSpec(memory_space=pl.ANY)] * 2,
-        out_specs=[pl.BlockSpec(memory_space=pl.ANY)] * 2,
-        scratch_shapes=gather_sems() + gather_sems(),
-        compiler_params=pltpu.CompilerParams(collective_id=0, has_side_effects=True),
-        name="gather_weights",
-    )(mixer_rows, feed_rows)
+        in_specs=[hbm] + [vmem] * 5,
+        out_specs=[vmem, hbm] + [vmem] * 5,
+        scratch_shapes=[
+            pltpu.VMEM((count, width), BF),
+            pltpu.VMEM((2, rows, part), BF),
+            pltpu.VMEM((2, 3, rows, part), BF),
+            pltpu.VMEM(vec_rows.shape, F32),
+            pltpu.VMEM((count, width), BF),
+            pltpu.VMEM((count + HALO, wide), F32),
+            pltpu.VMEM((count, wide), BF),
+            pltpu.VMEM((count, width), BF),
+            pltpu.VMEM((count, width), BF),
+            pltpu.VMEM((HALO, wide), BF),
+            dma,
+            dma((2, 2)),
+            dma((2,)),
+            *gather_sems(),
+            *gather_sems(),
+        ],
+        compiler_params=pltpu.CompilerParams(
+            collective_id=0, has_side_effects=True, vmem_limit_bytes=48 * 1024 * 1024
+        ),
+        name="gather_and_forward",
+    )(tokens, w_in, w_out, w_gu, w_down, vec_rows)
     total = 4 * RING * RING * rows
-    return mixer.reshape(halves, total, width), feed.reshape(halves, kinds, total, width)
+    return (mixer.reshape(2, total, part), feed.reshape(2, 3, total, part), *rest)
 
 
 class Scattering:
@@ -537,18 +711,6 @@
         dma((2, 3)),
         dma((4,)),
     ]
-
-
-def rows_of(count, step):
-    return [slice(i, i + step) for i in range(0, count, step)]
-
-
-def mean_square(values):
-    return jnp.mean(values * values, axis=-1, keepdims=True)
-
-
-ROWS = 32
-HALO = 16
 
 
 def backward_kernel(
@@ -595,13 +757,16 @@
         loads,
         pairs,
         halo_sem,
-    ) = refs[:26]
+        vec_own,
+        vec_theirs,
+        vec_sem,
+    ) = refs[:29]
     me = Place()
     pair = me.pair()
     ahead_of, behind = me.along()
     chan = lax.axis_index("chan")
-    mixer = Scattering(me, pm_ref, om_ref, refs[26:38], (), in_place=True)
-    feed = Scattering(me, pf_ref, of_ref, refs[38:], EVERY)
+    mixer = Scattering(me, pm_ref, om_ref, refs[29:41], (), in_place=True)
+    feed = Scattering(me, pf_ref, of_ref, refs[41:], EVERY)
     one_own, one_sum = cot, block_ref
     count, width = middle.shape
     wide = back_inner.shape[1]
@@ -638,7 +803,8 @@
 
     gain_one = vec[0:1, :]
     gain_two = vec[1:2, :]
-    taps = [vec[2 + i : 3 + i, :wide] for i in range(3)]
+    tap_at = pl.ds(pl.multiple_of(chan * wide, LANES), wide)
+    taps = [vec[2 + i : 3 + i, tap_at] for i in range(3)]
     sums[...] = jnp.zeros_like(sums)
     wide_gated[...] = gated[...].astype(F32)
 
@@ -689,7 +855,6 @@
     halo.wait_recv()
     last = me.s % (lax.axis_size("seq") // 2) == lax.axis_size("seq") // 2 - 1
     wide_conv[count : count + HALO, :] = jnp.where(last, 0.0, halo_in[...].astype(F32))
-    tap_at = pl.ds(pl.multiple_of(chan * wide, wide), wide)
     for at in rows_of(count, ROWS):
         back_gated = (
             taps[0] * wide_conv[at.start + 2 : at.stop + 2, :]
@@ -704,15 +869,10 @@
             term = wide_conv[at, :] * wide_gated[at.start + shift : at.stop + shift, :]
             sums[2 + i : 3 + i, tap_at] += jnp.sum(term, axis=0, keepdims=True)
 
-    def in_tile(j):
-        lanes = part // 3
-        at = pl.ds(pl.multiple_of((j % 3) * lanes, 128), lanes)
-        return j // 3, at, pl.ds(pl.multiple_of(j * lanes, 128), lanes)
-
     one_sum[...] = jnp.zeros_like(one_sum)
 
     def back_step(j, carry):
-        half, at, lanes = in_tile(j)
+        half, at, lanes = in_tile(j, part)
         one_sum[...] += dot(back_mixed[:, lanes], weights[half, :, at], ((1,), (1,)))
         return carry
 
@@ -731,7 +891,7 @@
     exchange(2).start()
 
     def term_step(j, carry):
-        half, at, lanes = in_tile(j)
+        half, at, lanes = in_tile(j, part)
         term = dot(turned[...], back_mixed[:, lanes], ((1,), (0,))).astype(BF)
         pm_ref[half, :, :, :, :, :, at] = term.reshape(*shape, part // 3)
         return carry
@@ -774,8 +934,13 @@
         return carry
 
     lax.fori_loop(0, count // ROWS, grad_step, 0)
+    mixer.finish()
+    vec_own[...] = om_ref[1, :, cut + wide : cut + wide + LANES]
+    swap_vec = remote(vec_own, vec_theirs, vec_sem.at[0], vec_sem.at[1], pair)
+    swap_vec.start()
     feed.finish()
-    mixer.finish()
+    swap_vec.wait()
+    om_ref[1, :, cut + wide : cut + wide + LANES] = vec_own[...] + vec_theirs[...]
     halo.wait_send()
     for i in range(3):
         exchange(i).wait_send()
@@ -824,6 +989,9 @@
             dma((9,)),
             dma((2, 3)),
             dma((2,)),
+            pltpu.VMEM((rows, LANES), F32),
+            pltpu.VMEM((rows, LANES), F32),
+            dma((2,)),
             *scatter_scratch((), rows, width, in_place=True),
             *scatter_scratch((kinds,), rows, width),
         ],
@@ -918,25 +1086,6 @@
     )(normed, cotangent, weights)
 
 
-def shifted(block, axis, distance):
-    devices = range(lax.axis_size(axis))
-    route = [(i - distance, i) for i in devices if i - distance in devices]
-    return lax.ppermute(block, axis, route)
-
-
-def swapped(block):
-    return lax.ppermute(block, "chan", [(0, 1), (1, 0)])
-
-
-def low(x):
-    return lax.reduce_precision(x, 8, 7)
-
-
-def both_sum(part):
-    rounded = low(part)
-    return rounded + swapped(rounded.astype(BF)).astype(F32)
-
-
 def dot(a, b, dims):
     return lax.dot_general(a, b, (dims, ((), ())), preferred_element_type=F32)
 
@@ -956,6 +1105,57 @@
         first_hat / (jnp.sqrt(second_hat) + adam_eps) + weight_decay * weight
     )
     return (weight_new, first_new, second_new)
+
+
+def adam_kernel(om_ref, of_ref, *refs):
+    chan = lax.axis_index("chan")
+    w_in, w_out, w_gu, w_down, vectors = [refs[3 * i : 3 * i + 3] for i in range(5)]
+    in_new, out_new, gu_new, down_new, vec_new = [refs[15 + 3 * i : 18 + 3 * i] for i in range(5)]
+    part = om_ref.shape[2]
+    wide = w_out[0].shape[1]
+    cut = 3 * wide - part
+
+    def update(arrays, results, index, gradient, rate=rate_matrix, decay=decay_matrix):
+        new = adam_update(*[a[index] for a in arrays], gradient, rate, decay)
+        for ref, value in zip(results, new):
+            ref[index] = value
+
+    def both(at):
+        return slice(None), at
+
+    for c in range(2):
+        at = slice(c * wide, (c + 1) * wide)
+        update(w_in, in_new, (slice(None), c), om_ref[0, :, at])
+    left = part - 2 * wide
+    update(w_in, in_new, (slice(None), 2, slice(0, left)), om_ref[0, :, 2 * wide :])
+    update(w_in, in_new, (slice(None), 2, slice(left, wide)), om_ref[1, :, :cut])
+    update(w_out, out_new, both(slice(None)), om_ref[1, :, cut : cut + wide])
+    for half in range(2):
+        at = slice(half * part, (half + 1) * part)
+        for kind in range(2):
+            update(w_gu, gu_new, (slice(None), kind, at), of_ref[half, kind])
+        update(w_down, down_new, both(at), of_ref[half, 2])
+    rows = om_ref.shape[1]
+    block = om_ref[1, :, cut + wide : cut + wide + LANES]
+    turned = jnp.concatenate([block, jnp.zeros((LANES - rows, LANES), F32)], axis=0).T
+    own = jnp.where(chan == 0, turned[:5, : rows // 2], turned[:5, rows // 2 : rows])
+    update(vectors, vec_new, both(slice(None)), own, rate_vector, 0.0)
+
+
+def adam(sum_mixer, sum_feed, arrays):
+    def whole(x):
+        return pl.BlockSpec(x.shape, lambda i, n=x.ndim: (0,) * n)
+
+    ins = (sum_mixer, sum_feed, *arrays)
+    return pl.pallas_call(
+        adam_kernel,
+        grid=(1,),
+        out_shape=[jax.ShapeDtypeStruct(x.shape, x.dtype) for x in arrays],
+        in_specs=[whole(x) for x in ins],
+        out_specs=[whole(x) for x in arrays],
+        compiler_params=pltpu.CompilerParams(vmem_limit_bytes=48 * 1024 * 1024),
+        name="adam",
+    )(*ins)
 
 
 def body(
@@ -977,89 +1177,30 @@
     vectors_m,
     vectors_v,
 ):
-    seq_count = lax.axis_size("seq")
-    seq_index = lax.axis_index("seq")
     chan = lax.axis_index("chan")
-    half_seq = seq_count // 2
-    rows = w_in.shape[0]
-    wide = w_in.shape[2]
-    n_in = 3 * wide
-    n_out = wide
-    hid = w_down.shape[1]
-    part = hid // 2
-    n_vec = hid - n_in - n_out
-
-    theirs = swapped(vectors)
-    first = jnp.where(chan == 0, vectors, theirs)
-    second = jnp.where(chan == 0, theirs, vectors)
-    vec_rows = jnp.concatenate([first, second], axis=1).T
-    vec_high = low(vec_rows)
-    vec_low = vec_rows - vec_high
-    vec_cols = jnp.pad(
-        jnp.concatenate([vec_high, vec_low], axis=1).astype(BF), ((0, 0), (0, n_vec - 10))
+    turned = vectors.T
+    none = jnp.zeros_like(turned)
+    vec_rows = jnp.where(
+        chan == 0,
+        jnp.concatenate([turned, none], axis=0),
+        jnp.concatenate([none, turned], axis=0),
     )
-    mixer_rows = jnp.concatenate(
-        [w_in.astype(BF).reshape(rows, n_in), w_out.astype(BF), vec_cols], axis=1
+    vec_rows = jnp.pad(vec_rows, ((0, 0), (0, LANES - vec_rows.shape[1])))
+    full_mixer, full_feed, middle, normed_two, mixed, gated, vec = forward(
+        tokens, w_in, w_out, w_gu, w_down, vec_rows
     )
-    mixer_rows = jnp.stack([mixer_rows[:, :part], mixer_rows[:, part:]], axis=0)
-    low_gu = w_gu.astype(BF)
-    low_down = w_down.astype(BF)
-    feed_rows = jnp.stack(
-        [
-            jnp.stack([low_gu[:, 0, at], low_gu[:, 1, at], low_down[:, at]], axis=0)
-            for at in (slice(0, part), slice(part, hid))
-        ],
-        axis=0,
-    )
-    full_mixer, full_feed = gather(mixer_rows, feed_rows)
-    cut = n_in - part
-    full_in = jnp.concatenate([full_mixer[0], full_mixer[1, :, :cut]], axis=1)
-    full_out = full_mixer[1, :, cut : cut + n_out]
-    vec_all = full_mixer[1, :, cut + n_out : cut + n_out + 10].astype(F32)
-    vec_all = (vec_all[:, :5] + vec_all[:, 5:]).T
-    taps = lax.dynamic_slice_in_dim(vec_all[2:5], chan * wide, wide, 1)
-    gain_one, gain_two = vec_all[0], vec_all[1]
-
-    inputs = tokens.astype(F32)
-    inverse_one = lax.rsqrt(jnp.mean(inputs * inputs, axis=-1, keepdims=True) + norm_eps)
-    normed = (inputs * inverse_one * gain_one).astype(BF)
-    mixed = dot(normed, full_in, ((1,), (0,)))
-    gate_b = mixed[:, :wide]
-    gate_c = mixed[:, wide : 2 * wide]
-    values = mixed[:, 2 * wide :]
-    gated = (gate_b * values).astype(BF)
-    carried = shifted(gated[-HALO:], "seq", 1)
-    carried = jnp.where(seq_index % half_seq == 0, jnp.zeros_like(carried), carried)
-    gated = jnp.concatenate([carried, gated], axis=0)
-    extended = gated[HALO - 2 :].astype(F32)
-    convolved = taps[0] * extended[:-2] + taps[1] * extended[1:-1] + taps[2] * extended[2:]
-    inner = (gate_c * convolved).astype(BF)
-    middle = inputs + both_sum(dot(inner, full_out, ((1,), (1,))))
-    inverse_two = lax.rsqrt(jnp.mean(middle * middle, axis=-1, keepdims=True) + norm_eps)
-    normed_two = (middle * inverse_two * gain_two).astype(BF)
-
     term_feed, feed_part, back_two_part = feed_forward(normed_two, cotangent, full_feed)
-    width = inputs.shape[1]
-    vec = jnp.concatenate(
-        [vec_all[:2], jnp.pad(taps, ((0, 0), (0, width - wide))), jnp.zeros((3, width), F32)], axis=0
-    )
     sum_mixer, sum_feed, block_out, input_grad = backward(
         term_feed, back_two_part, feed_part, middle, cotangent, tokens, mixed, gated, full_mixer, vec
     )
-    grad_in = jnp.concatenate([sum_mixer[0], sum_mixer[1, :, :cut]], axis=1).reshape(w_in.shape)
-    grad_out = sum_mixer[1, :, cut : cut + n_out]
-    both = jnp.concatenate([sum_feed[0], sum_feed[1]], axis=2)
-    grad_gu = jnp.stack([both[0], both[1]], axis=1)
-    grad_down = both[2]
-    sum_vec = sum_mixer[1, :, cut + n_out : cut + n_out + 5].T
-    sum_vec = sum_vec + swapped(sum_vec)
-    grad_vectors = lax.dynamic_slice_in_dim(sum_vec, chan * (rows // 2), rows // 2, 1)
-    in_new = adam_update(w_in, w_in_m, w_in_v, grad_in, rate_matrix, decay_matrix)
-    out_new = adam_update(w_out, w_out_m, w_out_v, grad_out, rate_matrix, decay_matrix)
-    gu_new = adam_update(w_gu, w_gu_m, w_gu_v, grad_gu, rate_matrix, decay_matrix)
-    down_new = adam_update(w_down, w_down_m, w_down_v, grad_down, rate_matrix, decay_matrix)
-    vec_new = adam_update(vectors, vectors_m, vectors_v, grad_vectors, rate_vector, 0.0)
-    return (block_out, input_grad, *in_new, *out_new, *gu_new, *down_new, *vec_new)
+    state = (
+        *(w_in, w_in_m, w_in_v),
+        *(w_out, w_out_m, w_out_v),
+        *(w_gu, w_gu_m, w_gu_v),
+        *(w_down, w_down_m, w_down_v),
+        *(vectors, vectors_m, vectors_v),
+    )
+    return (block_out, input_grad, *adam(sum_mixer, sum_feed, state))
 
 
 def solution(mesh):

time: 243 us -> 222 us (0.914); the launches traced: 240 us -> 221 us
  Pallas kernels: 177 us -> 203 us
  waiting for transfers between devices: 17.2 us -> 0 us
  other arithmetic: 10.9 us -> 0.01 us
  starting transfers between devices: 8.32 us -> 0 us
  matrix products: 4.27 us -> 0 us
  local copies, waits for them, and re-layouts: 21.2 us -> 17.6 us
    pallas_call x1 -> x2, Pallas kernels: 65.6 us -> 83.5 us  [the longest x1 81.5 us: forward(): pl.pallas_call(forward_kernel, out_shape=(jax.ShapeDtypeStruct((2, *whole...]
    ppermute x4 -> x0, waiting for transfers between devices: 17.2 us -> none  [the longest x3 16.1 us: swapped(): return lax.ppermute(block, 'chan', [(0, 1), (1, 0)])]
    ppermute x4 -> x0, starting transfers between devices: 8.32 us -> none  [the longest x3 6.4 us: swapped(): return lax.ppermute(block, 'chan', [(0, 1), (1, 0)])]
    pallas_call x1, Pallas kernels: 87.2 us -> 95.2 us  [backward(): pl.pallas_call(backward_kernel, out_shape=(jax.ShapeDtypeStruct((halves,...]
    unnamed x62 -> x65, local copies, waits for them, and re-layouts: 11.3 us -> 17.6 us
    slice x9 -> x0, local copies, waits for them, and re-layouts: 5.2 us -> none  [the longest x1 1.92 us: body(): full_in = jnp.concatenate([full_mixer[0], full_mixer[1, :, :cut]], axis=1)]
    dot_general x2 -> x0, matrix products: 4.27 us -> none  [dot(): return lax.dot_general(a, b, (dims, ((), ())), preferred_element_type=F32)]
    squeeze x4 -> x0, local copies, waits for them, and re-layouts: 3.91 us -> none  [the longest x1 1.21 us: body(): full_in = jnp.concatenate([full_mixer[0], full_mixer[1, :, :cut]], axis=1)]
  transfers between devices with their start and end apart: 4 -> 0, of which waited for: 2 -> 0; matrix products, arithmetic and copies ran while one was open for 6% -> 0% of each run, Pallas kernels for 0% -> 0%
where the time goes in v4:
time: 222 us; the launch traced here: 221 us
  Pallas kernels  203 us (91%)
  local copies, waits for them, and re-layouts  17.6 us (8%)
    pallas_call x1, Pallas kernels, backward(): pl.pallas_call(backward_kernel, out_shape=(jax.ShapeDtypeStruct((halves,...  95.2 us
    pallas_call x1, Pallas kernels, forward(): pl.pallas_call(forward_kernel, out_shape=(jax.ShapeDtypeStruct((2, *whole...  81.5 us
    pallas_call x1, Pallas kernels, feed_forward(): pl.pallas_call(feed_kernel, grid=(width // lanes,), out_shape=(jax.ShapeD...  24.2 us
    unnamed x65, local copies, waits for them, and re-layouts  17.6 us

profile of v4, /device:TPU:1, one launch (start us, length us, event | category | flops | bytes accessed | tf_op | source)
XLA Modules:
  0.0 221.5 jit_solution(3798366112344009137)
XLA Ops:
  0.7 1.0 copy.35.in_ref.refs_0_
  1.6 0.8 copy.34
  2.4 1.1 copy-done
  3.5 1.0 copy-done.2
  4.5 0.9 copy-done.7
  5.4 0.8 copy-done.16
  6.2 81.5 %gather_and_forward.1 = (bf16[2,2,4,4,2,16,1152]{6,5,4,3,2,1,0:T(8,128)(2,1)}, bf16[2,3,2,4,4,2,16,1152]{7,6,5,4,3,2,1,0:T(8,128)(2,1)}, f32[384,1024]{1,0:T(8,1...) custom-call(bf16[384,1024]{1,0:T(8,128)(2,1)S(1)} %copy-done, ...), custom_call_target="tpu_custom_call" | custom-call | tf_op jit(solution)/shard_map/gather_and_forward/pallas_call | solution.py:419
  87.7 1.1 copy-done.1
  88.8 0.6 copy-done.20
  89.5 1.3 copy-done.4
  90.7 24.2 %feed_forward.1 = (bf16[2,3,1024,1152]{3,2,1,0:T(8,128)(2,1)}, bf16[384,1024]{1,0:T(8,128)(2,1)S(1)}, bf16[384,1024]{1,0:T(8,128)(2,1)S(1)}) custom-call(bf16[384,1024]{1,0:T(8,128)(2,1)S(1)} %get-tuple-element.46.n_ref, bf16[384,1024]{1,0:T(8,128)(2,1)S(1)} %copy-done.4, bf16[2,3,1024,1152]{3,2,1,0:T(8,128)(2,1)} %bitcast.7), custom_call_target="tpu_custom_call" | custom-call | flops 16307453952 | bytes 28311552 | tf_op jit(solution)/shard_map/feed_forward/pallas_call | solution.py:1065
  114.9 0.9 copy-done.5
  115.8 0.9 copy-done.6
  116.8 95.2 %backward_and_scatter.1 = (f32[2,16,1152]{2,1,0:T(8,128)}, f32[2,3,16,1152]{3,2,1,0:T(8,128)}, f32[384,1024]{1,0:T(8,128)}, f32[384,1024]{1,0:T(8,128)}) custom-call(bf16[2,3,2,4,4,2,16,1152]{7,6,5,4,3,2,1,0:T(8,128)(2,1)} %bitcast.4, bf16[384,1024]{1,0:T(8,128)(2,1)} %copy-done.6, bf16[384,1024]{1,0:T(8,128)(2,1)} %copy-done.5, f32[384,1024]{1,0:T(8,128)} %copy-done.1, ...), custom_call_target="tpu_custom_call" | custom-call | tf_op jit(solution)/shard_map/backward_and_scatter/pallas_call | solution.py:961
  212.2 0.1 copy.38.refs_2_
  212.4 1.0 copy-done.9
  213.4 0.9 copy-done.15
  214.3 2.0 adam.1
  216.3 0.7 copy.39
  217.0 0.7 copy.40
  217.7 0.7 copy.41
  218.3 1.1 copy.44
  219.5 0.8 copy-done.24
  220.3 1.1 copy.45
  (47 shorter events, 0.2 us)
Async XLA Ops:
  2.4 1.1 copy-start
  3.5 1.0 copy-start.2
  4.5 0.9 copy-start.7
  87.7 1.1 copy-start.1
  89.5 25.5 %copy-start.10 = (bf16[400,512]{1,0:T(8,128)(2,1)}, bf16[400,512]{1,0:T(8,128)(2,1)S(1)}, u32[]{:S(2)}) copy-start(bf16[400,512]{1,0:T(8,128)(2,1)S(1)} %get-tuple-element.53.gated_hbm) | copy-start | bytes 1228804
  89.5 1.3 copy-start.4
  114.9 0.9 copy-start.5
  116.7 95.4 %copy-start.26 = (f32[16,3,512]{2,0,1:T(8,128)S(1)}, f32[16,3,512]{2,0,1:T(8,128)}, u32[]{:S(2)}) copy-start(f32[16,3,512]{2,0,1:T(8,128)} %param.20) | copy-start | bytes 294916
  116.7 95.5 %copy-start.27 = (f32[16,3,512]{2,0,1:T(8,128)S(1)}, f32[16,3,512]{2,0,1:T(8,128)}, u32[]{:S(2)}) copy-start(f32[16,3,512]{2,0,1:T(8,128)} %param.21) | copy-start | bytes 294916
  116.7 95.5 %copy-start.3 = (f32[16,2,2304]{2,1,0:T(2,128)S(1)}, f32[16,2,2304]{2,1,0:T(2,128)}, u32[]{:S(2)}) copy-start(f32[16,2,2304]{2,1,0:T(2,128)} %refs_6_.1) | copy-start | bytes 884740
  116.7 95.6 %copy-start.8 = (f32[16,2304]{1,0:T(8,128)S(1)}, f32[16,2304]{1,0:T(8,128)}, u32[]{:S(2)}) copy-start(f32[16,2304]{1,0:T(8,128)} %refs_9_.1) | copy-start | bytes 442372
  116.7 95.6 %copy-start.11 = (f32[16,2,2304]{2,1,0:T(2,128)S(1)}, f32[16,2,2304]{2,1,0:T(2,128)}, u32[]{:S(2)}) copy-start(f32[16,2,2304]{2,1,0:T(2,128)} %refs_7_.1) | copy-start | bytes 884740
  116.7 95.6 %copy-start.12 = (f32[16,2,2304]{2,1,0:T(2,128)S(1)}, f32[16,2,2304]{2,1,0:T(2,128)}, u32[]{:S(2)}) copy-start(f32[16,2,2304]{2,1,0:T(2,128)} %refs_8_.1) | copy-start | bytes 884740
  116.7 95.6 %copy-start.13 = (f32[16,2304]{1,0:T(8,128)S(1)}, f32[16,2304]{1,0:T(8,128)}, u32[]{:S(2)}) copy-start(f32[16,2304]{1,0:T(8,128)} %refs_10_.1) | copy-start | bytes 442372
  116.8 95.6 %copy-start.14 = (f32[16,2304]{1,0:T(8,128)S(1)}, f32[16,2304]{1,0:T(8,128)}, u32[]{:S(2)}) copy-start(f32[16,2304]{1,0:T(8,128)} %refs_11_.1) | copy-start | bytes 442372
  116.8 95.6 %copy-start.17 = (f32[16,512]{1,0:T(8,128)S(1)}, f32[16,512]{1,0:T(8,128)}, u32[]{:S(2)}) copy-start(f32[16,512]{1,0:T(8,128)} %refs_3_.1) | copy-start | bytes 98308
  116.8 95.6 %copy-start.18 = (f32[16,512]{1,0:T(8,128)S(1)}, f32[16,512]{1,0:T(8,128)}, u32[]{:S(2)}) copy-start(f32[16,512]{1,0:T(8,128)} %refs_4_.1) | copy-start | bytes 98308
  116.8 95.5 %copy-start.19 = (f32[16,512]{1,0:T(8,128)S(1)}, f32[16,512]{1,0:T(8,128)}, u32[]{:S(2)}) copy-start(f32[16,512]{1,0:T(8,128)} %refs_5_.1) | copy-start | bytes 98308
  116.8 95.5 %copy-start.21 = (f32[5,8]{1,0:T(8,128)S(1)}, f32[5,8]{1,0:T(8,128)}, u32[]{:S(2)}) copy-start(f32[5,8]{1,0:T(8,128)} %refs_12_.1) | copy-start | bytes 484
  116.8 95.5 %copy-start.22 = (f32[5,8]{1,0:T(8,128)S(1)}, f32[5,8]{1,0:T(8,128)}, u32[]{:S(2)}) copy-start(f32[5,8]{1,0:T(8,128)} %refs_13_.1) | copy-start | bytes 484
  116.8 95.5 %copy-start.23 = (f32[5,8]{1,0:T(8,128)S(1)}, f32[5,8]{1,0:T(8,128)}, u32[]{:S(2)}) copy-start(f32[5,8]{1,0:T(8,128)} %refs_14_.1) | copy-start | bytes 484
  212.4 1.0 copy-start.9
  214.3 4.0 %copy-start.25 = (f32[384,1024]{1,0:T(8,128)S(1)}, f32[384,1024]{1,0:T(8,128)}, u32[]{:S(2)}) copy-start(f32[384,1024]{1,0:T(8,128)} %get-tuple-element.109) | copy-start | bytes 4718596
  218.3 2.0 copy-start.24
  (4 other events, 3.2 us)

commit v5 on v4

--- a/solution.py
+++ b/solution.py
@@ -19,6 +19,7 @@
 F32 = jnp.float32
 
 RING = 4
+PLANE = ((1, 0), (0, 3), (0, 1), (1, 3), (1, 1), (0, 2), (1, 2))
 
 
 class Place:
@@ -44,6 +45,9 @@
     def on_b(self, off):
         return self.s + ((self.pb + off) % RING - self.pb) * self.step_b
 
+    def on_plane(self, rr, off):
+        return self.on_b(off) + rr * (1 - 2 * self.y) * 2 * RING * RING
+
     def row(self, rr):
         return self.y + rr * (1 - 2 * self.y)
 
@@ -54,7 +58,8 @@
 
     def peers(self):
         near = (self.sibling, self.other_y, self.on_a(1), self.on_a(3), self.on_b(1), self.on_b(3))
-        return [{"seq": peer} for peer in near]
+        far = [self.on_plane(rr, off) for rr, off in PLANE if (rr, off) not in ((1, 0), (0, 3), (0, 1))]
+        return [{"seq": peer} for peer in (*near, *far)]
 
     def along(self):
         count = lax.axis_size("seq")
@@ -135,6 +140,27 @@
         self.own().wait()
         self.first(me.core, 1 - me.core).wait_recv()
         self.start((YY, AR, AL, BR, BL, SIB), 0, me.pa, me.pb)
+
+    def plane_copy(self, rr, off):
+        me = self.me
+        block = self.block(me.core, me.y, me.x, me.z)
+        at = (me.y * RING + me.x) * RING + me.z
+        send = self.send.at[YY, rr * RING + off]
+        return remote(block, block, send, self.recv.at[at], me.on_plane(rr, off))
+
+    def enter_plane(self):
+        me = self.me
+        self.own().wait()
+        self.first(me.core, 1 - me.core).wait_recv()
+        for rr, off in PLANE:
+            self.plane_copy(rr, off).start()
+        self.start((AR, AL, SIB), 0, me.pa, me.pb)
+
+    def along_plane(self):
+        me = self.me
+        for rr, off in PLANE:
+            self.arrived(rr, me.pa, me.pb + off)
+            self.start((AR, AL, SIB), rr, me.pa, me.pb + off)
 
     def second_row(self):
         me = self.me
@@ -200,16 +226,20 @@
 
         lax.fori_loop(0, 2 * RING * RING, step, 0)
 
-    def sent(self):
+    def sent(self, plane=False):
         me = self.me
         pa, pb = me.pa, me.pb
         self.first(1 - me.core, me.core).wait_send()
-        self.copy(YY, 0, pa, pb).wait_send()
-        for rr in range(2):
-            self.copy(BR, rr, pa, pb).wait_send()
-            self.copy(BL, rr, pa, pb).wait_send()
-        self.copy(BR, 0, pa, pb + 3).wait_send()
-        self.copy(BL, 1, pa, pb + 1).wait_send()
+        if plane:
+            for rr, off in PLANE:
+                self.plane_copy(rr, off).wait_send()
+        else:
+            self.copy(YY, 0, pa, pb).wait_send()
+            for rr in range(2):
+                self.copy(BR, rr, pa, pb).wait_send()
+                self.copy(BL, rr, pa, pb).wait_send()
+            self.copy(BR, 0, pa, pb + 3).wait_send()
+            self.copy(BL, 1, pa, pb + 1).wait_send()
 
         def step(b, carry):
             for rr in range(2):
@@ -237,8 +267,8 @@
     ]
 
 
-def rows_of(count, step):
-    return [slice(i, i + step) for i in range(0, count, step)]
+def rows_of(stop, step, start=0):
+    return [slice(i, i + step) for i in range(start, stop, step)]
 
 
 def mean_square(values):
@@ -251,12 +281,12 @@
     return j // 3, at, pl.ds(pl.multiple_of(j * lanes, 128), lanes)
 
 
-def row_loop(count, step):
+def row_loop(count, step, start=0, rows=32):
     def body(i, carry):
-        step(pl.ds(pl.multiple_of(i * ROWS, ROWS), ROWS))
+        step(pl.ds(pl.multiple_of(start + i * rows, HALO), rows))
         return carry
 
-    lax.fori_loop(0, count // ROWS, body, 0)
+    lax.fori_loop(0, count // rows, body, 0)
 
 
 ROWS = 32
@@ -270,17 +300,23 @@
     out_ref,
     gu_ref,
     down_ref,
-    vec_rows,
-    m_ref,
+    vec_ref,
+    m_hbm,
     f_ref,
     middle,
     normed_two,
-    mixed,
-    gated,
+    mixed_hbm,
+    gated_hbm,
     vec,
     *refs,
 ):
     (
+        m_ref,
+        mixed,
+        gated,
+        vec_square,
+        vec_rows,
+        out_sems,
         tokens,
         mixer_rows,
         feed_rows,
@@ -294,20 +330,38 @@
         load_sem,
         pairs,
         halo_sem,
-    ) = refs[:13]
+    ) = refs[:19]
     me = Place()
     pair = me.pair()
     ahead_of, behind = me.along()
-    mixer = Gathering(me, mixer_rows, m_ref, refs[13:18], ())
-    feed = Gathering(me, feed_rows, f_ref, refs[18:], EVERY)
+    mixer = Gathering(me, mixer_rows, m_ref, refs[19:24], ())
+    feed = Gathering(me, feed_rows, f_ref, refs[24:], EVERY)
     count, width = middle.shape
     wide = inner.shape[1]
     part = mixer_rows.shape[2]
     cut = 3 * wide - part
     load = pltpu.make_async_copy(tokens_hbm, tokens, load_sem)
     load.start()
+    chan = lax.axis_index("chan")
+    vec_square[...] = jnp.zeros_like(vec_square)
+    vec_square[: vec_ref.shape[0], : vec_ref.shape[1]] = vec_ref[...]
+    turned = vec_square[...].T
+    own_rows = vec_ref.shape[1]
+    vec_rows[...] = jnp.zeros_like(vec_rows)
+    vec_rows[pl.ds(pl.multiple_of(chan * own_rows, own_rows), own_rows), :] = turned[:own_rows, :]
+
+    def keep(i):
+        src, dst = ((m_ref, m_hbm), (mixed, mixed_hbm), (gated, gated_hbm))[i]
+        return pltpu.make_async_copy(src, dst, out_sems.at[i])
+
     swap_vec = remote(vec_rows, vec_theirs, pairs.at[0, 0], pairs.at[1, 0], pair)
-    swap_part = remote(part_own, part_theirs, pairs.at[0, 1], pairs.at[1, 1], pair)
+
+    def swap_part(lo):
+        at = pl.ds(lo, count // 2)
+        i = 1 if lo else 2
+        src, dst = part_own.at[at], part_theirs.at[at]
+        return remote(src, dst, pairs.at[0, i], pairs.at[1, i], pair)
+
     me.greet((pair, ahead_of, behind))
     swap_vec.start()
     for kind in range(2):
@@ -315,29 +369,28 @@
         feed_rows[1, kind] = gu_ref[:, kind, part:].astype(BF)
     feed_rows[0, 2] = down_ref[:, :part].astype(BF)
     feed_rows[1, 2] = down_ref[:, part:].astype(BF)
-    mixer_rows[0, :, :wide] = in_ref[:, 0, :].astype(BF)
-    mixer_rows[0, :, wide : 2 * wide] = in_ref[:, 1, :].astype(BF)
-    mixer_rows[0, :, 2 * wide :] = in_ref[:, 2, : part - 2 * wide].astype(BF)
-    mixer_rows[1, :, :cut] = in_ref[:, 2, part - 2 * wide :].astype(BF)
+    mixer_rows[0, :, :wide] = in_ref[0].astype(BF)
+    mixer_rows[0, :, wide : 2 * wide] = in_ref[1].astype(BF)
+    mixer_rows[0, :, 2 * wide :] = in_ref[2, :, : part - 2 * wide].astype(BF)
+    mixer_rows[1, :, :cut] = in_ref[2, :, part - 2 * wide :].astype(BF)
     mixer_rows[1, :, cut : cut + wide] = out_ref[...].astype(BF)
+    feed.begin()
     swap_vec.wait_recv()
     both = vec_rows[...] + vec_theirs[...]
     high = both.astype(BF)
     mixer_rows[1, :, cut + wide : cut + wide + LANES] = high
     mixer_rows[1, :, cut + wide + LANES :] = (both - high.astype(F32)).astype(BF)
     mixer.begin()
-    feed.begin()
-    mixer.enter()
-    mixer.second_row()
     feed.enter()
-    mixer.along_b()
+    mixer.enter_plane()
     feed.second_row()
-    mixer.across_b()
+    mixer.along_plane()
     feed.along_b()
     mixer.along_a()
     feed.across_b()
     mixer.across_a()
     mixer.from_sibling()
+    keep(0).start()
     load.wait()
 
     def columns(at, lanes):
@@ -348,7 +401,6 @@
     vec[...] = vec_columns.T[:8, :]
     gain_one = vec[0:1, :]
     gain_two = vec[1:2, :]
-    chan = lax.axis_index("chan")
     tap_at = pl.ds(pl.multiple_of(chan * wide, LANES), wide)
     taps = [vec[2 + i : 3 + i, tap_at] for i in range(3)]
 
@@ -358,39 +410,50 @@
 
     row_loop(count, norm_step)
 
-    def mixed_step(j, carry):
-        half, at, lanes = in_tile(j, part)
-        block = m_ref[half, :, :, :, :, :, at].reshape(width, part // 3)
-        mixed[:, lanes] = dot(normed[...], block, ((1,), (0,)))
-        return carry
-
-    lax.fori_loop(0, 4, mixed_step, 0)
-    for at in rows_of(count, ROWS):
-        rows = slice(at.start + HALO, at.stop + HALO)
-        product = (mixed[at, :wide] * mixed[at, 2 * wide :]).astype(BF)
-        gated[rows, :] = product
-        wide_gated[rows, :] = product.astype(F32)
+    half = count // 2
+    edge = half - HALO
+
+    def gated_rows(lo, hi):
+        def mixed_step(j, carry):
+            which, at, lanes = in_tile(j, part)
+            block = m_ref[which, :, :, :, :, :, at].reshape(width, part // 3)
+            mixed[lo:hi, lanes] = dot(normed[lo:hi, :], block, ((1,), (0,)))
+            return carry
+
+        lax.fori_loop(0, 4, mixed_step, 0)
+        for at in rows_of(hi, HALO, lo):
+            rows = slice(at.start + HALO, at.stop + HALO)
+            product = (mixed[at, :wide] * mixed[at, 2 * wide :]).astype(BF)
+            gated[rows, :] = product
+            wide_gated[rows, :] = product.astype(F32)
+
+    def branch_rows(lo, hi):
+        for at in rows_of(hi, ROWS, lo):
+            convolved = taps[0] * wide_gated[at.start + HALO - 2 : at.stop + HALO - 2, :]
+            convolved = convolved + taps[1] * wide_gated[at.start + HALO - 1 : at.stop + HALO - 1, :]
+            convolved = convolved + taps[2] * wide_gated[at.start + HALO : at.stop + HALO, :]
+            inner[at, :] = (mixed[at, wide : 2 * wide] * convolved).astype(BF)
+        part_own[lo:hi, :] = dot(inner[lo:hi, :], columns(cut, wide), ((1,), (1,))).astype(BF)
+
+    gated_rows(edge, count)
     halo = remote(
         gated.at[pl.ds(count, HALO)], halo_in, halo_sem.at[0], halo_sem.at[1], ahead_of
     )
     halo.start()
+    branch_rows(half, count)
+    swap_part(half).start()
+    gated_rows(0, edge)
+    keep(1).start()
     halo.wait_recv()
     starts = me.s % (lax.axis_size("seq") // 2) == 0
     carried = jnp.where(starts, 0.0, halo_in[...].astype(F32))
     gated[:HALO, :] = carried.astype(BF)
+    keep(2).start()
     wide_gated[:HALO, :] = carried
-    for at in rows_of(count, ROWS):
-        convolved = taps[0] * wide_gated[at.start + HALO - 2 : at.stop + HALO - 2, :]
-        convolved = convolved + taps[1] * wide_gated[at.start + HALO - 1 : at.stop + HALO - 1, :]
-        convolved = convolved + taps[2] * wide_gated[at.start + HALO : at.stop + HALO, :]
-        inner[at, :] = (mixed[at, wide : 2 * wide] * convolved).astype(BF)
-    for rr in range(2):
-        at = slice(rr * (count // 2), (rr + 1) * (count // 2))
-        part_own[at, :] = dot(inner[at, :], columns(cut, wide), ((1,), (1,))).astype(BF)
-    swap_part.start()
+    branch_rows(0, half)
+    swap_part(0).start()
     feed.along_a()
     feed.across_a()
-    swap_part.wait_recv()
 
     def middle_step(at):
         total = part_own[at, :].astype(F32) + part_theirs[at, :].astype(F32)
@@ -399,18 +462,24 @@
         inverse = lax.rsqrt(mean_square(total) + norm_eps)
         normed_two[at, :] = (total * inverse * gain_two).astype(BF)
 
-    row_loop(count, middle_step)
+    swap_part(half).wait_recv()
+    row_loop(half, middle_step, half)
+    swap_part(0).wait_recv()
+    row_loop(half, middle_step)
     feed.from_sibling()
-    mixer.sent()
+    mixer.sent(plane=True)
     feed.sent()
     swap_vec.wait_send()
-    swap_part.wait_send()
+    swap_part(half).wait_send()
+    swap_part(0).wait_send()
     halo.wait_send()
-
-
-def forward(tokens, w_in, w_out, w_gu, w_down, vec_rows):
+    for i in range(3):
+        keep(i).wait()
+
+
+def forward(tokens, w_in, w_out, w_gu, w_down, vectors):
     count, width = tokens.shape
-    rows, _, wide = w_in.shape
+    _, rows, wide = w_in.shape
     part = w_down.shape[1] // 2
     whole = (2, RING, RING, 2, rows, part)
     vmem = pl.BlockSpec(memory_space=pltpu.VMEM)
@@ -428,12 +497,18 @@
             jax.ShapeDtypeStruct((8, width), F32),
         ),
         in_specs=[hbm] + [vmem] * 5,
-        out_specs=[vmem, hbm] + [vmem] * 5,
+        out_specs=[hbm, hbm, vmem, vmem, hbm, hbm, vmem],
         scratch_shapes=[
+            pltpu.VMEM((2, *whole), BF),
+            pltpu.VMEM((count, 3 * wide), F32),
+            pltpu.VMEM((count + HALO, wide), BF),
+            pltpu.VMEM((LANES, LANES), F32),
+            pltpu.VMEM((rows, LANES), F32),
+            dma((3,)),
             pltpu.VMEM((count, width), BF),
             pltpu.VMEM((2, rows, part), BF),
             pltpu.VMEM((2, 3, rows, part), BF),
-            pltpu.VMEM(vec_rows.shape, F32),
+            pltpu.VMEM((rows, LANES), F32),
             pltpu.VMEM((count, width), BF),
             pltpu.VMEM((count + HALO, wide), F32),
             pltpu.VMEM((count, wide), BF),
@@ -441,16 +516,16 @@
             pltpu.VMEM((count, width), BF),
             pltpu.VMEM((HALO, wide), BF),
             dma,
-            dma((2, 2)),
+            dma((2, 3)),
             dma((2,)),
             *gather_sems(),
             *gather_sems(),
         ],
         compiler_params=pltpu.CompilerParams(
-            collective_id=0, has_side_effects=True, vmem_limit_bytes=48 * 1024 * 1024
+            collective_id=0, has_side_effects=True, vmem_limit_bytes=60 * 1024 * 1024
         ),
         name="gather_and_forward",
-    )(tokens, w_in, w_out, w_gu, w_down, vec_rows)
+    )(tokens, w_in, w_out, w_gu, w_down, vectors)
     total = 4 * RING * RING * rows
     return (mixer.reshape(2, total, part), feed.reshape(2, 3, total, part), *rest)
 
@@ -484,6 +559,9 @@
 
     def add(self, where, *others):
         index = (*self.head, *where)
+        if len(others) == 1:
+            self.mine[index] = self.mine[index] + others[0][0][others[0][1]]
+            return
         total = self.mine[index].astype(F32)
         for ref, i in others:
             total = total + ref[i].astype(F32)
@@ -612,7 +690,7 @@
         self.send_b(side, slot, rr, b).wait_recv()
         self.add(self.at(rr, self.me.pa, b), (self.from_b, (side, slot)))
 
-    def ring_b(self):
+    def begin_b(self):
         pb = self.me.pb
         self.finish_a(0, pb + 2)
         self.send_b(0, 0, 0, pb + 2).start()
@@ -623,13 +701,48 @@
         self.finish_a(0, pb + 3)
         self.send_b(1, 1, 0, pb + 3).start()
         self.finish_a(0, pb + 1)
+        self.finish_a(1, pb + 3)
+        self.finish_a(1, pb)
+        self.finish_a(0, pb)
+
+    def onward_b(self):
+        pb = self.me.pb
         self.add_b(0, 0, 0, pb + 1)
         self.send_b(0, 1, 0, pb + 1).start()
-        self.finish_a(1, pb + 3)
         self.add_b(1, 0, 1, pb + 3)
         self.send_b(1, 2, 1, pb + 3).start()
-        self.finish_a(1, pb)
-        self.finish_a(0, pb)
+
+    def plane_copy(self, rr, off):
+        me = self.me
+        slot = rr * RING + (RING - off) % RING
+        return remote(
+            self.mine.at[(*self.head, *self.at(rr, me.pa, me.pb + off))],
+            self.from_b.at[slot],
+            self.b_send.at[rr * RING + off],
+            self.b_recv.at[slot],
+            me.on_plane(rr, off),
+        )
+
+    def begin_plane(self):
+        for rr, off in PLANE[::-1]:
+            self.finish_a(rr, self.me.pb + off)
+            self.plane_copy(rr, off).start()
+        self.finish_a(0, self.me.pb)
+
+    def end_plane(self):
+        me = self.me
+        for rr, off in PLANE:
+            self.plane_copy(rr, off).wait_recv()
+        slots = [(self.from_b, (rr * RING + off,)) for rr, off in PLANE]
+        self.add(self.at(0, me.pa, me.pb), *slots)
+        self.hand_over()
+
+    def hand_over(self):
+        me = self.me
+        self.last().start()
+        self.out[me.core] = self.mine[
+            (*self.head, *self.at(0, me.pa, me.pb), me.core)
+        ].astype(F32)
 
     def over(self):
         me = self.me
@@ -663,16 +776,12 @@
         me = self.me
         self.over().wait_recv()
         self.add(self.at(0, me.pa, me.pb), (self.from_y, ...))
-        self.last().start()
-        self.out[me.core] = self.mine[
-            (*self.head, *self.at(0, me.pa, me.pb), me.core)
-        ].astype(F32)
-
-    def finish(self):
+        self.hand_over()
+
+    def finish(self, plane=False):
         self.last().wait_recv()
         self.out[1 - self.me.core] = self.from_core[...].astype(F32)
         self.last().wait_send()
-        self.over().wait_send()
 
         def sent_sibling(at, carry):
             self.to_sibling(at).wait_send()
@@ -686,20 +795,26 @@
             return carry
 
         lax.fori_loop(0, 3 * RING, sent_a, 0)
+        if plane:
+            for rr, off in PLANE:
+                self.plane_copy(rr, off).wait_send()
+            return
+        self.over().wait_send()
         for slot in range(3):
             self.send_b(0, slot, 0, 0).wait_send()
             self.send_b(1, slot, 0, 0).wait_send()
 
 
-def scatter_scratch(kinds, rows, width, in_place=False):
+def scatter_scratch(kinds, rows, width, in_place=False, plane=False):
     blocks = 2 * RING * RING
     dma = pltpu.SemaphoreType.DMA
+    slots = (2 * RING,) if plane else (2, 3)
     mine = [] if in_place else [pltpu.VMEM((*kinds, 2, RING, RING, 2, rows, width), BF)]
     return [
         *mine,
         pltpu.VMEM((*kinds, 2, RING, RING, 2, rows, width), BF),
         pltpu.VMEM((2, 3 * RING, *kinds, 2, rows, width), BF),
-        pltpu.VMEM((2, 3, *kinds, 2, rows, width), BF),
+        pltpu.VMEM((*slots, *kinds, 2, rows, width), BF),
         pltpu.VMEM((*kinds, 2, rows, width), BF),
         pltpu.VMEM((*kinds, rows, width), BF),
         *([] if in_place else [dma]),
@@ -707,8 +822,8 @@
         dma((blocks,)),
         dma((2, 3 * RING)),
         dma((2, 3 * RING)),
-        dma((2, 3)),
-        dma((2, 3)),
+        dma(slots),
+        dma(slots),
         dma((4,)),
     ]
 
@@ -771,6 +886,8 @@
     count, width = middle.shape
     wide = back_inner.shape[1]
     part = weights.shape[2]
+    half = count // 2
+    edge = half - HALO
 
     def load(i):
         src, dst = (
@@ -787,14 +904,22 @@
         return pltpu.make_async_copy(src, dst, loads.at[i])
 
     def exchange(i):
-        src, dst = ((back_own, back_theirs), (feed_own, feed_theirs), (one_own, one_theirs))[i]
-        return remote(src, dst, pairs.at[0, i], pairs.at[1, i], pair)
+        src, dst, lo, hi = (
+            (back_own, back_theirs, 0, half),
+            (back_own, back_theirs, half, count),
+            (one_own, one_theirs, 0, edge),
+            (one_own, one_theirs, edge, count),
+            (feed_own, feed_theirs, 0, count),
+        )[i]
+        at = pl.ds(lo, hi - lo)
+        return remote(src.at[at], dst.at[at], pairs.at[0, i], pairs.at[1, i], pair)
 
     for i in range(9):
         load(i).start()
     me.greet((pair, ahead_of, behind))
     load(0).wait()
     exchange(0).start()
+    exchange(1).start()
     feed.begin()
     for i in range(1, 9):
         load(i).wait()
@@ -816,13 +941,15 @@
     for at in rows_of(count, ROWS):
         inner[at, :] = (mixed[at, wide : 2 * wide] * convolved(at)).astype(BF)
     feed.direct()
-    feed.onward()
-
-    exchange(0).wait_recv()
-    exchange(1).start()
-
-    def norm_step(i, carry):
-        at = pl.ds(pl.multiple_of(i * ROWS, ROWS), ROWS)
+
+    def turn_step(at):
+        values = tokens[at, :].astype(F32)
+        inverse = lax.rsqrt(mean_square(values) + norm_eps)
+        branch[at, :] = (values * inverse * gain_one).astype(BF)
+
+    row_loop(count, turn_step)
+    turned[...] = branch[...].T
+    def norm_step(at):
         mid = middle[at, :]
         inverse = lax.rsqrt(mean_square(mid) + norm_eps)
         own = back_own[at, :].astype(F32)
@@ -831,118 +958,117 @@
         grad_ref[at, :] = total
         branch[at, :] = total.astype(BF)
         sums[1:2, :] += jnp.sum(own * mid * inverse, axis=0, keepdims=True)
-        return carry
-
-    lax.fori_loop(0, count // ROWS, norm_step, 0)
+
     cut = 3 * wide - part
-    w_out = weights[1, :, cut : cut + wide]
-    back_inner[...] = dot(branch[...], w_out, ((1,), (0,)))
-    for at in rows_of(count, ROWS):
-        wide_conv[at, :] = (back_inner[at, :] * mixed[at, wide : 2 * wide]).astype(BF).astype(F32)
-    halo_out[...] = wide_conv[0:HALO, :].astype(BF)
-    halo = remote(halo_out, halo_in, halo_sem.at[0], halo_sem.at[1], behind)
-    halo.start()
-    turned[...] = branch[...].T
-    term_out = dot(turned[...], inner[...], ((1,), (0,))).astype(BF)
-    shape = pm_ref.shape[1:-1]
-    pm_ref[1, :, :, :, :, :, cut : cut + wide] = term_out.reshape(*shape, wide)
-    for at in rows_of(count, ROWS):
-        values = tokens[at, :].astype(F32)
-        inverse = lax.rsqrt(mean_square(values) + norm_eps)
-        branch[at, :] = (values * inverse * gain_one).astype(BF)
-    turned[...] = branch[...].T
-    feed.kept()
-    halo.wait_recv()
-    last = me.s % (lax.axis_size("seq") // 2) == lax.axis_size("seq") // 2 - 1
-    wide_conv[count : count + HALO, :] = jnp.where(last, 0.0, halo_in[...].astype(F32))
-    for at in rows_of(count, ROWS):
-        back_gated = (
-            taps[0] * wide_conv[at.start + 2 : at.stop + 2, :]
-            + taps[1] * wide_conv[at.start + 1 : at.stop + 1, :]
-            + taps[2] * wide_conv[at, :]
-        )
-        back_mixed[at, :wide] = (back_gated * mixed[at, 2 * wide :]).astype(BF)
-        back_mixed[at, wide : 2 * wide] = (back_inner[at, :] * convolved(at)).astype(BF)
-        back_mixed[at, 2 * wide :] = (back_gated * mixed[at, :wide]).astype(BF)
-        for i in range(3):
-            shift = HALO - 2 + i
-            term = wide_conv[at, :] * wide_gated[at.start + shift : at.stop + shift, :]
-            sums[2 + i : 3 + i, tap_at] += jnp.sum(term, axis=0, keepdims=True)
-
-    one_sum[...] = jnp.zeros_like(one_sum)
-
-    def back_step(j, carry):
-        half, at, lanes = in_tile(j, part)
-        one_sum[...] += dot(back_mixed[:, lanes], weights[half, :, at], ((1,), (1,)))
-        return carry
-
-    lax.fori_loop(0, 4, back_step, 0)
-
-    def gain_step(i, carry):
-        at = pl.ds(pl.multiple_of(i * ROWS, ROWS), ROWS)
+
+    def inner_rows(lo, hi):
+        row_loop(hi - lo, norm_step, lo)
+        w_out = weights[1, :, cut : cut + wide]
+        back_inner[lo:hi, :] = dot(branch[lo:hi, :], w_out, ((1,), (0,)))
+        for at in rows_of(hi, ROWS, lo):
+            product = back_inner[at, :] * mixed[at, wide : 2 * wide]
+            wide_conv[at, :] = product.astype(BF).astype(F32)
+
+    def gain_step(at):
         values = tokens[at, :].astype(F32)
         inverse = lax.rsqrt(mean_square(values) + norm_eps)
         own = one_sum[at, :]
         one_own[at, :] = own.astype(BF)
         sums[0:1, :] += jnp.sum(own * values * inverse, axis=0, keepdims=True)
+
+    def mixed_rows(lo, hi):
+        for at in rows_of(hi, HALO, lo):
+            back_gated = (
+                taps[0] * wide_conv[at.start + 2 : at.stop + 2, :]
+                + taps[1] * wide_conv[at.start + 1 : at.stop + 1, :]
+                + taps[2] * wide_conv[at, :]
+            )
+            back_mixed[at, :wide] = (back_gated * mixed[at, 2 * wide :]).astype(BF)
+            back_mixed[at, wide : 2 * wide] = (back_inner[at, :] * convolved(at)).astype(BF)
+            back_mixed[at, 2 * wide :] = (back_gated * mixed[at, :wide]).astype(BF)
+            for i in range(3):
+                shift = HALO - 2 + i
+                term = wide_conv[at, :] * wide_gated[at.start + shift : at.stop + shift, :]
+                sums[2 + i : 3 + i, tap_at] += jnp.sum(term, axis=0, keepdims=True)
+        one_sum[lo:hi, :] = jnp.zeros((hi - lo, width), F32)
+
+        def back_step(j, carry):
+            which, at, lanes = in_tile(j, part)
+            one_sum[lo:hi, :] += dot(back_mixed[lo:hi, lanes], weights[which, :, at], ((1,), (1,)))
+            return carry
+
+        lax.fori_loop(0, 4, back_step, 0)
+        row_loop(hi - lo, gain_step, lo, HALO)
+
+    exchange(0).wait_recv()
+    inner_rows(0, half)
+    halo_out[...] = wide_conv[0:HALO, :].astype(BF)
+    halo = remote(halo_out, halo_in, halo_sem.at[0], halo_sem.at[1], behind)
+    halo.start()
+    mixed_rows(0, edge)
+    exchange(2).start()
+    feed.onward()
+    exchange(1).wait_recv()
+    inner_rows(half, count)
+    halo.wait_recv()
+    last = me.s % (lax.axis_size("seq") // 2) == lax.axis_size("seq") // 2 - 1
+    wide_conv[count : count + HALO, :] = jnp.where(last, 0.0, halo_in[...].astype(F32))
+    mixed_rows(edge, count)
+    vec_own[...] = sums[: vec_own.shape[0], :]
+    swap_vec = remote(vec_own, vec_theirs, vec_sem.at[0], vec_sem.at[1], pair)
+    swap_vec.start()
+    exchange(3).start()
+    exchange(4).start()
+    term_out = dot(branch[...], inner[...], ((0,), (0,))).astype(BF)
+    shape = pm_ref.shape[1:-1]
+    pm_ref[1, :, :, :, :, :, cut : cut + wide] = term_out.reshape(*shape, wide)
+
+    def term_step(j, carry):
+        which, at, lanes = in_tile(j, part)
+        term = dot(turned[...], back_mixed[:, lanes], ((1,), (0,))).astype(BF)
+        pm_ref[which, :, :, :, :, :, at] = term.reshape(*shape, part // 3)
         return carry
 
-    lax.fori_loop(0, count // ROWS, gain_step, 0)
-    exchange(2).start()
-
-    def term_step(j, carry):
-        half, at, lanes = in_tile(j, part)
-        term = dot(turned[...], back_mixed[:, lanes], ((1,), (0,))).astype(BF)
-        pm_ref[half, :, :, :, :, :, at] = term.reshape(*shape, part // 3)
-        return carry
-
     lax.fori_loop(0, 4, term_step, 0)
+    swap_vec.wait()
+    sums[: vec_own.shape[0], :] = vec_own[...] + vec_theirs[...]
     vec_term = sums[...].T.astype(BF)
     lanes = vec_term.shape[1]
     pm_ref[1, :, :, :, :, :, cut + wide : cut + wide + lanes] = vec_term.reshape(*shape, lanes)
     pm_ref[1, :, :, :, :, :, cut + wide + lanes :] = jnp.zeros(
         (*shape, part - cut - wide - lanes), BF
     )
-    mixer.begin()
-    feed.ring_b()
-    mixer.opposite()
-    mixer.direct()
-    feed.across_y()
-    mixer.onward()
-    mixer.kept()
-    feed.across_cores()
-    exchange(1).wait_recv()
-
-    def out_step(i, carry):
-        at = pl.ds(pl.multiple_of(i * ROWS, ROWS), ROWS)
+    def out_step(at):
         total = feed_own[at, :].astype(F32) + feed_theirs[at, :].astype(F32)
         block_ref[at, :] = middle[at, :] + total
-        return carry
-
-    lax.fori_loop(0, count // ROWS, out_step, 0)
-    mixer.ring_b()
-    mixer.across_y()
-    mixer.across_cores()
-    exchange(2).wait_recv()
-
-    def grad_step(i, carry):
-        at = pl.ds(pl.multiple_of(i * ROWS, ROWS), ROWS)
+
+    def grad_step(at):
         values = tokens[at, :].astype(F32)
         inverse = lax.rsqrt(mean_square(values) + norm_eps)
         back = one_own[at, :].astype(F32) + one_theirs[at, :].astype(F32)
         grad_ref[at, :] += norm_back(values, inverse, gain_one, back)
-        return carry
-
-    lax.fori_loop(0, count // ROWS, grad_step, 0)
-    mixer.finish()
-    vec_own[...] = om_ref[1, :, cut + wide : cut + wide + LANES]
-    swap_vec = remote(vec_own, vec_theirs, vec_sem.at[0], vec_sem.at[1], pair)
-    swap_vec.start()
+
+    mixer.begin()
+    feed.kept()
+    feed.begin_b()
+    mixer.opposite()
+    mixer.direct()
+    feed.onward_b()
+    mixer.onward()
+    mixer.kept()
+    feed.across_y()
+    mixer.begin_plane()
+    feed.across_cores()
+    exchange(2).wait_recv()
+    exchange(3).wait_recv()
+    row_loop(count, grad_step)
+    mixer.end_plane()
+    mixer.finish(plane=True)
     feed.finish()
-    swap_vec.wait()
-    om_ref[1, :, cut + wide : cut + wide + LANES] = vec_own[...] + vec_theirs[...]
+    exchange(4).wait_recv()
+    row_loop(count, out_step)
     halo.wait_send()
-    for i in range(3):
+    for i in range(5):
         exchange(i).wait_send()
 
 
@@ -987,12 +1113,12 @@
             pltpu.VMEM((HALO, wide), BF),
             pltpu.VMEM((halves, *whole), BF),
             dma((9,)),
-            dma((2, 3)),
+            dma((2, 5)),
             dma((2,)),
-            pltpu.VMEM((rows, LANES), F32),
-            pltpu.VMEM((rows, LANES), F32),
+            like(vec),
+            like(vec),
             dma((2,)),
-            *scatter_scratch((), rows, width, in_place=True),
+            *scatter_scratch((), rows, width, in_place=True, plane=True),
             *scatter_scratch((kinds,), rows, width),
         ],
         compiler_params=pltpu.CompilerParams(
@@ -1078,7 +1204,7 @@
             pltpu.VMEM((tokens, total), F32),
             pltpu.VMEM((tokens, total), F32),
         ],
-        compiler_params=pltpu.CompilerParams(vmem_limit_bytes=48 * 1024 * 1024),
+        compiler_params=pltpu.CompilerParams(vmem_limit_bytes=60 * 1024 * 1024),
         cost_estimate=pl.CostEstimate(
             flops=flops, bytes_accessed=4 * halves * kinds * total * width, transcendentals=0
         ),
@@ -1107,17 +1233,27 @@
     return (weight_new, first_new, second_new)
 
 
-def adam_kernel(om_ref, of_ref, *refs):
+def adam_kernel(om_ref, of_ref, block_ref, grad_ref, *refs):
     chan = lax.axis_index("chan")
     w_in, w_out, w_gu, w_down, vectors = [refs[3 * i : 3 * i + 3] for i in range(5)]
     in_new, out_new, gu_new, down_new, vec_new = [refs[15 + 3 * i : 18 + 3 * i] for i in range(5)]
+    count = block_ref.shape[0] // 4
+    moves = []
+    for k, (src, dst) in enumerate(((block_ref, refs[30]), (grad_ref, refs[31]))):
+        held = refs[32].at[k]
+        for i in range(4):
+            at = pl.ds(i * count, count)
+            into = pltpu.make_async_copy(src.at[at], held.at[at], refs[33].at[0, k, i])
+            out = pltpu.make_async_copy(held.at[at], dst.at[at], refs[33].at[1, k, i])
+            into.start()
+            moves.append((into, out))
     part = om_ref.shape[2]
     wide = w_out[0].shape[1]
     cut = 3 * wide - part
 
     def update(arrays, results, index, gradient, rate=rate_matrix, decay=decay_matrix):
         new = adam_update(*[a[index] for a in arrays], gradient, rate, decay)
-        for ref, value in zip(results, new):
+        for ref, value in zip(results, new, strict=True):
             ref[index] = value
 
     def both(at):
@@ -1125,10 +1261,10 @@
 
     for c in range(2):
         at = slice(c * wide, (c + 1) * wide)
-        update(w_in, in_new, (slice(None), c), om_ref[0, :, at])
+        update(w_in, in_new, (c,), om_ref[0, :, at])
     left = part - 2 * wide
-    update(w_in, in_new, (slice(None), 2, slice(0, left)), om_ref[0, :, 2 * wide :])
-    update(w_in, in_new, (slice(None), 2, slice(left, wide)), om_ref[1, :, :cut])
+    update(w_in, in_new, (2, slice(None), slice(0, left)), om_ref[0, :, 2 * wide :])
+    update(w_in, in_new, (2, slice(None), slice(left, wide)), om_ref[1, :, :cut])
     update(w_out, out_new, both(slice(None)), om_ref[1, :, cut : cut + wide])
     for half in range(2):
         at = slice(half * part, (half + 1) * part)
@@ -1140,22 +1276,30 @@
     turned = jnp.concatenate([block, jnp.zeros((LANES - rows, LANES), F32)], axis=0).T
     own = jnp.where(chan == 0, turned[:5, : rows // 2], turned[:5, rows // 2 : rows])
     update(vectors, vec_new, both(slice(None)), own, rate_vector, 0.0)
-
-
-def adam(sum_mixer, sum_feed, arrays):
+    for into, out in moves:
+        into.wait()
+        out.start()
+    for _, out in moves:
+        out.wait()
+
+
+def adam(sum_mixer, sum_feed, block_out, input_grad, arrays):
     def whole(x):
         return pl.BlockSpec(x.shape, lambda i, n=x.ndim: (0,) * n)
 
-    ins = (sum_mixer, sum_feed, *arrays)
+    moved = (block_out, input_grad)
+    hbm = pl.BlockSpec(memory_space=pl.ANY)
+    dma = pltpu.SemaphoreType.DMA
     return pl.pallas_call(
         adam_kernel,
         grid=(1,),
-        out_shape=[jax.ShapeDtypeStruct(x.shape, x.dtype) for x in arrays],
-        in_specs=[whole(x) for x in ins],
-        out_specs=[whole(x) for x in arrays],
-        compiler_params=pltpu.CompilerParams(vmem_limit_bytes=48 * 1024 * 1024),
+        out_shape=[jax.ShapeDtypeStruct(x.shape, x.dtype) for x in (*arrays, *moved)],
+        in_specs=[whole(sum_mixer), whole(sum_feed), hbm, hbm, *[whole(x) for x in arrays]],
+        out_specs=[*[whole(x) for x in arrays], hbm, hbm],
+        scratch_shapes=[pltpu.VMEM((2, *block_out.shape), F32), dma((2, 2, 4))],
+        compiler_params=pltpu.CompilerParams(vmem_limit_bytes=60 * 1024 * 1024),
         name="adam",
-    )(*ins)
+    )(sum_mixer, sum_feed, *moved, *arrays)
 
 
 def body(
@@ -1177,30 +1321,24 @@
     vectors_m,
     vectors_v,
 ):
-    chan = lax.axis_index("chan")
-    turned = vectors.T
-    none = jnp.zeros_like(turned)
-    vec_rows = jnp.where(
-        chan == 0,
-        jnp.concatenate([turned, none], axis=0),
-        jnp.concatenate([none, turned], axis=0),
-    )
-    vec_rows = jnp.pad(vec_rows, ((0, 0), (0, LANES - vec_rows.shape[1])))
+    in_state = [jnp.transpose(a, (1, 0, 2)) for a in (w_in, w_in_m, w_in_v)]
     full_mixer, full_feed, middle, normed_two, mixed, gated, vec = forward(
-        tokens, w_in, w_out, w_gu, w_down, vec_rows
+        tokens, in_state[0], w_out, w_gu, w_down, vectors
     )
     term_feed, feed_part, back_two_part = feed_forward(normed_two, cotangent, full_feed)
     sum_mixer, sum_feed, block_out, input_grad = backward(
         term_feed, back_two_part, feed_part, middle, cotangent, tokens, mixed, gated, full_mixer, vec
     )
     state = (
-        *(w_in, w_in_m, w_in_v),
+        *in_state,
         *(w_out, w_out_m, w_out_v),
         *(w_gu, w_gu_m, w_gu_v),
         *(w_down, w_down_m, w_down_v),
         *(vectors, vectors_m, vectors_v),
     )
-    return (block_out, input_grad, *adam(sum_mixer, sum_feed, state))
+    *new, block_out, input_grad = adam(sum_mixer, sum_feed, block_out, input_grad, state)
+    in_new = [jnp.transpose(a, (1, 0, 2)) for a in new[:3]]
+    return (block_out, input_grad, *in_new, *new[3:])
 
 
 def solution(mesh):

time: 222 us -> 187 us (0.84)
  local copies, waits for them, and re-layouts: 17.6 us -> 0 us
  Pallas kernels: 203 us -> 186 us
    pallas_call x1, Pallas kernels: 95.2 us -> 75.7 us  [backward(): pl.pallas_call(backward_kernel, out_shape=(jax.ShapeDtypeStruct((halves,...]
    unnamed x65 -> x0, local copies, waits for them, and re-layouts: 17.6 us -> none
    pallas_call x1, Pallas kernels: 2.01 us -> 5.79 us  [adam(): pl.pallas_call(adam_kernel, grid=(1,), out_shape=[jax.ShapeDtypeStruct(x....]
where the time goes in v5:
time: 187 us
  Pallas kernels  186 us (99%)
    pallas_call x1, Pallas kernels, forward(): pl.pallas_call(forward_kernel, out_shape=(jax.ShapeDtypeStruct((2, *whole...  79.8 us
    pallas_call x1, Pallas kernels, backward(): pl.pallas_call(backward_kernel, out_shape=(jax.ShapeDtypeStruct((halves,...  75.7 us
    pallas_call x1, Pallas kernels, feed_forward(): pl.pallas_call(feed_kernel, grid=(width // lanes,), out_shape=(jax.ShapeD...  25.1 us
    pallas_call x1, Pallas kernels, adam(): pl.pallas_call(adam_kernel, grid=(1,), out_shape=[jax.ShapeDtypeStruct(x....  5.79 us

profile of v5, /device:TPU:1, one launch (start us, length us, event | category | flops | bytes accessed | tf_op | source)
XLA Modules:
  0.0 187.3 jit_solution(4203635744593565147)
XLA Ops:
  0.7 79.8 %gather_and_forward.1 = (bf16[2,2,4,4,2,16,1152]{6,5,4,3,2,1,0:T(8,128)(2,1)}, bf16[2,3,2,4,4,2,16,1152]{7,6,5,4,3,2,1,0:T(8,128)(2,1)}, f32[384,1024]{1,0:T(8,1...) custom-call(bf16[384,1024]{1,0:T(8,128)(2,1)} %tokens_hbm.3, ...), custom_call_target="tpu_custom_call" | custom-call | tf_op jit(solution)/shard_map/gather_and_forward/pallas_call | solution.py:488
  80.5 25.1 %feed_forward.1 = (bf16[2,3,1024,1152]{3,2,1,0:T(8,128)(2,1)}, bf16[384,1024]{1,0:T(8,128)(2,1)}, bf16[384,1024]{1,0:T(8,128)(2,1)}) custom-call(bf16[384,1024]{1,0:T(8,128)(2,1)} %get-tuple-element.48.n_ref, bf16[384,1024]{1,0:T(8,128)(2,1)} %cot_hbm.1, bf16[2,3,1024,1152]{3,2,1,0:T(8,128)(2,1)} %bitcast.15), custom_call_target="tpu_custom_call" | custom-call | flops 16307453952 | bytes 28311552 | tf_op jit(solution)/shard_map/feed_forward/pallas_call | solution.py:1191
  105.6 75.7 %backward_and_scatter.1 = (f32[2,16,1152]{2,1,0:T(8,128)}, f32[2,3,16,1152]{3,2,1,0:T(8,128)}, f32[384,1024]{1,0:T(8,128)}, f32[384,1024]{1,0:T(8,128)}) custom-call(bf16[2,3,2,4,4,2,16,1152]{7,6,5,4,3,2,1,0:T(8,128)(2,1)} %bitcast.9, bf16[384,1024]{1,0:T(8,128)(2,1)} %get-tuple-element.51.back_hbm, bf16[384,1024]{1,0:T(8,128)(2,1)} %get-tuple-element.52.feed_hbm, ...), custom_call_target="tpu_custom_call" | custom-call | tf_op jit(solution)/shard_map/backward_and_scatter/pallas_call | solution.py:1087
  181.3 5.8 %adam.1 = (f32[3,16,512]{2,1,0:T(8,128)}, f32[3,16,512]{2,1,0:T(8,128)}, f32[3,16,512]{2,1,0:T(8,128)}, f32[16,512]{1,0:T(8,128)}, f32[16,512]{1,0:T(8,128)}, /*...) custom-call(f32[2,16,1152]{2,1,0:T(8,128)} %get-tuple-element.58.om_, ...), custom_call_target="tpu_custom_call" | custom-call | tf_op jit(solution)/shard_map/adam/pallas_call | solution.py:1293
